TPU v7x, 128 devices: a whole 4x4x4 slice. The times are simulated.
128 devices in a mesh: gx: 4 (over x), gy: 4 (over z), gz: 8 (over y, core).
Axes of the slice: x: 4, y: 4, z: 4, core: 2. Of those that a mesh axis runs over, the one named last changes fastest.
Arguments:
- block: float32 [4, 128, 256, 512], P(None, 'gz', 'gy', 'gx'), may hold values from -40 to 40, as said below
- kappa: float32 [128, 256, 512], P('gz', 'gy', 'gx'), may hold values from 0.5 to 2
Outputs:
- ortho_block: float32 [4, 128, 256, 512], P(None, 'gz', 'gy', 'gx')
- triangle: float32 [20, 20], replicated
Inputs may be any that keep to these rules, and one draw needn't show every extreme that they name: `block`: real values.
All inputs are finite; a program needn't handle non-finite values.
Results may differ from a plain program's by a relative error of at most 0.0003.
Values sent between devices are 32-bit elements; how exact they have to be, the bound alone decides.
No kernel may reach another device: no remote copies, remote signals or barrier semaphores. Data moves between devices by JAX's collectives and lax.ppermute only.
A program may use at most 128 MiB of HBM per device.

v0:
```python
import jax
import jax.numpy as jnp
from jax import lax
from jax.sharding import PartitionSpec as P

COLS = 4
BASIS = 4
KRYLOV = 20


basis_shift = 6.0
basis_scale = 3.0


def extended(value, sides, width):
    for axis, dim in sides:
        peers, length = (lax.axis_size(axis), value.shape[dim])
        up = [(i, (i + 1) % peers) for i in range(peers - 1)]
        down = [(j, i) for i, j in up]
        last = lax.slice_in_dim(value, length - width, length, axis=dim)
        leading = lax.slice_in_dim(value, 0, width, axis=dim)
        before = lax.ppermute(last, axis, up)
        after = lax.ppermute(leading, axis, down)
        value = jnp.concatenate([before, value, after], axis=dim)
    return value


def upper_factor(matrix):
    count = matrix.shape[0]
    positions = jnp.arange(count, dtype=jnp.int32)
    rows = []
    for k in range(count):
        target = matrix[k]
        if k > 0:
            prior = jnp.stack(rows, 0)
            target = target - jnp.sum(prior[:, k][:, None] * prior, 0)
        pivot = jnp.sqrt(target[k])
        row = jnp.where(positions == k, pivot, target / pivot)
        row = jnp.where(positions >= k, row, jnp.zeros_like(row))
        rows.append(row)
    return jnp.stack(rows, 0)


def upper_inverse(upper):
    count = upper.shape[0]
    positions = jnp.arange(count, dtype=jnp.int32)
    rows = [None] * count
    for i in range(count - 1, -1, -1):
        unit = (positions == i).astype(upper.dtype)
        total = unit
        for k in range(i + 1, count):
            total = total - upper[i, k] * rows[k]
        rows[i] = total / upper[i, i]
    return jnp.stack(rows, 0)


def stencil_inner(padded, kpad):
    nz = kpad.shape[0] - 2
    ny = kpad.shape[1] - 2
    nx = kpad.shape[2] - 2
    centre = padded[:, 1:-1, 1:-1, 1:-1]
    kcentre = kpad[1:-1, 1:-1, 1:-1]
    offsets = [(2, 1, 1), (0, 1, 1), (1, 2, 1), (1, 0, 1), (1, 1, 2), (1, 1, 0)]
    total = jnp.zeros_like(centre)
    for oz, oy, ox in offsets:
        near = padded[:, oz : oz + nz, oy : oy + ny, ox : ox + nx]
        knear = kpad[oz : oz + nz, oy : oy + ny, ox : ox + nx]
        total = total + (0.5 * (kcentre + knear))[None] * (centre - near)
    return total


def shards(block, kappa):
    depth_z, depth_y, depth_x = kappa.shape
    stacked = jnp.concatenate([block, kappa[None]], 0)
    blocks = [block]
    padded = extended(stacked, (("gx", 3), ("gy", 2), ("gz", 1)), 1)
    kpad = padded[COLS]
    current_pad = padded[:COLS]
    for step in range(BASIS):
        centre = current_pad[:, 1:-1, 1:-1, 1:-1]
        following = (stencil_inner(current_pad, kpad) - basis_shift * centre) / basis_scale
        blocks.append(following)
        if step + 1 < BASIS:
            current_pad = extended(following, (("gx", 3), ("gy", 2), ("gz", 1)), 1)
    basis = jnp.concatenate(blocks, 0).reshape(KRYLOV, -1)
    local_gram = jnp.dot(basis, basis.T, precision=lax.Precision.HIGHEST)
    ncells = float(
        depth_z
        * depth_y
        * depth_x
        * lax.axis_size("gx")
        * lax.axis_size("gy")
        * lax.axis_size("gz")
    )
    gram = lax.psum(local_gram, ("gx", "gy", "gz"))
    triangle = upper_factor(gram / ncells)
    inverse = upper_inverse(triangle[:COLS, :COLS])
    ortho_block = jnp.einsum("ij,izyx->jzyx", inverse, block, precision=lax.Precision.HIGHEST)
    return (ortho_block, triangle)


def solution(mesh):
    return jax.shard_map(
        shards,
        mesh=mesh,
        in_specs=(P(None, "gz", "gy", "gx"), P("gz", "gy", "gx")),
        out_specs=(P(None, "gz", "gy", "gx"), P()),
        check_vma=False,
    )
```

profile of v0, /device:TPU:1, one launch (start us, length us, event | category | flops | bytes accessed | tf_op | source)
XLA Modules:
  0.0 433.0 jit_solution(1316134869751614836)
XLA Ops:
  0.6 3.0 copy.78
  3.7 4.9 %pad_maximum_fusion = (f32[5,16,64,1]{3,0,2,1:T(8,128)}, f32[5,16,64,1]{3,0,2,1:T(8,128)}) fusion(f32[1,16,64,128]{3,0,2,1:T(1,128)S(1)} %bitcast.153, f32[4,16,64,128]{3,0,2,1:T(4,128)S(1)} %copy.78), kind=kLoop, calls=%fused_computation.2 | loop fusion | flops 10240 | bytes 2662400 | tf_op jit(solution)/shard_map/concatenate | solution.py:74
  8.7 2.7 copy.35
  12.6 2.7 copy.34
  15.3 4.6 %collective-permute-start = (f32[5,16,64,1]{2,1,3,0:T(8,128)S(1)}, f32[5,16,64,1]{2,1,3,0:T(8,128)S(1)}, u32[]{:S(2)}, u32[]{:S(2)}) collective-permute-start(f32[5,16,64,1]{2,1,3,0:T(8,128)S(1)} %copy.34), channel_id=1, source_target_pairs={{0,32},{32,64},{64,96},{1,33},{33,65},{65,97},{2,34},{34,66},{66,9... | collective-permute-start | bytes 61448 | tf_op jit(solution)/shard_map/ppermute | solution.py:22
  19.9 2.7 copy.37
  22.6 2.6 copy.36
  26.6 4.1 collective-permute-start.2
  32.6 4.0 collective-permute-done.3
  36.5 1.6 pad_maximum_fusion.89
  38.1 1.9 copy.39
  40.0 4.4 %collective-permute-start.5 = (f32[5,1,66,130]{2,1,3,0:T(1,128)}, f32[5,1,66,130]{2,1,3,0:T(1,128)}, u32[]{:S(2)}, u32[]{:S(2)}) collective-permute-start(f32[5,1,66,130]{2,1,3,0:T(1,128)} %copy.39), channel_id=1, source_target_pairs={{1,0},{2,1},{3,2},{4,3},{5,4},{6,5},{7,6},{9,8},{10,9},{11,10},{12... | collective-permute-start | bytes 514808 | tf_op jit(solution)/shard_map/ppermute | solution.py:23
  45.4 3.3 collective-permute-start.4
  48.7 2.0 collective-permute-done.5
  52.9 2.2 copy.40
  55.1 10.4 %pad_maximum_fusion.79 = f32[1,18,66,130]{3,0,2,1:T(1,128)} fusion(f32[5,1,66,130]{3,0,2,1:T(8,128)S(1)} %copy.41, f32[5,1,66,130]{3,0,2,1:T(8,128)} %copy.40, f32[5,16,1,130]{3,0,2,1:T(8,128)S(1)} %collective-permute-done.3, f32[5,16,1,130]{3,0,2,1:T(8,128)S(1)} %collective-permute-done.2, f32[5,16,64,1]{3,0,2,1:T(8,128)} %copy.37, ...), kind=kLoop, calls=%fused_computation.157 | loop fusion | flops 1081080 | bytes 3706560 | tf_op jit(solution)/shard_map/concatenate | solution.py:24
  65.5 2.8 copy.42
  68.3 4.4 %fusion.80 = (f32[16,64,128]{1,2,0:T(8,128)}, f32[16,64,128]{1,2,0:T(8,128)}, f32[16,64,128]{1,2,0:T(8,128)}, f32[16,64,128]{1,2,0:T(8,128)}, f32[16,64,128]{1,2,0:T(8,128)}, /*index=5*/f32[16,64,128]{1,2,0:T(8,128)}) fusion(f32[18,66,130]{1,2,0:T(8,128)S(1)} %bitcast.151), kind=kLoop, calls=%fused_computation.174 | loop fusion | flops 1572864 | bytes 6815744 | tf_op jit(solution)/shard_map/mul | solution.py:68
  72.7 1.6 copy.43
  74.7 2.4 copy.51
  77.1 2.3 copy.49
  81.7 22.9 %broadcast_multiply_fusion.2 = (f32[4,16,64,128]{3,0,2,1:T(4,128)S(1)}, f32[4,16,64,128]{3,0,2,1:T(4,128)}) fusion(f32[4,16,64,128]{3,0,2,1:T(4,128)} %copy-done.6, f32[1,16,64,128]{3,0,2,1:T(1,128)} %bitcast.152, f32[5,16,64,1]{3,0,2,1:T(8,128)} %copy.36, f32[16,64,128]{2,1,0:T(8,128)} %copy.56, f32[5,16,64,1]{3,0,2,1:T(8,128)} %copy.37, ...), kind=kLoop, calls=%fused_computation.177 | loop fusion | flops 23068672 | bytes 10428832 | tf_op jit(solution)/shard_map/div | solution.py:81
  104.6 3.3 fusion.96
  107.9 2.2 copy.61
  111.4 2.0 copy.60
  113.3 4.0 collective-permute-start.6
  117.3 1.8 copy.63
  119.2 1.9 copy.62
  123.7 4.4 %collective-permute-start.8 = (f32[4,16,1,130]{3,0,2,1:T(4,128)S(1)}, f32[4,16,1,130]{3,0,2,1:T(4,128)S(1)}, u32[]{:S(2)}, u32[]{:S(2)}) collective-permute-start(f32[4,16,1,130]{3,0,2,1:T(4,128)S(1)} %get-tuple-element.29), channel_id=1, source_target_pairs={{0,8},{8,16},{16,24},{1,9},{9,17},{17,25},{2,10},{10,18},{18,26},{... | collective-permute-start | bytes 99848 | tf_op jit(solution)/shard_map/ppermute | solution.py:22
  129.9 1.9 collective-permute-start.10
  131.8 5.9 %collective-permute-start.11 = (f32[4,1,66,130]{3,0,2,1:T(4,128)S(1)}, f32[4,1,66,130]{3,0,2,1:T(4,128)S(1)}, u32[]{:S(2)}, u32[]{:S(2)}) collective-permute-start(f32[4,1,66,130]{3,0,2,1:T(4,128)S(1)} %get-tuple-element.23), channel_id=1, source_target_pairs={{0,1},{1,2},{2,3},{3,4},{4,5},{5,6},{6,7},{8,9},{9,10},{10,11},{11... | collective-permute-start | bytes 411848 | tf_op jit(solution)/shard_map/ppermute | solution.py:22
  137.7 2.2 collective-permute-done.10
  141.1 16.1 %broadcast_multiply_fusion.1 = (f32[4,16,64,128]{3,0,2,1:T(4,128)S(1)}, f32[4,16,64,128]{3,0,2,1:T(4,128)}) fusion(f32[4,16,64,128]{3,0,2,1:T(4,128)S(1)} %copy-done.27, f32[4,16,64,128]{3,0,2,1:T(4,128)S(1)} %get-tuple-element.12, f32[4,16,64,1]{3,0,2,1:T(4,128)S(1)} %copy-done.9, f32[16,64,128]{2,1,0:T(8,128)S(1)} %copy-done.22, ...), kind=kLoop, calls=%fused_computation.176 | loop fusion | flops 19922944 | bytes 11908224 | tf_op jit(solution)/shard_map/div | solution.py:81
  157.2 3.3 fusion.95
  160.5 2.0 copy.67
  163.8 2.0 copy.66
  165.8 4.3 collective-permute-start.12
  170.1 1.9 copy.69
  171.9 1.8 copy.68
  174.9 1.6 collective-permute-start.15
  176.5 4.9 %collective-permute-start.14 = (f32[4,16,1,130]{3,0,2,1:T(4,128)S(1)}, f32[4,16,1,130]{3,0,2,1:T(4,128)S(1)}, u32[]{:S(2)}, u32[]{:S(2)}) collective-permute-start(f32[4,16,1,130]{3,0,2,1:T(4,128)S(1)} %get-tuple-element.27), channel_id=1, source_target_pairs={{0,8},{8,16},{16,24},{1,9},{9,17},{17,25},{2,10},{10,18},{18,26},{... | collective-permute-start | bytes 99848 | tf_op jit(solution)/shard_map/ppermute | solution.py:22
  183.2 1.9 collective-permute-start.16
  185.2 5.5 %collective-permute-start.17 = (f32[4,1,66,130]{3,0,2,1:T(4,128)S(1)}, f32[4,1,66,130]{3,0,2,1:T(4,128)S(1)}, u32[]{:S(2)}, u32[]{:S(2)}) collective-permute-start(f32[4,1,66,130]{3,0,2,1:T(4,128)S(1)} %get-tuple-element.21), channel_id=1, source_target_pairs={{0,1},{1,2},{2,3},{3,4},{4,5},{5,6},{6,7},{8,9},{9,10},{10,11},{11... | collective-permute-start | bytes 411848 | tf_op jit(solution)/shard_map/ppermute | solution.py:22
  190.7 2.2 collective-permute-done.16
  194.1 16.1 %broadcast_multiply_fusion = (f32[4,16,64,128]{3,0,2,1:T(4,128)S(1)}, f32[4,16,64,128]{3,0,2,1:T(4,128)}) fusion(f32[4,16,64,128]{3,0,2,1:T(4,128)S(1)} %copy-done.26, f32[4,16,64,128]{3,0,2,1:T(4,128)S(1)} %copy-done.3, f32[4,16,64,1]{3,0,2,1:T(4,128)S(1)} %copy-done.10, f32[16,64,128]{2,1,0:T(8,128)S(1)} %copy-done.23, f32[4,16,64,1]{3,0,2,1:T(4,128)S(1)} %copy-done.8, ...), kind=kLoop, calls=%fused_computation.175 | loop fusion | flops 19922944 | bytes 11908224 | tf_op jit(solution)/shard_map/div | solution.py:81
  210.2 3.3 fusion.94
  213.5 2.0 copy.73
  216.7 2.0 copy.72
  218.7 4.3 collective-permute-start.18
  223.0 1.9 copy.75
  224.9 1.8 copy.74
  227.9 1.6 collective-permute-start.21
  229.5 5.1 %collective-permute-start.20 = (f32[4,16,1,130]{3,0,2,1:T(4,128)S(1)}, f32[4,16,1,130]{3,0,2,1:T(4,128)S(1)}, u32[]{:S(2)}, u32[]{:S(2)}) collective-permute-start(f32[4,16,1,130]{3,0,2,1:T(4,128)S(1)} %get-tuple-element.25), channel_id=1, source_target_pairs={{0,8},{8,16},{16,24},{1,9},{9,17},{17,25},{2,10},{10,18},{18,26},{... | collective-permute-start | bytes 99848 | tf_op jit(solution)/shard_map/ppermute | solution.py:22
  236.2 1.9 collective-permute-start.22
  238.1 5.5 %collective-permute-start.23 = (f32[4,1,66,130]{3,0,2,1:T(4,128)S(1)}, f32[4,1,66,130]{3,0,2,1:T(4,128)S(1)}, u32[]{:S(2)}, u32[]{:S(2)}) collective-permute-start(f32[4,1,66,130]{3,0,2,1:T(4,128)S(1)} %get-tuple-element.19), channel_id=1, source_target_pairs={{0,1},{1,2},{2,3},{3,4},{4,5},{5,6},{6,7},{8,9},{9,10},{10,11},{11... | collective-permute-start | bytes 411848 | tf_op jit(solution)/shard_map/ppermute | solution.py:22
  243.6 2.2 collective-permute-done.22
  247.0 16.2 %fusion.4 = f32[4,16,64,128]{3,0,2,1:T(4,128)} fusion(f32[4,16,64,128]{3,0,2,1:T(4,128)S(1)} %copy-done.5, f32[4,16,64,1]{3,0,2,1:T(4,128)S(1)} %copy-done.12, f32[4,16,64,1]{3,0,2,1:T(4,128)S(1)} %copy-done.11, f32[4,16,1,130]{3,0,2,1:T(4,128)S(1)} %collective-permute-done.20, f32[4,16,1,130]{3,0,2,1:T(4,128)S(1)} %collective-permute-done.21, ...), kind=kLoop, calls=%fused_computation.9 | loop fusion | flops 19922944 | bytes 9811072 | tf_op jit(solution)/shard_map/div | solution.py:81
  263.2 31.5 %concatenate.144 = f32[20,16,64,128]{3,0,2,1:T(8,128)} concatenate(f32[4,16,64,128]{3,0,2,1:T(4,128)} %copy-done.6, f32[4,16,64,128]{3,0,2,1:T(4,128)S(1)} %get-tuple-element.12, f32[4,16,64,128]{3,0,2,1:T(4,128)} %copy-done.2, f32[4,16,64,128]{3,0,2,1:T(4,128)} %copy-done.4, f32[4,16,64,128]{3,0,2,1:T(4,128)} %fusion.4), dimensions={0} | concatenate | bytes 20971520 | tf_op jit(solution)/shard_map/concatenate | solution.py:85
  294.7 17.6 %convolution_bitcast_fusion = f32[20,20]{1,0:T(8,128)S(1)} fusion(f32[20,16,64,128]{3,0,2,1:T(8,128)} %concatenate.144), kind=kOutput, calls=%fused_computation.162 | convolution fusion | flops 629145600 | bytes 10487360 | tf_op jit(solution)/shard_map/dot_general | solution.py:86
  312.4 70.0 %psum.7 = f32[20,20]{1,0:T(8,128)S(1)} all-reduce(f32[20,20]{1,0:T(8,128)S(1)} %convolution_bitcast_fusion), channel_id=1, replica_groups=mesh['gx'=4,'gy'=4,'gz'=8] {'gx','gy','gz'}, use_global_device_ids=true, to_apply=%region_0.0 | all-reduce | flops 400 | bytes 3200 | tf_op jit(solution)/shard_map/psum | solution.py:95
  417.3 1.8 stack.59
  421.0 5.6 %subtract_divide_fusion = (f32[1,4]{0,1:T(4,128)S(1)}, f32[1,4]{0,1:T(4,128)S(1)}) fusion(f32[]{:T(128)} %bitcast.21, f32[]{:T(128)} %bitcast.20, f32[]{:T(128)} %bitcast.19, f32[]{:T(128)} %bitcast.15, f32[]{:T(128)} %bitcast.5, f32[]{:T(128)} %bitcast.16, f32[]{:T(128)} %bitcast.11, f32[]{:T(128)} %bitcast.18, f32[]{:T(128)} %bitcast.17, f32[]{:T(128)} %bitcast.7), kind=kLoop, calls=%fused_computation.255 | loop fusion | flops 92 | bytes 72 | tf_op jit(solution)/shard_map/div | solution.py:53
  426.6 4.3 fusion.81
  431.0 1.6 copy.80
  (224 shorter events, 49.9 us)
Async XLA Ops:
  0.6 3.1 copy-start.25
  3.7 51.4 %copy-start.6 = (f32[4,16,64,128]{3,0,2,1:T(4,128)}, f32[4,16,64,128]{3,0,2,1:T(4,128)S(1)}, u32[]{:S(2)}) copy-start(f32[4,16,64,128]{3,0,2,1:T(4,128)S(1)} %copy.78) | copy-start | bytes 6291460
  11.3 8.6 %collective-permute-start.1 = (f32[5,16,64,1]{2,1,3,0:T(8,128)S(1)}, f32[5,16,64,1]{2,1,3,0:T(8,128)S(1)}, u32[]{:S(2)}, u32[]{:S(2)}) collective-permute-start(f32[5,16,64,1]{2,1,3,0:T(8,128)S(1)} %copy.35), channel_id=1, source_target_pairs={{32,0},{64,32},{96,64},{33,1},{65,33},{97,65},{34,2},{66,34},{98,6... | collective-permute-start | bytes 61448 | tf_op jit(solution)/shard_map/ppermute | solution.py:23
  15.3 7.3 %collective-permute-start = (f32[5,16,64,1]{2,1,3,0:T(8,128)S(1)}, f32[5,16,64,1]{2,1,3,0:T(8,128)S(1)}, u32[]{:S(2)}, u32[]{:S(2)}) collective-permute-start(f32[5,16,64,1]{2,1,3,0:T(8,128)S(1)} %copy.34), channel_id=1, source_target_pairs={{0,32},{32,64},{64,96},{1,33},{33,65},{65,97},{2,34},{34,66},{66,9... | collective-permute-start | bytes 61448 | tf_op jit(solution)/shard_map/ppermute | solution.py:22
  25.2 11.3 %copy-start = (f32[5,16,64,1]{3,0,2,1:T(8,128)S(1)}, f32[5,16,64,1]{3,0,2,1:T(8,128)}, u32[]{:S(2)}) copy-start(f32[5,16,64,1]{3,0,2,1:T(8,128)} %copy.37) | copy-start | bytes 61444
  25.2 11.3 %copy-start.1 = (f32[5,16,64,1]{3,0,2,1:T(8,128)S(1)}, f32[5,16,64,1]{3,0,2,1:T(8,128)}, u32[]{:S(2)}) copy-start(f32[5,16,64,1]{3,0,2,1:T(8,128)} %copy.36) | copy-start | bytes 61444
  26.6 6.0 %collective-permute-start.2 = (f32[5,16,1,130]{3,0,2,1:T(8,128)S(1)}, f32[5,16,1,130]{3,0,2,1:T(8,128)S(1)}, u32[]{:S(2)}, u32[]{:S(2)}) collective-permute-start(f32[5,16,1,130]{3,0,2,1:T(8,128)S(1)} %get-tuple-element.16), channel_id=1, source_target_pairs={{0,8},{8,16},{16,24},{1,9},{9,17},{17,25},{2,10},{10,18},{18,26},{... | collective-permute-start | bytes 124808 | tf_op jit(solution)/shard_map/ppermute | solution.py:22
  30.6 5.9 %collective-permute-start.3 = (f32[5,16,1,130]{3,0,2,1:T(8,128)S(1)}, f32[5,16,1,130]{3,0,2,1:T(8,128)S(1)}, u32[]{:S(2)}, u32[]{:S(2)}) collective-permute-start(f32[5,16,1,130]{3,0,2,1:T(8,128)S(1)} %get-tuple-element.17), channel_id=1, source_target_pairs={{8,0},{16,8},{24,16},{9,1},{17,9},{25,17},{10,2},{18,10},{26,18},{... | collective-permute-start | bytes 124808 | tf_op jit(solution)/shard_map/ppermute | solution.py:23
  40.0 10.7 %collective-permute-start.5 = (f32[5,1,66,130]{2,1,3,0:T(1,128)}, f32[5,1,66,130]{2,1,3,0:T(1,128)}, u32[]{:S(2)}, u32[]{:S(2)}) collective-permute-start(f32[5,1,66,130]{2,1,3,0:T(1,128)} %copy.39), channel_id=1, source_target_pairs={{1,0},{2,1},{3,2},{4,3},{5,4},{6,5},{7,6},{9,8},{10,9},{11,10},{12... | collective-permute-start | bytes 514808 | tf_op jit(solution)/shard_map/ppermute | solution.py:23
  45.4 7.5 %collective-permute-start.4 = (f32[5,1,66,130]{2,1,3,0:T(1,128)}, f32[5,1,66,130]{2,1,3,0:T(1,128)}, u32[]{:S(2)}, u32[]{:S(2)}) collective-permute-start(f32[5,1,66,130]{2,1,3,0:T(1,128)} %copy.38), channel_id=1, source_target_pairs={{0,1},{1,2},{2,3},{3,4},{4,5},{5,6},{6,7},{8,9},{9,10},{10,11},{11... | collective-permute-start | bytes 514808 | tf_op jit(solution)/shard_map/ppermute | solution.py:22
  52.2 13.3 %copy-start.30 = (f32[5,1,66,130]{3,0,2,1:T(8,128)}, f32[5,1,66,130]{3,0,2,1:T(8,128)S(1)}, u32[]{:S(2)}) copy-start(f32[5,1,66,130]{3,0,2,1:T(8,128)S(1)} %copy.41) | copy-start | bytes 514804
  72.7 1.6 copy-start.33
  74.3 5.1 %copy-start.32 = (f32[16,64,128]{1,2,0:T(8,128)S(1)}, f32[16,64,128]{1,2,0:T(8,128)}, u32[]{:S(2)}) copy-start(f32[16,64,128]{1,2,0:T(8,128)} %get-tuple-element.42) | copy-start | bytes 1572868
  74.6 5.9 %copy-start.31 = (f32[16,64,128]{1,2,0:T(8,128)S(1)}, f32[16,64,128]{1,2,0:T(8,128)}, u32[]{:S(2)}) copy-start(f32[16,64,128]{1,2,0:T(8,128)} %get-tuple-element.43) | copy-start | bytes 1572868
  110.1 7.3 %collective-permute-start.7 = (f32[4,16,64,1]{2,1,3,0:T(8,128)S(1)}, f32[4,16,64,1]{2,1,3,0:T(8,128)S(1)}, u32[]{:S(2)}, u32[]{:S(2)}) collective-permute-start(f32[4,16,64,1]{2,1,3,0:T(8,128)S(1)} %copy.61), channel_id=1, source_target_pairs={{32,0},{64,32},{96,64},{33,1},{65,33},{97,65},{34,2},{66,34},{98,6... | collective-permute-start | bytes 49160 | tf_op jit(solution)/shard_map/ppermute | solution.py:23
  113.3 5.8 %collective-permute-start.6 = (f32[4,16,64,1]{2,1,3,0:T(8,128)S(1)}, f32[4,16,64,1]{2,1,3,0:T(8,128)S(1)}, u32[]{:S(2)}, u32[]{:S(2)}) collective-permute-start(f32[4,16,64,1]{2,1,3,0:T(8,128)S(1)} %copy.60), channel_id=1, source_target_pairs={{0,32},{32,64},{64,96},{1,33},{33,65},{65,97},{2,34},{34,66},{66,9... | collective-permute-start | bytes 49160 | tf_op jit(solution)/shard_map/ppermute | solution.py:22
  121.0 8.4 %copy-start.7 = (f32[4,16,64,1]{3,0,2,1:T(4,128)S(1)}, f32[4,16,64,1]{3,0,2,1:T(4,128)}, u32[]{:S(2)}) copy-start(f32[4,16,64,1]{3,0,2,1:T(4,128)} %copy.63) | copy-start | bytes 49156
  121.0 8.4 %copy-start.9 = (f32[4,16,64,1]{3,0,2,1:T(4,128)S(1)}, f32[4,16,64,1]{3,0,2,1:T(4,128)}, u32[]{:S(2)}) copy-start(f32[4,16,64,1]{3,0,2,1:T(4,128)} %copy.62) | copy-start | bytes 49156
  122.2 5.9 %collective-permute-start.9 = (f32[4,16,1,130]{3,0,2,1:T(4,128)S(1)}, f32[4,16,1,130]{3,0,2,1:T(4,128)S(1)}, u32[]{:S(2)}, u32[]{:S(2)}) collective-permute-start(f32[4,16,1,130]{3,0,2,1:T(4,128)S(1)} %get-tuple-element.28), channel_id=1, source_target_pairs={{8,0},{16,8},{24,16},{9,1},{17,9},{25,17},{10,2},{18,10},{26,18},{... | collective-permute-start | bytes 99848 | tf_op jit(solution)/shard_map/ppermute | solution.py:23
  123.6 17.5 %copy-start.13 = (f32[16,64,128]{2,1,0:T(8,128)S(1)}, f32[16,64,128]{2,1,0:T(8,128)}, u32[]{:S(2)}) copy-start(f32[16,64,128]{2,1,0:T(8,128)} %copy.51) | copy-start | bytes 1572868
  123.6 17.5 %copy-start.16 = (f32[16,64,128]{2,1,0:T(8,128)S(1)}, f32[16,64,128]{2,1,0:T(8,128)}, u32[]{:S(2)}) copy-start(f32[16,64,128]{2,1,0:T(8,128)} %copy.49) | copy-start | bytes 1572868
  123.6 17.5 %copy-start.19 = (f32[16,64,128]{2,1,0:T(8,128)S(1)}, f32[16,64,128]{2,1,0:T(8,128)}, u32[]{:S(2)}) copy-start(f32[16,64,128]{2,1,0:T(8,128)} %copy.46) | copy-start | bytes 1572868
  123.6 17.5 %copy-start.22 = (f32[16,64,128]{2,1,0:T(8,128)S(1)}, f32[16,64,128]{2,1,0:T(8,128)}, u32[]{:S(2)}) copy-start(f32[16,64,128]{2,1,0:T(8,128)} %copy.56) | copy-start | bytes 1572868
  123.6 17.5 %copy-start.27 = (f32[4,16,64,128]{3,0,2,1:T(4,128)S(1)}, f32[4,16,64,128]{3,0,2,1:T(4,128)}, u32[]{:S(2)}) copy-start(f32[4,16,64,128]{3,0,2,1:T(4,128)} %get-tuple-element.13) | copy-start | bytes 6291460
  123.7 5.8 %collective-permute-start.8 = (f32[4,16,1,130]{3,0,2,1:T(4,128)S(1)}, f32[4,16,1,130]{3,0,2,1:T(4,128)S(1)}, u32[]{:S(2)}, u32[]{:S(2)}) collective-permute-start(f32[4,16,1,130]{3,0,2,1:T(4,128)S(1)} %get-tuple-element.29), channel_id=1, source_target_pairs={{0,8},{8,16},{16,24},{1,9},{9,17},{17,25},{2,10},{10,18},{18,26},{... | collective-permute-start | bytes 99848 | tf_op jit(solution)/shard_map/ppermute | solution.py:22
  129.9 10.0 %collective-permute-start.10 = (f32[4,1,66,130]{3,0,2,1:T(4,128)S(1)}, f32[4,1,66,130]{3,0,2,1:T(4,128)S(1)}, u32[]{:S(2)}, u32[]{:S(2)}) collective-permute-start(f32[4,1,66,130]{3,0,2,1:T(4,128)S(1)} %get-tuple-element.22), channel_id=1, source_target_pairs={{1,0},{2,1},{3,2},{4,3},{5,4},{6,5},{7,6},{9,8},{10,9},{11,10},{12... | collective-permute-start | bytes 411848 | tf_op jit(solution)/shard_map/ppermute | solution.py:23
  131.8 9.3 %collective-permute-start.11 = (f32[4,1,66,130]{3,0,2,1:T(4,128)S(1)}, f32[4,1,66,130]{3,0,2,1:T(4,128)S(1)}, u32[]{:S(2)}, u32[]{:S(2)}) collective-permute-start(f32[4,1,66,130]{3,0,2,1:T(4,128)S(1)} %get-tuple-element.23), channel_id=1, source_target_pairs={{0,1},{1,2},{2,3},{3,4},{4,5},{5,6},{6,7},{8,9},{9,10},{10,11},{11... | collective-permute-start | bytes 411848 | tf_op jit(solution)/shard_map/ppermute | solution.py:22
  157.2 3.3 copy-start.2
  162.5 7.6 %collective-permute-start.13 = (f32[4,16,64,1]{2,1,3,0:T(8,128)S(1)}, f32[4,16,64,1]{2,1,3,0:T(8,128)S(1)}, u32[]{:S(2)}, u32[]{:S(2)}) collective-permute-start(f32[4,16,64,1]{2,1,3,0:T(8,128)S(1)} %copy.67), channel_id=1, source_target_pairs={{32,0},{64,32},{96,64},{33,1},{65,33},{97,65},{34,2},{66,34},{98,6... | collective-permute-start | bytes 49160 | tf_op jit(solution)/shard_map/ppermute | solution.py:23
  165.8 6.2 %collective-permute-start.12 = (f32[4,16,64,1]{2,1,3,0:T(8,128)S(1)}, f32[4,16,64,1]{2,1,3,0:T(8,128)S(1)}, u32[]{:S(2)}, u32[]{:S(2)}) collective-permute-start(f32[4,16,64,1]{2,1,3,0:T(8,128)S(1)} %copy.66), channel_id=1, source_target_pairs={{0,32},{32,64},{64,96},{1,33},{33,65},{65,97},{2,34},{34,66},{66,9... | collective-permute-start | bytes 49160 | tf_op jit(solution)/shard_map/ppermute | solution.py:22
  173.8 9.0 %copy-start.3 = (f32[4,16,64,128]{3,0,2,1:T(4,128)S(1)}, f32[4,16,64,128]{3,0,2,1:T(4,128)}, u32[]{:S(2)}) copy-start(f32[4,16,64,128]{3,0,2,1:T(4,128)} %copy-done.2) | copy-start | bytes 6291460
  173.8 9.0 %copy-start.8 = (f32[4,16,64,1]{3,0,2,1:T(4,128)S(1)}, f32[4,16,64,1]{3,0,2,1:T(4,128)}, u32[]{:S(2)}) copy-start(f32[4,16,64,1]{3,0,2,1:T(4,128)} %copy.69) | copy-start | bytes 49156
  173.8 9.0 %copy-start.10 = (f32[4,16,64,1]{3,0,2,1:T(4,128)S(1)}, f32[4,16,64,1]{3,0,2,1:T(4,128)}, u32[]{:S(2)}) copy-start(f32[4,16,64,1]{3,0,2,1:T(4,128)} %copy.68) | copy-start | bytes 49156
  174.9 6.5 %collective-permute-start.15 = (f32[4,16,1,130]{3,0,2,1:T(4,128)S(1)}, f32[4,16,1,130]{3,0,2,1:T(4,128)S(1)}, u32[]{:S(2)}, u32[]{:S(2)}) collective-permute-start(f32[4,16,1,130]{3,0,2,1:T(4,128)S(1)} %get-tuple-element.26), channel_id=1, source_target_pairs={{8,0},{16,8},{24,16},{9,1},{17,9},{25,17},{10,2},{18,10},{26,18},{... | collective-permute-start | bytes 99848 | tf_op jit(solution)/shard_map/ppermute | solution.py:23
  176.5 17.6 %copy-start.14 = (f32[16,64,128]{2,1,0:T(8,128)S(1)}, f32[16,64,128]{2,1,0:T(8,128)}, u32[]{:S(2)}) copy-start(f32[16,64,128]{2,1,0:T(8,128)} %copy.51) | copy-start | bytes 1572868
  176.5 17.6 %copy-start.17 = (f32[16,64,128]{2,1,0:T(8,128)S(1)}, f32[16,64,128]{2,1,0:T(8,128)}, u32[]{:S(2)}) copy-start(f32[16,64,128]{2,1,0:T(8,128)} %copy.49) | copy-start | bytes 1572868
  176.5 17.6 %copy-start.20 = (f32[16,64,128]{2,1,0:T(8,128)S(1)}, f32[16,64,128]{2,1,0:T(8,128)}, u32[]{:S(2)}) copy-start(f32[16,64,128]{2,1,0:T(8,128)} %copy.46) | copy-start | bytes 1572868
  176.5 17.6 %copy-start.23 = (f32[16,64,128]{2,1,0:T(8,128)S(1)}, f32[16,64,128]{2,1,0:T(8,128)}, u32[]{:S(2)}) copy-start(f32[16,64,128]{2,1,0:T(8,128)} %copy.56) | copy-start | bytes 1572868
  176.5 17.6 %copy-start.26 = (f32[4,16,64,128]{3,0,2,1:T(4,128)S(1)}, f32[4,16,64,128]{3,0,2,1:T(4,128)}, u32[]{:S(2)}) copy-start(f32[4,16,64,128]{3,0,2,1:T(4,128)} %get-tuple-element.11) | copy-start | bytes 6291460
  176.5 6.2 %collective-permute-start.14 = (f32[4,16,1,130]{3,0,2,1:T(4,128)S(1)}, f32[4,16,1,130]{3,0,2,1:T(4,128)S(1)}, u32[]{:S(2)}, u32[]{:S(2)}) collective-permute-start(f32[4,16,1,130]{3,0,2,1:T(4,128)S(1)} %get-tuple-element.27), channel_id=1, source_target_pairs={{0,8},{8,16},{16,24},{1,9},{9,17},{17,25},{2,10},{10,18},{18,26},{... | collective-permute-start | bytes 99848 | tf_op jit(solution)/shard_map/ppermute | solution.py:22
  183.2 9.7 %collective-permute-start.16 = (f32[4,1,66,130]{3,0,2,1:T(4,128)S(1)}, f32[4,1,66,130]{3,0,2,1:T(4,128)S(1)}, u32[]{:S(2)}, u32[]{:S(2)}) collective-permute-start(f32[4,1,66,130]{3,0,2,1:T(4,128)S(1)} %get-tuple-element.20), channel_id=1, source_target_pairs={{1,0},{2,1},{3,2},{4,3},{5,4},{6,5},{7,6},{9,8},{10,9},{11,10},{12... | collective-permute-start | bytes 411848 | tf_op jit(solution)/shard_map/ppermute | solution.py:23
  185.2 8.9 %collective-permute-start.17 = (f32[4,1,66,130]{3,0,2,1:T(4,128)S(1)}, f32[4,1,66,130]{3,0,2,1:T(4,128)S(1)}, u32[]{:S(2)}, u32[]{:S(2)}) collective-permute-start(f32[4,1,66,130]{3,0,2,1:T(4,128)S(1)} %get-tuple-element.21), channel_id=1, source_target_pairs={{0,1},{1,2},{2,3},{3,4},{4,5},{5,6},{6,7},{8,9},{9,10},{10,11},{11... | collective-permute-start | bytes 411848 | tf_op jit(solution)/shard_map/ppermute | solution.py:22
  210.2 3.3 copy-start.4
  215.4 7.6 %collective-permute-start.19 = (f32[4,16,64,1]{2,1,3,0:T(8,128)S(1)}, f32[4,16,64,1]{2,1,3,0:T(8,128)S(1)}, u32[]{:S(2)}, u32[]{:S(2)}) collective-permute-start(f32[4,16,64,1]{2,1,3,0:T(8,128)S(1)} %copy.73), channel_id=1, source_target_pairs={{32,0},{64,32},{96,64},{33,1},{65,33},{97,65},{34,2},{66,34},{98,6... | collective-permute-start | bytes 49160 | tf_op jit(solution)/shard_map/ppermute | solution.py:23
  218.7 6.2 %collective-permute-start.18 = (f32[4,16,64,1]{2,1,3,0:T(8,128)S(1)}, f32[4,16,64,1]{2,1,3,0:T(8,128)S(1)}, u32[]{:S(2)}, u32[]{:S(2)}) collective-permute-start(f32[4,16,64,1]{2,1,3,0:T(8,128)S(1)} %copy.72), channel_id=1, source_target_pairs={{0,32},{32,64},{64,96},{1,33},{33,65},{65,97},{2,34},{34,66},{66,9... | collective-permute-start | bytes 49160 | tf_op jit(solution)/shard_map/ppermute | solution.py:22
  226.7 9.0 %copy-start.5 = (f32[4,16,64,128]{3,0,2,1:T(4,128)S(1)}, f32[4,16,64,128]{3,0,2,1:T(4,128)}, u32[]{:S(2)}) copy-start(f32[4,16,64,128]{3,0,2,1:T(4,128)} %copy-done.4) | copy-start | bytes 6291460
  226.7 9.0 %copy-start.11 = (f32[4,16,64,1]{3,0,2,1:T(4,128)S(1)}, f32[4,16,64,1]{3,0,2,1:T(4,128)}, u32[]{:S(2)}) copy-start(f32[4,16,64,1]{3,0,2,1:T(4,128)} %copy.75) | copy-start | bytes 49156
  226.7 9.0 %copy-start.12 = (f32[4,16,64,1]{3,0,2,1:T(4,128)S(1)}, f32[4,16,64,1]{3,0,2,1:T(4,128)}, u32[]{:S(2)}) copy-start(f32[4,16,64,1]{3,0,2,1:T(4,128)} %copy.74) | copy-start | bytes 49156
  227.9 6.8 %collective-permute-start.21 = (f32[4,16,1,130]{3,0,2,1:T(4,128)S(1)}, f32[4,16,1,130]{3,0,2,1:T(4,128)S(1)}, u32[]{:S(2)}, u32[]{:S(2)}) collective-permute-start(f32[4,16,1,130]{3,0,2,1:T(4,128)S(1)} %get-tuple-element.24), channel_id=1, source_target_pairs={{8,0},{16,8},{24,16},{9,1},{17,9},{25,17},{10,2},{18,10},{26,18},{... | collective-permute-start | bytes 99848 | tf_op jit(solution)/shard_map/ppermute | solution.py:23
  229.4 17.6 %copy-start.15 = (f32[16,64,128]{2,1,0:T(8,128)S(1)}, f32[16,64,128]{2,1,0:T(8,128)}, u32[]{:S(2)}) copy-start(f32[16,64,128]{2,1,0:T(8,128)} %copy.51) | copy-start | bytes 1572868
  229.4 17.6 %copy-start.18 = (f32[16,64,128]{2,1,0:T(8,128)S(1)}, f32[16,64,128]{2,1,0:T(8,128)}, u32[]{:S(2)}) copy-start(f32[16,64,128]{2,1,0:T(8,128)} %copy.49) | copy-start | bytes 1572868
  229.4 17.6 %copy-start.21 = (f32[16,64,128]{2,1,0:T(8,128)S(1)}, f32[16,64,128]{2,1,0:T(8,128)}, u32[]{:S(2)}) copy-start(f32[16,64,128]{2,1,0:T(8,128)} %copy.46) | copy-start | bytes 1572868
  229.4 17.6 %copy-start.24 = (f32[16,64,128]{2,1,0:T(8,128)S(1)}, f32[16,64,128]{2,1,0:T(8,128)}, u32[]{:S(2)}) copy-start(f32[16,64,128]{2,1,0:T(8,128)} %copy.56) | copy-start | bytes 1572868
  229.5 17.6 %copy-start.29 = (f32[4,16,64,128]{3,0,2,1:T(4,128)S(1)}, f32[4,16,64,128]{3,0,2,1:T(4,128)}, u32[]{:S(2)}) copy-start(f32[4,16,64,128]{3,0,2,1:T(4,128)} %get-tuple-element.9) | copy-start | bytes 6291460
  229.5 6.2 %collective-permute-start.20 = (f32[4,16,1,130]{3,0,2,1:T(4,128)S(1)}, f32[4,16,1,130]{3,0,2,1:T(4,128)S(1)}, u32[]{:S(2)}, u32[]{:S(2)}) collective-permute-start(f32[4,16,1,130]{3,0,2,1:T(4,128)S(1)} %get-tuple-element.25), channel_id=1, source_target_pairs={{0,8},{8,16},{16,24},{1,9},{9,17},{17,25},{2,10},{10,18},{18,26},{... | collective-permute-start | bytes 99848 | tf_op jit(solution)/shard_map/ppermute | solution.py:22
  236.2 9.7 %collective-permute-start.22 = (f32[4,1,66,130]{3,0,2,1:T(4,128)S(1)}, f32[4,1,66,130]{3,0,2,1:T(4,128)S(1)}, u32[]{:S(2)}, u32[]{:S(2)}) collective-permute-start(f32[4,1,66,130]{3,0,2,1:T(4,128)S(1)} %get-tuple-element.18), channel_id=1, source_target_pairs={{1,0},{2,1},{3,2},{4,3},{5,4},{6,5},{7,6},{9,8},{10,9},{11,10},{12... | collective-permute-start | bytes 411848 | tf_op jit(solution)/shard_map/ppermute | solution.py:23
  238.1 8.9 %collective-permute-start.23 = (f32[4,1,66,130]{3,0,2,1:T(4,128)S(1)}, f32[4,1,66,130]{3,0,2,1:T(4,128)S(1)}, u32[]{:S(2)}, u32[]{:S(2)}) collective-permute-start(f32[4,1,66,130]{3,0,2,1:T(4,128)S(1)} %get-tuple-element.19), channel_id=1, source_target_pairs={{0,1},{1,2},{2,3},{3,4},{4,5},{5,6},{6,7},{8,9},{9,10},{10,11},{11... | collective-permute-start | bytes 411848 | tf_op jit(solution)/shard_map/ppermute | solution.py:22
  294.7 131.9 %copy-start.28 = (f32[4,16,64,128]{3,2,1,0:T(8,128)S(1)}, f32[4,16,64,128]{3,2,1,0:T(8,128)}, u32[]{:S(2)}) copy-start(f32[4,16,64,128]{3,2,1,0:T(8,128)} %param.2) | copy-start | bytes 6291460
where the time goes:
time: 440 us; the launch traced here: 433 us
  local copies, waits for them, and re-layouts  118 us (27%)
  other arithmetic  108 us (25%)
  starting transfers between devices  77 us (18%)
  blocking collectives  70 us (16%)
  matrix products  22 us (5%)
  waiting for transfers between devices  21.2 us (5%)
  between operations  16.3 us (4%)
    div x4, other arithmetic, shards(): (stencil_inner(current_pad, kpad) - basis_shift * centre) / basis_scale  71.3 us
    psum x1, blocking collectives, shards(): gram = lax.psum(local_gram, ('gx', 'gy', 'gz'))  70 us
    ppermute x12, starting transfers between devices, extended(): before = lax.ppermute(last, axis, up)  55.9 us
    concatenate x1, local copies, waits for them, and re-layouts, shards(): basis = jnp.concatenate(blocks, 0).reshape(KRYLOV, -1)  31.5 us
    ppermute x12, starting transfers between devices, extended(): after = lax.ppermute(leading, axis, down)  21.2 us
    slice x8, local copies, waits for them, and re-layouts, extended(): leading = lax.slice_in_dim(value, 0, width, axis=dim)  20.5 us
    dot_general x1, matrix products, shards(): local_gram = jnp.dot(basis, basis.T, precision=lax.Precision.HIGHEST)  17.6 us
    concatenate x4, other arithmetic, extended(): value = jnp.concatenate([before, value, after], axis=dim)  13.9 us
  transfers between devices with their start and end apart: 24, of which 13 were waited for; matrix products, arithmetic and copies ran while one was open for 4% of the time, Pallas kernels for 0%

commit v1 on v0

v1 whole, which is shorter than its diff:
```python
import jax
import jax.numpy as jnp
from jax import lax
from jax.experimental import pallas as pl
from jax.experimental.pallas import tpu as pltpu
from jax.sharding import PartitionSpec as P

COLS = 4
BASIS = 4
KRYLOV = 20
MOMENTS = 2 * BASIS + 1
PAIRS = COLS * (COLS + 1) // 2
DEEP = BASIS

basis_shift = 6.0
basis_scale = 3.0

F32 = jnp.float32
VMEM = pl.BlockSpec(memory_space=pltpu.VMEM)
PARAMS = pltpu.CompilerParams(vmem_limit_bytes=48 * 1024 * 1024)


def lanes(rows):
    return lax.broadcasted_iota(jnp.int32, (rows, 128), 1)


def sublanes(rows):
    return lax.broadcasted_iota(jnp.int32, (rows, 128), 0)


def permute_lanes(value, index):
    return jnp.take_along_axis(value, index, axis=1, mode="promise_in_bounds")


def even_first(axis, first, second):
    return jnp.where(lax.axis_index(axis) % 2 == 0, first, second)


def sides(axis, first, second):
    at = lax.axis_index(axis)
    upper = jnp.where(at == lax.axis_size(axis) - 1, 0.0, even_first(axis, first, second))
    lower = jnp.where(at == 0, 0.0, even_first(axis, second, first))
    return upper, lower


def swap(first, second, axis):
    peers = lax.axis_size(axis)
    other = [(i, (i - 1 if i % 2 == 0 else i + 1) % peers) for i in range(peers)]
    second = lax.ppermute(second, axis, other)
    first = lax.ppermute(first, axis, [(i, i ^ 1) for i in range(peers)])
    return first, second


def pack_x_kernel(block, kappa, own, to_first, to_second):
    lane = lanes(64)
    offset, group = lane % 16, lane // 16
    keep = (offset < 4) | (offset >= 12)
    index = jnp.where(offset < 4, 124 + offset, jnp.where(offset >= 12, offset - 12, 0))

    def body(quad, carry):
        upper = jnp.zeros((64, 128), F32)
        lower = jnp.zeros((64, 128), F32)
        for part in range(4):
            z = quad * 4 + part
            strip = jnp.zeros((64, 128), F32)
            for g in range(COLS + 1):
                plane = block[g, z] if g < COLS else kappa[z]
                strip = jnp.where(keep & (group == g), permute_lanes(plane, index), strip)
            own[z] = strip
            here = offset // 4 == part
            upper = jnp.where(here, pltpu.roll(strip, 4 * part, 1), upper)
            lower = jnp.where(here, pltpu.roll(strip, (4 * part - 12) % 128, 1), lower)
        to_first[quad] = even_first("gx", upper, lower)
        to_second[quad] = even_first("gx", lower, upper)
        return carry

    lax.fori_loop(0, own.shape[0] // 4, body, 0)


def pack_x(block, kappa):
    nz, ny, nx = kappa.shape
    return pl.pallas_call(
        pack_x_kernel,
        out_shape=[
            jax.ShapeDtypeStruct((nz, ny, nx), F32),
            jax.ShapeDtypeStruct((nz // 4, ny, nx), F32),
            jax.ShapeDtypeStruct((nz // 4, ny, nx), F32),
        ],
        in_specs=[VMEM] * 2,
        out_specs=[VMEM] * 3,
        compiler_params=PARAMS,
        name="pack_x",
    )(block, kappa)


def pack_y_kernel(own, first, second, b_low, b_high, k_low, k_high, strip, to_first, to_second):
    offset = lanes(64) % 16
    half = sublanes(8) < 4

    def body(quad, carry):
        upper, lower = sides("gx", first[quad], second[quad])
        for part in range(4):
            z = quad * 4 + part
            beyond = jnp.where(
                offset < 8,
                pltpu.roll(upper, (4 - 4 * part) % 128, 1),
                pltpu.roll(lower, (8 - 4 * part) % 128, 1),
            )
            strip[z] = jnp.where((offset < 4) | (offset >= 12), own[z], beyond)
        return carry

    lax.fori_loop(0, strip.shape[0] // 4, body, 0)

    def pairs(duo, carry):
        z = duo * 2
        for a in range(COLS + 2):
            if a < COLS:
                low = [b_low[a, z + i] for i in range(2)]
                high = [b_high[a, z + i] for i in range(2)]
            elif a == COLS:
                low = [k_low[z + i] for i in range(2)]
                high = [k_high[z + i] for i in range(2)]
            else:
                low = [strip[z + i, 0:8] for i in range(2)]
                high = [strip[z + i, 56:64] for i in range(2)]
            upper = jnp.where(half, pltpu.roll(high[0], 4, 0), high[1])
            lower = jnp.where(half, low[0], pltpu.roll(low[1], 4, 0))
            to_first[a, duo] = even_first("gy", upper, lower)
            to_second[a, duo] = even_first("gy", lower, upper)
        return carry

    lax.fori_loop(0, strip.shape[0] // 2, pairs, 0)


def pack_y(block, kappa, own, first, second):
    nz, ny, nx = kappa.shape
    whole = lambda shape: pl.BlockSpec(shape, lambda i: (0,) * len(shape))
    edge4 = lambda at: pl.BlockSpec((COLS, nz, 8, nx), lambda i: (0, 0, at, 0))
    edge = lambda at: pl.BlockSpec((nz, 8, nx), lambda i: (0, at, 0))
    faces = (COLS + 2, nz // 2, 8, nx)
    return pl.pallas_call(
        pack_y_kernel,
        grid=(1,),
        out_shape=[
            jax.ShapeDtypeStruct((nz, ny, nx), F32),
            jax.ShapeDtypeStruct(faces, F32),
            jax.ShapeDtypeStruct(faces, F32),
        ],
        in_specs=[
            whole((nz, ny, nx)),
            whole((nz // 4, ny, nx)),
            whole((nz // 4, ny, nx)),
            edge4(0),
            edge4(ny // 8 - 1),
            edge(0),
            edge(ny // 8 - 1),
        ],
        out_specs=[whole((nz, ny, nx)), whole(faces), whole(faces)],
        compiler_params=PARAMS,
        name="pack_y",
    )(own, first, second, block, block, kappa, kappa)


def pack_z_kernel(first, second, b_low, b_high, k_low, k_high, s_low, s_high, rim, to_first, to_second):
    half = sublanes(8) < 4

    def pairs(duo, carry):
        for a in range(COLS + 2):
            upper, lower = sides("gy", first[a, duo], second[a, duo])
            rim[a, duo * 2] = jnp.where(half, upper, pltpu.roll(lower, 4, 0))
            rim[a, duo * 2 + 1] = jnp.where(half, pltpu.roll(upper, 4, 0), lower)
        return carry

    lax.fori_loop(0, rim.shape[1] // 2, pairs, 0)
    last = rim.shape[1] - DEEP
    ny = b_low.shape[2]

    def slabs(z, carry):
        for a in range(COLS + 2):
            if a < COLS:
                low, high = b_low[a, z], b_high[a, z]
            elif a == COLS:
                low, high = k_low[z], k_high[z]
            else:
                low, high = s_low[z], s_high[z]
            to_first[a, z, 0:ny] = even_first("gz", high, low)
            to_second[a, z, 0:ny] = even_first("gz", low, high)
            low, high = rim[a, z], rim[a, last + z]
            to_first[a, z, ny : ny + 8] = even_first("gz", high, low)
            to_second[a, z, ny : ny + 8] = even_first("gz", low, high)
        return carry

    lax.fori_loop(0, DEEP, slabs, 0)


def pack_z(block, kappa, strip, first, second):
    nz, ny, nx = kappa.shape
    whole = lambda shape: pl.BlockSpec(shape, lambda i: (0,) * len(shape))
    edge4 = lambda at: pl.BlockSpec((COLS, DEEP, ny, nx), lambda i: (0, at, 0, 0))
    edge = lambda at: pl.BlockSpec((DEEP, ny, nx), lambda i: (at, 0, 0))
    top = nz // DEEP - 1
    faces = (COLS + 2, nz // 2, 8, nx)
    rims = (COLS + 2, nz, 8, nx)
    slabs = (COLS + 2, DEEP, ny + 8, nx)
    return pl.pallas_call(
        pack_z_kernel,
        grid=(1,),
        out_shape=[jax.ShapeDtypeStruct(s, F32) for s in (rims, slabs, slabs)],
        in_specs=[whole(faces), whole(faces), edge4(0), edge4(top), edge(0), edge(top), edge(0), edge(top)],
        out_specs=[whole(rims), whole(slabs), whole(slabs)],
        compiler_params=PARAMS,
        name="pack_z",
    )(first, second, block, block, kappa, kappa, strip, strip)


NCELLROWS = 64
TILES = NCELLROWS // 8 + 1
ROWS = 8 * (TILES + 2)


def powers_kernel(block, kappa, strip, rim, first, second, out, field, side, kfield, kside, wts, swts, acc):
    nz = block.shape[1]
    ny = block.shape[2]
    depth = nz + 2 * DEEP
    lane8 = lanes(8)
    lane = lanes(ny + 8)
    klanes = 64 + lane % 16

    def lay(put, body, edge):
        put(8, ny, body)
        put(8 + ny, 8, edge)
        put(0, 8, edge)
        put(16 + ny, 8, body[0:8])

    def lay_all(ze, get):
        for a in range(COLS + 2):
            body, edge = get(a)
            if a < COLS:
                def put(row, count, value, a=a):
                    field[0, a, ze, row : row + count] = value
            elif a == COLS:
                def put(row, count, value):
                    kfield[ze, row : row + count] = value
            else:
                def put(row, count, value):
                    side[0, ze, row : row + count] = value
                    kside[ze, row : row + count] = permute_lanes(value, klanes[0:count])
            lay(put, body, edge)

    def own_slab(z, carry):
        def get(a):
            body = block[a, z] if a < COLS else kappa[z] if a == COLS else strip[z]
            return body, rim[a, z]

        lay_all(z + DEEP, get)
        return carry

    lax.fori_loop(0, nz, own_slab, 0)

    def far_slab(z, carry):
        def get_side(which):
            def get(a):
                values = sides("gz", first[a, z], second[a, z])[which]
                return values[0:ny], values[ny : ny + 8]

            return get

        lay_all(z, get_side(1))
        lay_all(z + DEEP + nz, get_side(0))
        return carry

    lax.fori_loop(0, DEEP, far_slab, 0)

    mid = slice(8, 16 + ny)
    up = slice(9, 17 + ny)
    down = slice(7, 15 + ny)
    kedge = jnp.where(lane == 127, 64 + 4, 64 + 11)

    def weights(ze, carry):
        for k_ref, w_ref, main in ((kfield, wts, True), (kside, swts, False)):
            k = k_ref[ze, mid]
            right = pltpu.roll(k, 127, 1)
            left = pltpu.roll(k, 1, 1)
            if main:
                beyond = permute_lanes(side[0, ze, mid], kedge)
                right = jnp.where(lane == 127, beyond, right)
                left = jnp.where(lane == 0, beyond, left)
            above = k_ref[ze, up]
            below = k_ref[ze, down]
            far = k_ref[jnp.minimum(ze + 1, depth - 1), mid]
            near = k_ref[jnp.maximum(ze - 1, 0), mid]
            total = 3.0 * k + 0.5 * (right + left + above + below + far + near)
            w_ref[0, ze, mid] = (total - basis_shift) / basis_scale

            def link(other):
                return jnp.where(jnp.minimum(k, other) > 0.0, (k + other) * (0.5 / basis_scale), 0.0)

            w_ref[1, ze, mid] = link(right)
            w_ref[2, ze, mid] = link(left)
            above = link(above)
            w_ref[3, ze, mid] = above
            w_ref[3, ze, 0:8] = above[ny : ny + 8]
            w_ref[4, ze, mid] = link(far)
        return carry

    lax.fori_loop(0, depth, weights, 0)
    acc[...] = jnp.zeros_like(acc)
    pairs = [(c, d) for c in range(COLS) for d in range(c, COLS)]

    for k in range(1, BASIS + 1):
        src, dst = (k - 1) % 2, k % 2
        final = k == BASIS

        def slab(ze, carry, inner, k=k, src=src, dst=dst, final=final):
            sums = {}
            for t in range(TILES):
                at = slice(8 + 8 * t, 16 + 8 * t)
                above = slice(9 + 8 * t, 17 + 8 * t)
                below = slice(7 + 8 * t, 15 + 8 * t)
                edge = side[src, ze, at]
                if not final:
                    new = swts[0, ze, at] * edge
                    new -= swts[1, ze, at] * pltpu.roll(edge, 127, 1)
                    new -= swts[2, ze, at] * pltpu.roll(edge, 1, 1)
                    new -= swts[3, ze, at] * side[src, ze, above]
                    new -= swts[3, ze, below] * side[src, ze, below]
                    new -= swts[4, ze, at] * side[src, ze + 1, at]
                    new -= swts[4, ze - 1, at] * side[src, ze - 1, at]
                    side[dst, ze, at] = new
                    if t == 0:
                        side[dst, ze, 8 + 8 * TILES : 16 + 8 * TILES] = new
                    if t == TILES - 1:
                        side[dst, ze, 0:8] = new
                if final and t == TILES - 1:
                    continue
                olds, news = [], []
                for c in range(COLS):
                    v = field[src, c, ze, at]
                    beyond = permute_lanes(edge, jnp.where(lane8 == 127, 16 * c + 4, 16 * c + 11))
                    right = jnp.where(lane8 == 127, beyond, pltpu.roll(v, 127, 1))
                    left = jnp.where(lane8 == 0, beyond, pltpu.roll(v, 1, 1))
                    new = wts[0, ze, at] * v
                    new -= wts[1, ze, at] * right
                    new -= wts[2, ze, at] * left
                    new -= wts[3, ze, at] * field[src, c, ze, above]
                    new -= wts[3, ze, below] * field[src, c, ze, below]
                    new -= wts[4, ze, at] * field[src, c, ze + 1, at]
                    new -= wts[4, ze - 1, at] * field[src, c, ze - 1, at]
                    if not final:
                        field[dst, c, ze, at] = new
                        if t == 0:
                            field[dst, c, ze, 8 + 8 * TILES : 16 + 8 * TILES] = new
                        if t == TILES - 1:
                            field[dst, c, ze, 0:8] = new
                    olds.append(v)
                    news.append(new)
                if inner and t < TILES - 1:
                    for p, (c, d) in enumerate(pairs):
                        if k == 1:
                            sums.setdefault(p, []).append(olds[c] * olds[d])
                        sums.setdefault((2 * k - 1) * PAIRS + p, []).append(olds[c] * news[d])
                        sums.setdefault(2 * k * PAIRS + p, []).append(news[c] * news[d])
            for m, terms in sums.items():
                total = terms[0]
                for term in terms[1:]:
                    total = total + term
                acc[m] += total
            return carry

        def outer(ze, carry, slab=slab):
            return slab(ze, carry, False)

        def inner(ze, carry, slab=slab):
            return slab(ze, carry, True)

        if k < DEEP:
            lax.fori_loop(k, DEEP, outer, 0)
            lax.fori_loop(DEEP + nz, depth - k, outer, 0)
        lax.fori_loop(DEEP, DEEP + nz, inner, 0)

    rows = jnp.sum(acc[...], axis=1)
    row = lax.dot_general(
        jnp.ones((8, 128), F32),
        rows,
        (((1,), (1,)), ((), ())),
        precision=lax.Precision.HIGHEST,
        preferred_element_type=F32,
    )
    out[...] = jnp.broadcast_to(row[0:1][None], out.shape)


def powers(block, kappa, strip, rim, first, second, peers):
    nz, ny, nx = kappa.shape
    depth = nz + 2 * DEEP
    slab = (depth, ROWS, nx)
    return pl.pallas_call(
        powers_kernel,
        out_shape=jax.ShapeDtypeStruct((peers, 1, 128), F32),
        in_specs=[VMEM] * 6,
        out_specs=VMEM,
        scratch_shapes=[
            pltpu.VMEM((2, COLS) + slab, F32),
            pltpu.VMEM((2,) + slab, F32),
            pltpu.VMEM(slab, F32),
            pltpu.VMEM(slab, F32),
            pltpu.VMEM((5,) + slab, F32),
            pltpu.VMEM((5,) + slab, F32),
            pltpu.VMEM((128, 8, 128), F32),
        ],
        compiler_params=PARAMS,
        name="powers",
    )(block, kappa, strip, rim, first, second)


def finish_kernel(ncells, parts, block, ortho, triangle, coef):
    @pl.when(pl.program_id(0) == 0)
    def _():
        row = jnp.sum(parts[...], axis=0) * (1.0 / ncells)
        row = jnp.broadcast_to(row, (24, 128))
        a, b = sublanes(24), lanes(24)
        c, d = a % 4, b % 4
        low, high = jnp.minimum(c, d), jnp.maximum(c, d)
        pair = low * 4 - (low * (low - 1)) // 2 + high - low
        inside = (a < KRYLOV) & (b < KRYLOV)
        index = jnp.where(inside, (a // 4 + b // 4) * PAIRS + pair, 127)
        matrix = permute_lanes(row, index)
        lane = lanes(1)
        uppers = []
        for k in range(KRYLOV):
            line = matrix[k : k + 1, :]
            pivot = line[:, k : k + 1]
            upper = jnp.where(lane >= k, line / jnp.sqrt(pivot), 0.0)
            uppers.append(upper)
            triangle[k : k + 1, :] = upper[:, 0:KRYLOV]
            if k + 1 < KRYLOV:
                matrix = matrix - matrix[:, k : k + 1] * (line / pivot)
        at = 0
        for i in range(COLS):
            for j in range(i, COLS):
                value = uppers[i][:, j : j + 1]
                value = 1.0 / value if i == j else value
                coef[at] = jnp.broadcast_to(value, (8, 128))
                at += 1

    u = {}
    at = 0
    for i in range(COLS):
        for j in range(i, COLS):
            u[i, j] = coef[at]
            at += 1

    def slab(z, carry):
        for t in range(ortho.shape[2] // 8):
            rows = slice(8 * t, 8 * t + 8)
            done = []
            for j in range(COLS):
                value = block[j, z, rows]
                for i in range(j):
                    value = value - u[i, j] * done[i]
                value = value * u[j, j]
                ortho[j, z, rows] = value
                done.append(value)
        return carry

    lax.fori_loop(0, ortho.shape[1], slab, 0)


def finish(parts, block, ncells):
    cols, nz, ny, nx = block.shape
    steps = 4
    piece = pl.BlockSpec((cols, nz // steps, ny, nx), lambda i: (0, i, 0, 0))
    return pl.pallas_call(
        lambda *refs: finish_kernel(ncells, *refs),
        grid=(steps,),
        out_shape=[
            jax.ShapeDtypeStruct(block.shape, F32),
            jax.ShapeDtypeStruct((KRYLOV, KRYLOV), F32),
        ],
        in_specs=[pl.BlockSpec(parts.shape, lambda i: (0, 0, 0)), piece],
        out_specs=[piece, pl.BlockSpec((KRYLOV, KRYLOV), lambda i: (0, 0))],
        scratch_shapes=[pltpu.VMEM((PAIRS, 8, 128), F32)],
        compiler_params=PARAMS,
        name="finish",
    )(parts, block)


def shards(block, kappa):
    axes = ("gx", "gy", "gz")
    peers = lax.axis_size(axes)
    ncells = float(kappa.size * peers)
    own, first, second = pack_x(block, kappa)
    first, second = swap(first, second, "gx")
    strip, first, second = pack_y(block, kappa, own, first, second)
    first, second = swap(first, second, "gy")
    rim, first, second = pack_z(block, kappa, strip, first, second)
    first, second = swap(first, second, "gz")
    moments = powers(block, kappa, strip, rim, first, second, peers)
    parts = lax.all_to_all(moments, axes, 0, 0, tiled=True)
    return tuple(finish(parts, block, ncells))


def solution(mesh):
    return jax.shard_map(
        shards,
        mesh=mesh,
        in_specs=(P(None, "gz", "gy", "gx"), P("gz", "gy", "gx")),
        out_specs=(P(None, "gz", "gy", "gx"), P()),
        check_vma=False,
    )
```

time: 440 us -> 88.1 us (0.20); the launches traced: 433 us -> 87.8 us
  local copies, waits for them, and re-layouts: 118 us -> 2.63 us
  other arithmetic: 108 us -> 0 us
  starting transfers between devices: 77 us -> 12.8 us
  blocking collectives: 70 us -> 17.7 us
  Pallas kernels: 0 us -> 35.9 us
  matrix products: 22 us -> 0 us
  between operations: 16.3 us -> 0.67 us
    div x7 -> x0, other arithmetic: 78.2 us -> none  [the longest x4 71.3 us: shards(): (stencil_inner(current_pad, kpad) - basis_shift * centre) / basis_scale]
    psum x1 -> x0, blocking collectives: 70 us -> none  [shards(): gram = lax.psum(local_gram, ('gx', 'gy', 'gz'))]
    ppermute x24 -> x6, starting transfers between devices: 77 us -> 12.8 us  [the longest x3 7.44 us: swap(): first = lax.ppermute(first, axis, [(i, i ^ 1) for i in range(peers)])]
    slice x56 -> x0, local copies, waits for them, and re-layouts: 50.5 us -> none  [the longest x8 20.5 us: extended(): leading = lax.slice_in_dim(value, 0, width, axis=dim)]
    pallas_call x0 -> x5, Pallas kernels: none -> 35.9 us  [the longest x1 28.8 us: powers(): pl.pallas_call(powers_kernel, out_shape=jax.ShapeDtypeStruct((peers, 1, 1...]
    concatenate x1 -> x0, local copies, waits for them, and re-layouts: 31.5 us -> none  [shards(): basis = jnp.concatenate(blocks, 0).reshape(KRYLOV, -1)]
    dot_general x2 -> x0, matrix products: 22 us -> none  [the longest x1 17.6 us: shards(): local_gram = jnp.dot(basis, basis.T, precision=lax.Precision.HIGHEST)]
    ppermute x10 -> x0, local copies, waits for them, and re-layouts: 19.9 us -> none  [the longest x5 10.3 us: extended(): before = lax.ppermute(last, axis, up)]
  transfers between devices with their start and end apart: 24 -> 6, of which waited for: 13 -> 6; matrix products, arithmetic and copies ran while one was open for 4% -> 0% of each run, Pallas kernels for 0% -> 0%
where the time goes in v1:
time: 88.1 us; the launch traced here: 87.8 us
  Pallas kernels  35.9 us (41%)
  waiting for transfers between devices  18.2 us (21%)
  blocking collectives  17.7 us (20%)
  starting transfers between devices  12.8 us (15%)
  local copies, waits for them, and re-layouts  2.63 us (3%)
    pallas_call x1, Pallas kernels, powers(): pl.pallas_call(powers_kernel, out_shape=jax.ShapeDtypeStruct((peers, 1, 1...  28.8 us
    all_to_all x1, blocking collectives, shards(): parts = lax.all_to_all(moments, axes, 0, 0, tiled=True)  17.7 us
    ppermute x3, waiting for transfers between devices, swap(): second = lax.ppermute(second, axis, other)  15.7 us
    ppermute x3, starting transfers between devices, swap(): first = lax.ppermute(first, axis, [(i, i ^ 1) for i in range(peers)])  7.44 us
    ppermute x3, starting transfers between devices, swap(): second = lax.ppermute(second, axis, other)  5.33 us
    pallas_call x1, Pallas kernels, finish(): pl.pallas_call(lambda *refs: finish_kernel(ncells, *refs), grid=(steps,),...  3.92 us
    unnamed x4, local copies, waits for them, and re-layouts  2.63 us
    ppermute x3, waiting for transfers between devices, swap(): first = lax.ppermute(first, axis, [(i, i ^ 1) for i in range(peers)])  2.49 us
  transfers between devices with their start and end apart: 6, of which 6 were waited for; matrix products, arithmetic and copies ran while one was open for 0% of the time, Pallas kernels for 0%

profile of v1, /device:TPU:1, one launch (start us, length us, event | category | flops | bytes accessed | tf_op | source)
XLA Modules:
  0.0 87.8 jit_solution(2154083641608421325)
XLA Ops:
  0.6 0.0 copy-start
  0.6 1.6 %copy-done = f32[4,16,64,128]{3,2,1,0:T(8,128)S(1)} copy-done((f32[4,16,64,128]{3,2,1,0:T(8,128)S(1)}, f32[4,16,64,128]{3,2,1,0:T(8,128)}, u32[]{:S(2)}) %copy-start) | copy-done | bytes 2097176
  2.2 0.0 copy-start.1
  2.2 1.0 %copy-done.1 = f32[16,64,128]{2,1,0:T(8,128)S(1)} copy-done((f32[16,64,128]{2,1,0:T(8,128)S(1)}, f32[16,64,128]{2,1,0:T(8,128)}, u32[]{:S(2)}) %copy-start.1) | copy-done | bytes 524312
  3.3 2.0 %pack_x.1 = (f32[16,64,128]{2,1,0:T(8,128)S(1)}, f32[4,64,128]{2,1,0:T(8,128)S(1)}, f32[4,64,128]{2,1,0:T(8,128)S(1)}) custom-call(f32[4,16,64,128]{3,2,1,0:T(8,128)S(1)} %copy-done, f32[16,64,128]{2,1,0:T(8,128)S(1)} %copy-done.1), custom_call_target="tpu_custom_call" | custom-call | tf_op jit(solution)/shard_map/pack_x/pallas_call | solution.py:82
  5.3 2.1 %collective-permute-start = (f32[4,64,128]{2,1,0:T(8,128)S(1)}, f32[4,64,128]{2,1,0:T(8,128)S(1)}, u32[]{:S(2)}, u32[]{:S(2)}) collective-permute-start(f32[4,64,128]{2,1,0:T(8,128)S(1)} %get-tuple-element.12), channel_id=1, source_target_pairs={{0,32},{32,0},{64,96},{96,64},{1,33},{33,1},{65,97},{97,65},{2,34}... | collective-permute-start | bytes 393224 | tf_op jit(solution)/shard_map/ppermute | solution.py:50
  7.4 1.8 %collective-permute-start.1 = (f32[4,64,128]{2,1,0:T(8,128)S(1)}, f32[4,64,128]{2,1,0:T(8,128)S(1)}, u32[]{:S(2)}, u32[]{:S(2)}) collective-permute-start(f32[4,64,128]{2,1,0:T(8,128)S(1)} %get-tuple-element.13), channel_id=1, source_target_pairs={{0,96},{32,64},{64,32},{96,0},{1,97},{33,65},{65,33},{97,1},{2,98}... | collective-permute-start | bytes 393224 | tf_op jit(solution)/shard_map/ppermute | solution.py:49
  9.2 0.9 %collective-permute-done.first = f32[4,64,128]{2,1,0:T(8,128)S(1)} collective-permute-done((f32[4,64,128]{2,1,0:T(8,128)S(1)}, f32[4,64,128]{2,1,0:T(8,128)S(1)}, u32[]{:S(2)}, u32[]{:S(2)}) %collective-permute-start) | collective-permute-done | bytes 131104 | tf_op jit(solution)/shard_map/ppermute | solution.py:50
  10.1 2.3 %collective-permute-done.1.second = f32[4,64,128]{2,1,0:T(8,128)S(1)} collective-permute-done((f32[4,64,128]{2,1,0:T(8,128)S(1)}, f32[4,64,128]{2,1,0:T(8,128)S(1)}, u32[]{:S(2)}, u32[]{:S(2)}) %collective-permute-start.1) | collective-permute-done | bytes 131104 | tf_op jit(solution)/shard_map/ppermute | solution.py:49
  12.4 0.7 pack_y.1
  13.2 1.7 %collective-permute-start.2 = (f32[6,8,8,128]{3,2,1,0:T(8,128)S(1)}, f32[6,8,8,128]{3,2,1,0:T(8,128)S(1)}, u32[]{:S(2)}, u32[]{:S(2)}) collective-permute-start(f32[6,8,8,128]{3,2,1,0:T(8,128)S(1)} %get-tuple-element.15), channel_id=1, source_target_pairs={{0,8},{8,0},{16,24},{24,16},{1,9},{9,1},{17,25},{25,17},{2,10},{10... | collective-permute-start | bytes 589832 | tf_op jit(solution)/shard_map/ppermute | solution.py:50
  14.9 2.2 %collective-permute-start.3 = (f32[6,8,8,128]{3,2,1,0:T(8,128)S(1)}, f32[6,8,8,128]{3,2,1,0:T(8,128)S(1)}, u32[]{:S(2)}, u32[]{:S(2)}) collective-permute-start(f32[6,8,8,128]{3,2,1,0:T(8,128)S(1)} %get-tuple-element.16), channel_id=1, source_target_pairs={{0,24},{8,16},{16,8},{24,0},{1,25},{9,17},{17,9},{25,1},{2,26},{10... | collective-permute-start | bytes 589832 | tf_op jit(solution)/shard_map/ppermute | solution.py:49
  17.1 0.8 collective-permute-done.2.first
  17.9 2.7 %collective-permute-done.3.second = f32[6,8,8,128]{3,2,1,0:T(8,128)S(1)} collective-permute-done((f32[6,8,8,128]{3,2,1,0:T(8,128)S(1)}, f32[6,8,8,128]{3,2,1,0:T(8,128)S(1)}, u32[]{:S(2)}, u32[]{:S(2)}) %collective-permute-start.3) | collective-permute-done | bytes 196640 | tf_op jit(solution)/shard_map/ppermute | solution.py:49
  20.6 0.4 pack_z.1
  21.1 3.6 %collective-permute-start.4 = (f32[6,4,72,128]{3,2,1,0:T(8,128)S(1)}, f32[6,4,72,128]{3,2,1,0:T(8,128)S(1)}, u32[]{:S(2)}, u32[]{:S(2)}) collective-permute-start(f32[6,4,72,128]{3,2,1,0:T(8,128)S(1)} %get-tuple-element.18), channel_id=1, source_target_pairs={{0,1},{1,0},{2,3},{3,2},{4,5},{5,4},{6,7},{7,6},{8,9},{9,8},{10,11... | collective-permute-start | bytes 2654216 | tf_op jit(solution)/shard_map/ppermute | solution.py:50
  24.7 1.3 %collective-permute-start.5 = (f32[6,4,72,128]{3,2,1,0:T(8,128)S(1)}, f32[6,4,72,128]{3,2,1,0:T(8,128)S(1)}, u32[]{:S(2)}, u32[]{:S(2)}) collective-permute-start(f32[6,4,72,128]{3,2,1,0:T(8,128)S(1)} %get-tuple-element.19), channel_id=1, source_target_pairs={{0,7},{1,2},{2,1},{3,4},{4,3},{5,6},{6,5},{7,0},{8,15},{9,10},{10,... | collective-permute-start | bytes 2654216 | tf_op jit(solution)/shard_map/ppermute | solution.py:49
  25.9 0.8 collective-permute-done.4.first
  26.7 10.7 %collective-permute-done.5.second = f32[6,4,72,128]{3,2,1,0:T(8,128)S(1)} collective-permute-done((f32[6,4,72,128]{3,2,1,0:T(8,128)S(1)}, f32[6,4,72,128]{3,2,1,0:T(8,128)S(1)}, u32[]{:S(2)}, u32[]{:S(2)}) %collective-permute-start.5) | collective-permute-done | bytes 884768 | tf_op jit(solution)/shard_map/ppermute | solution.py:49
  37.4 28.8 %powers.1 = f32[128,1,128]{2,1,0:T(1,128)S(1)} custom-call(f32[4,16,64,128]{3,2,1,0:T(8,128)S(1)} %copy-done, f32[16,64,128]{2,1,0:T(8,128)S(1)} %copy-done.1, f32[16,64,128]{2,1,0:T(8,128)S(1)} %get-tuple-element.14.s_low.s_high.strip, f32[6,16,8,128]{3,2,1,0:T(8,128)S(1)} %get-tuple-element.17.rim, f32[6,4,72,128]{3,2,1,0:T(8,128)S(1)} %collective-permute-done.4.first, ...), custom_call_target="tpu_custom_call" | custom-call | tf_op jit(solution)/shard_map/powers/pallas_call | solution.py:396
  66.2 17.7 %all_to_all.5.refs_0_ = f32[128,1,128]{2,1,0:T(1,128)S(1)} all-to-all(f32[128,1,128]{2,1,0:T(1,128)S(1)} %powers.1), channel_id=1, replica_groups=mesh['gx'=4,'gy'=4,'gz'=8] {'gx','gy','gz'}, dimensions={0} | all-to-all | bytes 131072 | tf_op jit(solution)/shard_map/all_to_all | solution.py:498
  83.9 3.9 %finish.1 = (f32[4,16,64,128]{3,2,1,0:T(8,128)}, f32[20,20]{1,0:T(8,128)}) custom-call(f32[128,1,128]{2,1,0:T(1,128)S(1)} %all_to_all.5.refs_0_, f32[4,16,64,128]{3,2,1,0:T(8,128)S(1)} %copy-done), custom_call_target="tpu_custom_call" | custom-call | tf_op jit(solution)/shard_map/finish/pallas_call | solution.py:472
Async XLA Ops:
  0.6 1.6 %copy-start = (f32[4,16,64,128]{3,2,1,0:T(8,128)S(1)}, f32[4,16,64,128]{3,2,1,0:T(8,128)}, u32[]{:S(2)}) copy-start(f32[4,16,64,128]{3,2,1,0:T(8,128)} %refs_1_.1) | copy-start | bytes 6291460
  2.2 1.0 %copy-start.1 = (f32[16,64,128]{2,1,0:T(8,128)S(1)}, f32[16,64,128]{2,1,0:T(8,128)}, u32[]{:S(2)}) copy-start(f32[16,64,128]{2,1,0:T(8,128)} %kappa.3) | copy-start | bytes 1572868
  5.3 4.8 %collective-permute-start = (f32[4,64,128]{2,1,0:T(8,128)S(1)}, f32[4,64,128]{2,1,0:T(8,128)S(1)}, u32[]{:S(2)}, u32[]{:S(2)}) collective-permute-start(f32[4,64,128]{2,1,0:T(8,128)S(1)} %get-tuple-element.12), channel_id=1, source_target_pairs={{0,32},{32,0},{64,96},{96,64},{1,33},{33,1},{65,97},{97,65},{2,34}... | collective-permute-start | bytes 393224 | tf_op jit(solution)/shard_map/ppermute | solution.py:50
  7.4 5.0 %collective-permute-start.1 = (f32[4,64,128]{2,1,0:T(8,128)S(1)}, f32[4,64,128]{2,1,0:T(8,128)S(1)}, u32[]{:S(2)}, u32[]{:S(2)}) collective-permute-start(f32[4,64,128]{2,1,0:T(8,128)S(1)} %get-tuple-element.13), channel_id=1, source_target_pairs={{0,96},{32,64},{64,32},{96,0},{1,97},{33,65},{65,33},{97,1},{2,98}... | collective-permute-start | bytes 393224 | tf_op jit(solution)/shard_map/ppermute | solution.py:49
  13.2 4.8 %collective-permute-start.2 = (f32[6,8,8,128]{3,2,1,0:T(8,128)S(1)}, f32[6,8,8,128]{3,2,1,0:T(8,128)S(1)}, u32[]{:S(2)}, u32[]{:S(2)}) collective-permute-start(f32[6,8,8,128]{3,2,1,0:T(8,128)S(1)} %get-tuple-element.15), channel_id=1, source_target_pairs={{0,8},{8,0},{16,24},{24,16},{1,9},{9,1},{17,25},{25,17},{2,10},{10... | collective-permute-start | bytes 589832 | tf_op jit(solution)/shard_map/ppermute | solution.py:50
  14.9 5.7 %collective-permute-start.3 = (f32[6,8,8,128]{3,2,1,0:T(8,128)S(1)}, f32[6,8,8,128]{3,2,1,0:T(8,128)S(1)}, u32[]{:S(2)}, u32[]{:S(2)}) collective-permute-start(f32[6,8,8,128]{3,2,1,0:T(8,128)S(1)} %get-tuple-element.16), channel_id=1, source_target_pairs={{0,24},{8,16},{16,8},{24,0},{1,25},{9,17},{17,9},{25,1},{2,26},{10... | collective-permute-start | bytes 589832 | tf_op jit(solution)/shard_map/ppermute | solution.py:49
  21.1 5.7 %collective-permute-start.4 = (f32[6,4,72,128]{3,2,1,0:T(8,128)S(1)}, f32[6,4,72,128]{3,2,1,0:T(8,128)S(1)}, u32[]{:S(2)}, u32[]{:S(2)}) collective-permute-start(f32[6,4,72,128]{3,2,1,0:T(8,128)S(1)} %get-tuple-element.18), channel_id=1, source_target_pairs={{0,1},{1,0},{2,3},{3,2},{4,5},{5,4},{6,7},{7,6},{8,9},{9,8},{10,11... | collective-permute-start | bytes 2654216 | tf_op jit(solution)/shard_map/ppermute | solution.py:50
  24.7 12.8 %collective-permute-start.5 = (f32[6,4,72,128]{3,2,1,0:T(8,128)S(1)}, f32[6,4,72,128]{3,2,1,0:T(8,128)S(1)}, u32[]{:S(2)}, u32[]{:S(2)}) collective-permute-start(f32[6,4,72,128]{3,2,1,0:T(8,128)S(1)} %get-tuple-element.19), channel_id=1, source_target_pairs={{0,7},{1,2},{2,1},{3,4},{4,3},{5,6},{6,5},{7,0},{8,15},{9,10},{10,... | collective-permute-start | bytes 2654216 | tf_op jit(solution)/shard_map/ppermute | solution.py:49

commit v2 on v0

v2 whole, which is shorter than its diff:
```python
import jax
import jax.numpy as jnp
from jax import lax
from jax.experimental import pallas as pl
from jax.experimental.pallas import tpu as pltpu
from jax.sharding import PartitionSpec as P

COLS = 4
BASIS = 4
KRYLOV = 20
MOMENTS = 2 * BASIS + 1
PAIRS = [(c, d) for c in range(COLS) for d in range(c, COLS)]
NPAIRS = len(PAIRS)
DEEP = BASIS
ARRAYS = COLS + 1
PITCH = 6 * DEEP
SLABS = 5

basis_shift = 6.0
basis_scale = 3.0

F32 = jnp.float32
VMEM = pl.BlockSpec(memory_space=pltpu.VMEM)
HBM = pl.BlockSpec(memory_space=pltpu.HBM)


def params(mib):
    return pltpu.CompilerParams(vmem_limit_bytes=mib * 1024 * 1024)


def cost(flops):
    return pl.CostEstimate(flops=flops, bytes_accessed=1 << 20, transcendentals=0)


def lanes(rows):
    return lax.broadcasted_iota(jnp.int32, (rows, 128), 1)


def sublanes(rows):
    return lax.broadcasted_iota(jnp.int32, (rows, 128), 0)


def permute_lanes(value, index):
    return jnp.take_along_axis(value, index, axis=1, mode="promise_in_bounds")


def even_first(axis, first, second):
    return jnp.where(lax.axis_index(axis) % 2 == 0, first, second)


def sides(axis, first, second):
    at = lax.axis_index(axis)
    upper = jnp.where(at == lax.axis_size(axis) - 1, 0.0, even_first(axis, first, second))
    lower = jnp.where(at == 0, 0.0, even_first(axis, second, first))
    return upper, lower


def swap(first, second, axis):
    peers = lax.axis_size(axis)
    other = [(i, (i - 1 if i % 2 == 0 else i + 1) % peers) for i in range(peers)]
    second = lax.ppermute(second, axis, other)
    first = lax.ppermute(first, axis, [(i, i ^ 1) for i in range(peers)])
    return first, second


def link(one, other, bounded):
    weight = (one + other) * (0.5 / basis_scale)
    if bounded:
        weight = jnp.where(jnp.minimum(one, other) > 0.0, weight, 0.0)
    return weight


def centre(k, others):
    total = 6.0 * k
    for other in others:
        total = total + other
    return total * (0.5 / basis_scale) - basis_shift / basis_scale


def rows_above(ref, index, t, tiles, value):
    if t == tiles - 1:
        return pltpu.roll(value, 7, 0)
    return ref[index + (slice(8 * t + 1, 8 * t + 9),)]


def rows_below(ref, index, t, value):
    if t == 0:
        return pltpu.roll(value, 1, 0)
    return ref[index + (slice(8 * t - 1, 8 * t + 7),)]


def tile(t):
    return slice(8 * t, 8 * t + 8)


class Sums:
    def __init__(self):
        self.held = {}

    def add(self, at, term):
        self.held[at] = self.held[at] + term if at in self.held else term

    def products(self, k, olds, news):
        for p, (c, d) in enumerate(PAIRS):
            if k == 1:
                self.add(p, olds[c] * olds[d])
            self.add((2 * k - 1) * NPAIRS + p, olds[c] * news[d])
            self.add(2 * k * NPAIRS + p, news[c] * news[d])

    def flush(self, acc):
        for at, total in self.held.items():
            acc[at] += total


def apply(v, above, below, far, near, w):
    new = w[0] * v
    new -= w[1] * pltpu.roll(v, 127, 1)
    new -= w[2] * pltpu.roll(v, 1, 1)
    new -= w[3] * above
    new -= w[4] * below
    new -= w[5] * far
    new -= w[6] * near
    return new


def tile_weights(w, q, wz, far, near, t):
    c0, right, left, above = (w[i, q, tile(t)] for i in range(4))
    below = rows_below(w, (3, q), t, above)
    return c0, right, left, above, below, wz[far, tile(t)], wz[near, tile(t)]


def pack_z_kernel(block, kappa, to_first, to_second, sems):
    nz = kappa.shape[0]
    high = nz - DEEP
    even = lax.axis_index("gz") % 2 == 0
    copies = []
    for i, (out, at) in enumerate(
        ((to_second, jnp.where(even, 0, high)), (to_first, jnp.where(even, high, 0)))
    ):
        copies.append(pltpu.make_async_copy(block.at[:, pl.ds(at, DEEP)], out.at[0:COLS], sems.at[2 * i]))
        copies.append(pltpu.make_async_copy(kappa.at[pl.ds(at, DEEP)], out.at[COLS], sems.at[2 * i + 1]))
    for copy in copies:
        copy.start()
    for copy in copies:
        copy.wait()


def pack_z(block, kappa):
    nz, ny, nx = kappa.shape
    face = jax.ShapeDtypeStruct((ARRAYS, DEEP, ny, nx), F32)
    return pl.pallas_call(
        pack_z_kernel,
        out_shape=[face, face],
        in_specs=[HBM, HBM],
        out_specs=[VMEM] * 2,
        scratch_shapes=[pltpu.SemaphoreType.DMA((4,))],
        compiler_params=params(8),
        name="pack_z",
    )(block, kappa)


def inner_kernel(block, kappa, acc, edge, p1, p2, p3, w, wz):
    nz, ny, _ = kappa.shape
    tiles = ny // 8
    half = sublanes(8) < 4
    acc[...] = jnp.zeros_like(acc)

    def weights(z, carry):
        for t in range(tiles):
            k = kappa[z, tile(t)]
            right, left = pltpu.roll(k, 127, 1), pltpu.roll(k, 1, 1)
            above = rows_above(kappa, (z,), t, tiles, k)
            below = rows_below(kappa, (z,), t, k)
            far = kappa[z + 1, tile(t)]
            near = kappa[jnp.maximum(z - 1, 0), tile(t)]
            w[0, z, tile(t)] = centre(k, (right, left, above, below, far, near))
            w[1, z, tile(t)] = link(k, right, False)
            w[2, z, tile(t)] = link(k, left, False)
            w[3, z, tile(t)] = link(k, above, False)
            wz[z, tile(t)] = link(k, far, False)
        return carry

    lax.fori_loop(0, nz - 1, weights, 0, unroll=3)
    fields = (block, p1, p2, p3, None)
    for k in range(1, BASIS + 1):
        src, dst = fields[k - 1], fields[k]

        def slab(z, carry, k=k, src=src, dst=dst):
            sums = Sums()

            def step(t):
                ws = tile_weights(w, z, wz, z, z - 1, t)
                olds, news = [], []
                for c in range(COLS):
                    v = src[c, z, tile(t)]
                    above = rows_above(src, (c, z), t, tiles, v)
                    below = rows_below(src, (c, z), t, v)
                    news.append(apply(v, above, below, src[c, z + 1, tile(t)], src[c, z - 1, tile(t)], ws))
                    olds.append(v)
                if dst is not None:
                    for c in range(COLS):
                        dst[c, z, tile(t)] = news[c]
                return olds, news

            first, last = step(0), step(tiles - 1)
            olds, news = (
                [jnp.where(half, b, a) for a, b in zip(first[i], last[i])] for i in range(2)
            )
            sums.products(k, olds, news)
            for t in range(1, tiles - 1):
                sums.products(k, *step(t))
            sums.flush(acc)
            return carry

        lax.fori_loop(k, nz - k, slab, 0, unroll=2)
        if dst is not None:
            for i in range(2):
                edge[k - 1, 0, i] = dst[:, k + i]
                edge[k - 1, 1, i] = dst[:, nz - 1 - k - i]


def inner(block, kappa):
    nz, ny, nx = kappa.shape
    return pl.pallas_call(
        inner_kernel,
        out_shape=[
            jax.ShapeDtypeStruct((MOMENTS * NPAIRS, 8, nx), F32),
            jax.ShapeDtypeStruct((BASIS - 1, 2, 2, COLS, ny, nx), F32),
        ],
        in_specs=[VMEM] * 2,
        out_specs=[VMEM] * 2,
        scratch_shapes=[pltpu.VMEM(block.shape, F32)] * 3
        + [pltpu.VMEM((4, nz, ny, nx), F32), pltpu.VMEM((nz, ny, nx), F32)],
        compiler_params=params(24),
        cost_estimate=cost(1 << 28),
        name="inner",
    )(block, kappa)


def pack_y_kernel(
    b_low, b_high, k_low, k_high, f_low, f_high, s_low, s_high, after, edges, to_first, to_second
):
    nz = k_low.shape[0]

    def own(z, carry):
        for a in range(ARRAYS):
            edges[a, z + DEEP, 0] = b_low[a, z] if a < COLS else k_low[z]
            edges[a, z + DEEP, 1] = b_high[a, z] if a < COLS else k_high[z]
        return carry

    lax.fori_loop(0, nz, own, 0, unroll=4)

    def far(i, carry):
        for a in range(ARRAYS):
            for at, (one, other) in enumerate(((f_low, s_low), (f_high, s_high))):
                upper, lower = sides("gz", one[a, i], other[a, i])
                edges[a, i, at] = lower
                edges[a, nz + DEEP + i, at] = upper
        return carry

    lax.fori_loop(0, DEEP, far, 0, unroll=2)
    half = sublanes(8) < 4

    def pairs(duo, carry):
        z = duo * 2
        for a in range(ARRAYS):
            upper = jnp.where(half, pltpu.roll(edges[a, z, 1], 4, 0), edges[a, z + 1, 1])
            lower = jnp.where(half, edges[a, z, 0], pltpu.roll(edges[a, z + 1, 0], 4, 0))
            to_first[a, duo] = even_first("gy", upper, lower)
            to_second[a, duo] = even_first("gy", lower, upper)
        return carry

    lax.fori_loop(0, to_first.shape[1], pairs, 0, unroll=4)


def pack_y(block, kappa, first, second, after):
    nz, ny, nx = kappa.shape
    depth = nz + 2 * DEEP
    last = ny // 8 - 1
    whole = lambda shape: pl.BlockSpec(shape, lambda i: (0,) * len(shape))
    b_edge = lambda at: pl.BlockSpec((COLS, nz, 8, nx), lambda i: (0, 0, at, 0))
    k_edge = lambda at: pl.BlockSpec((nz, 8, nx), lambda i: (0, at, 0))
    f_edge = lambda at: pl.BlockSpec((ARRAYS, DEEP, 8, nx), lambda i: (0, 0, at, 0))
    edges = (ARRAYS, depth, 2, 8, nx)
    face = (ARRAYS, depth // 2, 8, nx)
    return pl.pallas_call(
        pack_y_kernel,
        grid=(1,),
        out_shape=[jax.ShapeDtypeStruct(s, F32) for s in (edges, face, face)],
        in_specs=[f(at) for f in (b_edge, k_edge, f_edge, f_edge) for at in (0, last)]
        + [pl.BlockSpec(memory_space=pl.ANY)],
        out_specs=[whole(edges), whole(face), whole(face)],
        compiler_params=params(16),
        name="pack_y",
    )(block, block, kappa, kappa, first, first, second, second, after)


def outer_kernel(block, kappa, edge, first, second, acc, f0, f1, f2, f3, kz, w, wz):
    nz, ny, _ = kappa.shape
    tiles = ny // 8
    half = sublanes(8) < 4
    acc[...] = jnp.zeros_like(acc)

    def far(i, carry):
        for a in range(ARRAYS):
            upper, lower = sides("gz", first[a, i], second[a, i])
            if a < COLS:
                f0[0, a, i] = lower
                f0[1, a, DEEP - 1 - i] = upper
            else:
                kz[0, i] = lower
                kz[1, DEEP - 1 - i] = upper
        return carry

    lax.fori_loop(0, DEEP, far, 0)
    for i in range(2):
        for c in range(COLS):
            f0[0, c, DEEP + i] = block[c, i]
            f0[1, c, DEEP + i] = block[c, nz - 1 - i]
            for k, f in enumerate((f1, f2, f3)):
                for side in range(2):
                    f[side, c, DEEP + i] = edge[k, side, i, c]
    for i in range(DEEP + 1):
        kz[0, DEEP + i] = kappa[i]
        kz[1, DEEP + i] = kappa[nz - 1 - i]

    def weights(at, carry):
        side, e = at // 8, at % 8
        for t in range(tiles):
            k = kz[side, e, tile(t)]
            right, left = pltpu.roll(k, 127, 1), pltpu.roll(k, 1, 1)
            above = rows_above(kz, (side, e), t, tiles, k)
            below = rows_below(kz, (side, e), t, k)
            far = kz[side, e + 1, tile(t)]
            near = kz[side, jnp.maximum(e - 1, 0), tile(t)]
            w[0, at, tile(t)] = centre(k, (right, left, above, below, far, near))
            w[1, at, tile(t)] = link(k, right, False)
            w[2, at, tile(t)] = link(k, left, False)
            w[3, at, tile(t)] = link(k, above, False)
            wz[at, tile(t)] = link(k, far, True)
        return carry

    lax.fori_loop(0, 16, weights, 0, unroll=2)
    fields = (f0, f1, f2, f3, None)
    for k in range(1, BASIS + 1):
        src, dst = fields[k - 1], fields[k]

        def both(side, carry, k=k, src=src, dst=dst):
            for j in range(DEEP):
                own = j >= DEEP - k
                sums = Sums()

                def step(t):
                    at = side * 8 + j + k
                    ws = tile_weights(w, at, wz, at, at - 1, t)
                    olds, news = [], []
                    for c in range(COLS):
                        v = src[side, c, j + 1, tile(t)]
                        above = rows_above(src, (side, c, j + 1), t, tiles, v)
                        below = rows_below(src, (side, c, j + 1), t, v)
                        far, near = src[side, c, j + 2, tile(t)], src[side, c, j, tile(t)]
                        news.append(apply(v, above, below, far, near, ws))
                        olds.append(v)
                    if dst is not None:
                        for c in range(COLS):
                            dst[side, c, j, tile(t)] = news[c]
                    return olds, news

                first, last = step(0), step(tiles - 1)
                if own:
                    olds, news = (
                        [jnp.where(half, b, a) for a, b in zip(first[i], last[i])] for i in range(2)
                    )
                    sums.products(k, olds, news)
                for t in range(1, tiles - 1):
                    pair = step(t)
                    if own:
                        sums.products(k, *pair)
                sums.flush(acc)
            return carry

        lax.fori_loop(0, 2, both, 0)


def outer(block, kappa, edge, first, second):
    nz, ny, nx = kappa.shape
    return pl.pallas_call(
        outer_kernel,
        out_shape=jax.ShapeDtypeStruct((MOMENTS * NPAIRS, 8, nx), F32),
        in_specs=[VMEM] * 5,
        out_specs=VMEM,
        scratch_shapes=[pltpu.VMEM((2, COLS, DEEP + 2, ny, nx), F32)] * 4
        + [
            pltpu.VMEM((2, 2 * DEEP + 1, ny, nx), F32),
            pltpu.VMEM((4, 16, ny, nx), F32),
            pltpu.VMEM((16, ny, nx), F32),
        ],
        compiler_params=params(24),
        cost_estimate=cost(1 << 27),
        name="outer",
    )(block, kappa, edge, first, second)


def strip_of(planes):
    lane = lanes(8)
    offset, group = lane % PITCH, lane // PITCH
    index = jnp.where(offset < 8, 120 + offset, jnp.maximum(offset - 16, 0))
    strip = jnp.zeros((8, 128), F32)
    for g, plane in enumerate(planes):
        strip = jnp.where(group == g, permute_lanes(plane, index), strip)
    return strip


def strips_kernel(block, kappa, first, second, strip):
    nz, ny, _ = kappa.shape

    def rows(t, carry):
        at = pl.ds(pl.multiple_of(t * 8, 8), 8)
        for a in range(ARRAYS):
            ends = [sides("gz", first[a, i, at], second[a, i, at]) for i in range(DEEP)]

            def plane(z):
                if z < DEEP:
                    return ends[z][1]
                if z >= nz + DEEP:
                    return ends[z - nz - DEEP][0]
                return block[a, z - DEEP, at] if a < COLS else kappa[z - DEEP, at]

            for q in range(SLABS):
                strip[a, q, at] = strip_of([plane(z) for z in range(q, nz + 2 * DEEP, SLABS)])
        return carry

    lax.fori_loop(0, ny // 8, rows, 0)


def strips(block, kappa, first, second):
    nz, ny, nx = kappa.shape
    return pl.pallas_call(
        strips_kernel,
        out_shape=jax.ShapeDtypeStruct((ARRAYS, SLABS, ny, nx), F32),
        in_specs=[VMEM] * 4,
        out_specs=VMEM,
        compiler_params=params(16),
        cost_estimate=cost(1 << 25),
        name="strips",
    )(block, kappa, first, second)


def pack_x_kernel(first, second, strip, after, rim, side, to_first, to_second):
    half = sublanes(8) < 4
    depth, tiles = rim.shape[1], to_first.shape[1] // 8

    def duos(duo, carry):
        for a in range(ARRAYS):
            upper, lower = sides("gy", first[a, duo], second[a, duo])
            rim[a, duo * 2] = jnp.where(half, upper, pltpu.roll(lower, 4, 0))
            rim[a, duo * 2 + 1] = jnp.where(half, pltpu.roll(upper, 4, 0), lower)
        return carry

    lax.fori_loop(0, depth // 2, duos, 0, unroll=4)
    slot = lanes(8) % PITCH // DEEP

    def arrays(a, carry):
        for q in range(SLABS):
            side[a, q] = strip_of([rim[a, z] for z in range(q, depth, SLABS)])
        for t in range(tiles):
            upper = jnp.zeros((8, 128), F32)
            lower = jnp.zeros((8, 128), F32)
            for q in range(SLABS):
                value = strip[a, q, tile(t)] if t < tiles - 1 else side[a, q]
                upper = jnp.where(slot == q, pltpu.roll(value, (4 * q - 4) % 128, 1), upper)
                lower = jnp.where(slot == q, pltpu.roll(value, (4 * q - 16) % 128, 1), lower)
            to_first[a, tile(t)] = even_first("gx", upper, lower)
            to_second[a, tile(t)] = even_first("gx", lower, upper)
        return carry

    lax.fori_loop(0, ARRAYS, arrays, 0)


def pack_x(first, second, strip, after):
    _, _, ny, nx = strip.shape
    depth = first.shape[1] * 2
    face = (ARRAYS, ny + 8, nx)
    return pl.pallas_call(
        pack_x_kernel,
        out_shape=[
            jax.ShapeDtypeStruct(s, F32)
            for s in ((ARRAYS, depth, 8, nx), (ARRAYS, SLABS, 8, nx), face, face)
        ],
        in_specs=[VMEM] * 3 + [pl.BlockSpec(memory_space=pl.ANY)],
        out_specs=[VMEM] * 4,
        compiler_params=params(16),
        name="pack_x",
    )(first, second, strip, after)


def y_strip_kernel(edges, rim, acc, g0, g1, g2, g3, kr, w, wz):
    depth = rim.shape[1]
    half = sublanes(8) < 4
    acc[...] = jnp.zeros_like(acc)

    def fill(z, carry):
        for a in range(ARRAYS):
            parts = (edges[a, z, 1], rim[a, z], edges[a, z, 0])
            for t, part in enumerate(parts):
                if a < COLS:
                    g0[a, z, tile(t)] = part
                else:
                    kr[z, tile(t)] = part
        return carry

    lax.fori_loop(0, depth, fill, 0, unroll=4)

    def weights(z, carry):
        for t in range(3):
            k = kr[z, tile(t)]
            right, left = pltpu.roll(k, 127, 1), pltpu.roll(k, 1, 1)
            above = rows_above(kr, (z,), t, 3, k)
            below = rows_below(kr, (z,), t, k)
            far = kr[z + 1, tile(t)]
            near = kr[jnp.maximum(z - 1, 0), tile(t)]
            w[0, z, tile(t)] = centre(k, (right, left, above, below, far, near))
            w[1, z, tile(t)] = link(k, right, False)
            w[2, z, tile(t)] = link(k, left, False)
            w[3, z, tile(t)] = link(k, above, True)
            wz[z, tile(t)] = link(k, far, True)
        return carry

    lax.fori_loop(0, depth - 1, weights, 0, unroll=4)
    fields = (g0, g1, g2, g3, None)
    for k in range(1, BASIS + 1):
        src, dst = fields[k - 1], fields[k]

        def slab(z, own, k=k, src=src, dst=dst):
            sums = Sums()
            kept = []
            for t in range(3):
                if dst is None and t == 1:
                    continue
                ws = tile_weights(w, z, wz, z, z - 1, t)
                olds, news = [], []
                for c in range(COLS):
                    v = src[c, z, tile(t)]
                    above = rows_above(src, (c, z), t, 3, v)
                    below = rows_below(src, (c, z), t, v)
                    news.append(apply(v, above, below, src[c, z + 1, tile(t)], src[c, z - 1, tile(t)], ws))
                    olds.append(v)
                if dst is not None:
                    for c in range(COLS):
                        dst[c, z, tile(t)] = news[c]
                if t != 1:
                    kept.append((olds, news))
            if own:
                olds, news = (
                    [jnp.where(half, b, a) for a, b in zip(kept[0][i], kept[1][i])] for i in range(2)
                )
                sums.products(k, olds, news)
                sums.flush(acc)

        def far(i, carry, k=k, slab=slab):
            slab(k + i, False)
            slab(depth - DEEP + i, False)
            return carry

        def own(z, carry, slab=slab):
            slab(z, True)
            return carry

        if k < DEEP:
            lax.fori_loop(0, DEEP - k, far, 0)
        lax.fori_loop(DEEP, depth - DEEP, own, 0, unroll=4)


def y_strip(edges, rim):
    _, depth, _, nx = rim.shape
    return pl.pallas_call(
        y_strip_kernel,
        out_shape=jax.ShapeDtypeStruct((MOMENTS * NPAIRS, 8, nx), F32),
        in_specs=[VMEM] * 2,
        out_specs=VMEM,
        scratch_shapes=[pltpu.VMEM((COLS, depth, 24, nx), F32)] * 4
        + [
            pltpu.VMEM((depth, 24, nx), F32),
            pltpu.VMEM((4, depth, 24, nx), F32),
            pltpu.VMEM((depth, 24, nx), F32),
        ],
        compiler_params=params(16),
        cost_estimate=cost(1 << 27),
        name="y_strip",
    )(edges, rim)


def x_strip_kernel(strip, side, first, second, acc1, acc2, acc3, out, s0, s1, s2, s3, kr, w, wz, acc):
    tiles = first.shape[1] // 8
    offset = lanes(8) % PITCH

    def rows(t):
        return slice(8 + 8 * t, 16 + 8 * t)

    def lay(ref, index, t, value):
        ref[index + (rows(t),)] = value
        if t == 0:
            ref[index + (slice(8 + 8 * tiles, 16 + 8 * tiles),)] = value
        if t == tiles - 1:
            ref[index + (slice(0, 8),)] = value

    def next_slab(ref, index, q, at):
        if q < SLABS - 1:
            return ref[index + (q + 1, at)]
        return pltpu.roll(ref[index + (0, at)], 128 - PITCH, 1)

    def last_slab(ref, index, q, at):
        if q > 0:
            return ref[index + (q - 1, at)]
        return pltpu.roll(ref[index + (SLABS - 1, at)], PITCH, 1)

    def fill(a, put):
        for t in range(tiles):
            upper, lower = sides("gx", first[a, tile(t)], second[a, tile(t)])
            for q in range(SLABS):
                value = strip[a, q, tile(t)] if t < tiles - 1 else side[a, q]
                value = jnp.where(offset // 4 == 2, pltpu.roll(upper, (8 - 4 * q) % 128, 1), value)
                value = jnp.where(offset // 4 == 3, pltpu.roll(lower, (12 - 4 * q) % 128, 1), value)
                put(q, t, value)

    fill(COLS, lambda q, t, value: lay(kr, (q,), t, value))

    def fill_column(c, carry):
        fill(c, lambda q, t, value: lay(s0, (c, q), t, value))
        return carry

    lax.fori_loop(0, COLS, fill_column, 0)

    for q in range(SLABS):
        for t in range(tiles):
            k = kr[q, rows(t)]
            right, left = pltpu.roll(k, 127, 1), pltpu.roll(k, 1, 1)
            above = kr[q, 9 + 8 * t : 17 + 8 * t]
            below = kr[q, 7 + 8 * t : 15 + 8 * t]
            far, near = next_slab(kr, (), q, rows(t)), last_slab(kr, (), q, rows(t))
            w[0, q, rows(t)] = centre(k, (right, left, above, below, far, near))
            w[1, q, rows(t)] = link(k, right, True)
            w[2, q, rows(t)] = link(k, left, True)
            above = link(k, above, True)
            w[3, q, rows(t)] = above
            if t == tiles - 1:
                w[3, q, 0:8] = above
            wz[q + 1, rows(t)] = link(k, far, True)
            if q == 0:
                wz[0, rows(t)] = link(k, near, True)
    acc[...] = jnp.zeros_like(acc)
    fields = (s0, s1, s2, s3, None)
    for k in range(1, BASIS + 1):
        src, dst = fields[k - 1], fields[k]

        def slab(q):
            sums = Sums()
            for t in range(tiles if dst is not None else tiles - 1):
                at, above, below = rows(t), slice(9 + 8 * t, 17 + 8 * t), slice(7 + 8 * t, 15 + 8 * t)
                ws = [w[i, q, at] for i in range(4)] + [w[3, q, below], wz[q + 1, at], wz[q, at]]
                olds, news = [], []
                for c in range(COLS):
                    v = src[c, q, at]
                    far, near = next_slab(src, (c,), q, at), last_slab(src, (c,), q, at)
                    news.append(apply(v, src[c, q, above], src[c, q, below], far, near, ws))
                    olds.append(v)
                if dst is not None:
                    for c in range(COLS):
                        lay(dst, (c, q), t, news[c])
                if t < tiles - 1:
                    sums.products(k, olds, news)
            sums.flush(acc.at[0 if q < SLABS - 1 else 1])

        for q in range(SLABS):
            slab(q)

    lane1 = lax.broadcasted_iota(jnp.int32, (1, 128), 1)
    group, place = lane1 // PITCH, lane1 % PITCH // DEEP
    here = (place == 1) | (place == 4)
    total = jnp.zeros((acc.shape[1], 128), F32)
    for kept, sums in (
        ((lane1 >= DEEP) & (lane1 < 128 - DEEP), acc1[...] + acc2[...] + acc3[...]),
        (here & (group >= 1) & (group <= 3), acc[0]),
        (here & (group <= 3), acc[1]),
    ):
        total = total + jnp.where(kept, jnp.sum(sums, axis=1), 0.0)
    total = jnp.concatenate([total, jnp.zeros((128 - total.shape[0], 128), F32)], 0)
    row = lax.dot_general(
        jnp.ones((8, 128), F32),
        total,
        (((1,), (1,)), ((), ())),
        precision=lax.Precision.HIGHEST,
        preferred_element_type=F32,
    )
    out[...] = jnp.broadcast_to(row[0:1][None], out.shape)


def x_strip(strip, side, first, second, accs, peers):
    cols, slabs, ny, nx = strip.shape
    laid = (slabs, ny + 24, nx)
    return pl.pallas_call(
        x_strip_kernel,
        out_shape=jax.ShapeDtypeStruct((peers, 1, 128), F32),
        in_specs=[VMEM] * 7,
        out_specs=VMEM,
        scratch_shapes=[pltpu.VMEM((COLS,) + laid, F32)] * 4
        + [
            pltpu.VMEM(laid, F32),
            pltpu.VMEM((4,) + laid, F32),
            pltpu.VMEM((slabs + 1,) + laid[1:], F32),
            pltpu.VMEM((2, MOMENTS * NPAIRS, 8, nx), F32),
        ],
        compiler_params=params(16),
        name="x_strip",
    )(strip, side, first, second, *accs)


def finish_kernel(ncells, parts, block, ortho, triangle, coef):
    @pl.when(pl.program_id(0) == 0)
    def _():
        row = jnp.sum(parts[...], axis=0) * (1.0 / ncells)
        row = jnp.broadcast_to(row, (24, 128))
        a, b = sublanes(24), lanes(24)
        c, d = a % 4, b % 4
        low, high = jnp.minimum(c, d), jnp.maximum(c, d)
        pair = low * 4 - (low * (low - 1)) // 2 + high - low
        inside = (a < KRYLOV) & (b < KRYLOV)
        index = jnp.where(inside, (a // 4 + b // 4) * NPAIRS + pair, 127)
        matrix = permute_lanes(row, index)
        lane = lanes(1)
        uppers = []
        for k in range(KRYLOV):
            line = matrix[k : k + 1, :]
            pivot = line[:, k : k + 1]
            upper = jnp.where(lane >= k, line / jnp.sqrt(pivot), 0.0)
            uppers.append(upper)
            triangle[k : k + 1, :] = upper[:, 0:KRYLOV]
            if k + 1 < KRYLOV:
                matrix = matrix - matrix[:, k : k + 1] * (line / pivot)
        at = 0
        for i in range(COLS):
            for j in range(i, COLS):
                value = uppers[i][:, j : j + 1]
                value = 1.0 / value if i == j else value
                coef[at] = jnp.broadcast_to(value, (8, 128))
                at += 1

    u = {}
    at = 0
    for i in range(COLS):
        for j in range(i, COLS):
            u[i, j] = coef[at]
            at += 1

    def slab(z, carry):
        for t in range(ortho.shape[2] // 8):
            rows = slice(8 * t, 8 * t + 8)
            done = []
            for j in range(COLS):
                value = block[j, z, rows]
                for i in range(j):
                    value = value - u[i, j] * done[i]
                value = value * u[j, j]
                ortho[j, z, rows] = value
                done.append(value)
        return carry

    lax.fori_loop(0, ortho.shape[1], slab, 0)


def finish(parts, block, ncells):
    cols, nz, ny, nx = block.shape
    steps = 4
    piece = pl.BlockSpec((cols, nz // steps, ny, nx), lambda i: (0, i, 0, 0))
    return pl.pallas_call(
        lambda *refs: finish_kernel(ncells, *refs),
        grid=(steps,),
        out_shape=[
            jax.ShapeDtypeStruct(block.shape, F32),
            jax.ShapeDtypeStruct((KRYLOV, KRYLOV), F32),
        ],
        in_specs=[pl.BlockSpec(parts.shape, lambda i: (0, 0, 0)), piece],
        out_specs=[piece, pl.BlockSpec((KRYLOV, KRYLOV), lambda i: (0, 0))],
        scratch_shapes=[pltpu.VMEM((NPAIRS, 8, 128), F32)],
        compiler_params=params(16),
        name="finish",
    )(parts, block)


def shards(block, kappa):
    axes = ("gx", "gy", "gz")
    peers = lax.axis_size(axes)
    ncells = float(kappa.size * peers)
    first, second = swap(*pack_z(block, kappa), "gz")
    acc1, edge = inner(block, kappa)
    edges, y_first, y_second = pack_y(block, kappa, first, second, acc1)
    y_first, y_second = swap(y_first, y_second, "gy")
    strip = strips(block, kappa, first, second)
    acc2 = outer(block, kappa, edge, first, second)
    rim, side, x_first, x_second = pack_x(y_first, y_second, strip, acc2)
    x_first, x_second = swap(x_first, x_second, "gx")
    acc3 = y_strip(edges, rim)
    moments = x_strip(strip, side, x_first, x_second, (acc1, acc2, acc3), peers)
    parts = lax.all_to_all(moments, axes, 0, 0, tiled=True)
    return tuple(finish(parts, block, ncells))


def solution(mesh):
    return jax.shard_map(
        shards,
        mesh=mesh,
        in_specs=(P(None, "gz", "gy", "gx"), P("gz", "gy", "gx")),
        out_specs=(P(None, "gz", "gy", "gx"), P()),
        check_vma=False,
    )
```

time: 440 us -> 62.4 us (0.14); the launches traced: 433 us -> 62.2 us
  local copies, waits for them, and re-layouts: 118 us -> 2.63 us
  other arithmetic: 108 us -> 0 us
  starting transfers between devices: 77 us -> 10 us
  blocking collectives: 70 us -> 19 us
  Pallas kernels: 0 us -> 27.6 us
  matrix products: 22 us -> 0 us
  waiting for transfers between devices: 21.2 us -> 2.19 us
  between operations: 16.3 us -> 0.74 us
    div x7 -> x0, other arithmetic: 78.2 us -> none  [the longest x4 71.3 us: shards(): (stencil_inner(current_pad, kpad) - basis_shift * centre) / basis_scale]
    psum x1 -> x0, blocking collectives: 70 us -> none  [shards(): gram = lax.psum(local_gram, ('gx', 'gy', 'gz'))]
    ppermute x24 -> x6, starting transfers between devices: 77 us -> 10 us  [the longest x3 5.42 us: swap(): second = lax.ppermute(second, axis, other)]
    slice x56 -> x0, local copies, waits for them, and re-layouts: 50.5 us -> none  [the longest x8 20.5 us: extended(): leading = lax.slice_in_dim(value, 0, width, axis=dim)]
    concatenate x1 -> x0, local copies, waits for them, and re-layouts: 31.5 us -> none  [shards(): basis = jnp.concatenate(blocks, 0).reshape(KRYLOV, -1)]
    pallas_call x0 -> x9, Pallas kernels: none -> 27.6 us  [the longest x1 6.75 us: inner(): pl.pallas_call(inner_kernel, out_shape=[jax.ShapeDtypeStruct((MOMENTS * N...]
    dot_general x2 -> x0, matrix products: 22 us -> none  [the longest x1 17.6 us: shards(): local_gram = jnp.dot(basis, basis.T, precision=lax.Precision.HIGHEST)]
    ppermute x10 -> x0, local copies, waits for them, and re-layouts: 19.9 us -> none  [the longest x5 10.3 us: extended(): before = lax.ppermute(last, axis, up)]
  transfers between devices with their start and end apart: 24 -> 6, of which waited for: 13 -> 1; matrix products, arithmetic and copies ran while one was open for 4% -> 0% of each run, Pallas kernels for 0% -> 29%
where the time goes in v2:
time: 62.4 us; the launch traced here: 62.2 us
  Pallas kernels  27.6 us (44%)
  blocking collectives  19 us (30%)
  starting transfers between devices  10 us (16%)
  local copies, waits for them, and re-layouts  2.63 us (4%)
  waiting for transfers between devices  2.19 us (4%)
  between operations  0.74 us (1%)
    all_to_all x1, blocking collectives, shards(): parts = lax.all_to_all(moments, axes, 0, 0, tiled=True)  19 us
    pallas_call x1, Pallas kernels, inner(): pl.pallas_call(inner_kernel, out_shape=[jax.ShapeDtypeStruct((MOMENTS * N...  6.75 us
    ppermute x3, starting transfers between devices, swap(): second = lax.ppermute(second, axis, other)  5.42 us
    pallas_call x1, Pallas kernels, outer(): pl.pallas_call(outer_kernel, out_shape=jax.ShapeDtypeStruct((MOMENTS * NP...  4.88 us
    pallas_call x1, Pallas kernels, y_strip(): pl.pallas_call(y_strip_kernel, out_shape=jax.ShapeDtypeStruct((MOMENTS *...  4.7 us
    ppermute x3, starting transfers between devices, swap(): first = lax.ppermute(first, axis, [(i, i ^ 1) for i in range(peers)])  4.59 us
    pallas_call x1, Pallas kernels, x_strip(): pl.pallas_call(x_strip_kernel, out_shape=jax.ShapeDtypeStruct((peers, 1,...  3.98 us
    pallas_call x1, Pallas kernels, finish(): pl.pallas_call(lambda *refs: finish_kernel(ncells, *refs), grid=(steps,),...  3.92 us
  transfers between devices with their start and end apart: 6, of which 1 were waited for; matrix products, arithmetic and copies ran while one was open for 0% of the time, Pallas kernels for 29%

profile of v2, /device:TPU:1, one launch (start us, length us, event | category | flops | bytes accessed | tf_op | source)
XLA Modules:
  0.0 62.2 jit_solution(9668235680972570795)
XLA Ops:
  0.6 0.0 copy-start
  0.6 1.6 %copy-done = f32[4,16,64,128]{3,2,1,0:T(8,128)S(1)} copy-done((f32[4,16,64,128]{3,2,1,0:T(8,128)S(1)}, f32[4,16,64,128]{3,2,1,0:T(8,128)}, u32[]{:S(2)}) %copy-start) | copy-done | bytes 2097176
  2.2 0.0 copy-start.2
  2.2 1.0 %copy-done.2 = f32[16,64,128]{2,1,0:T(8,128)S(1)} copy-done((f32[16,64,128]{2,1,0:T(8,128)S(1)}, f32[16,64,128]{2,1,0:T(8,128)}, u32[]{:S(2)}) %copy-start.2) | copy-done | bytes 524312
  3.3 0.0 copy-start.1
  3.3 0.0 copy-start.3
  3.3 0.4 pack_z.1
  3.7 1.5 %collective-permute-start = (f32[5,4,64,128]{3,2,1,0:T(8,128)S(1)}, f32[5,4,64,128]{3,2,1,0:T(8,128)S(1)}, u32[]{:S(2)}, u32[]{:S(2)}) collective-permute-start(f32[5,4,64,128]{3,2,1,0:T(8,128)S(1)} %get-tuple-element.13), channel_id=1, source_target_pairs={{0,1},{1,0},{2,3},{3,2},{4,5},{5,4},{6,7},{7,6},{8,9},{9,8},{10,11... | collective-permute-start | bytes 1966088 | tf_op jit(solution)/shard_map/ppermute | solution.py:62
  5.2 1.4 %collective-permute-start.1 = (f32[5,4,64,128]{3,2,1,0:T(8,128)S(1)}, f32[5,4,64,128]{3,2,1,0:T(8,128)S(1)}, u32[]{:S(2)}, u32[]{:S(2)}) collective-permute-start(f32[5,4,64,128]{3,2,1,0:T(8,128)S(1)} %get-tuple-element.14), channel_id=1, source_target_pairs={{0,7},{1,2},{2,1},{3,4},{4,3},{5,6},{6,5},{7,0},{8,15},{9,10},{10,... | collective-permute-start | bytes 1966088 | tf_op jit(solution)/shard_map/ppermute | solution.py:61
  6.6 0.0 copy-done.1
  6.6 0.0 copy-done.3
  6.6 6.7 %inner.1 = (f32[90,8,128]{2,1,0:T(8,128)S(1)}, f32[3,2,2,4,64,128]{5,4,3,2,1,0:T(8,128)S(1)}) custom-call(f32[4,16,64,128]{3,2,1,0:T(8,128)S(1)} %copy-done.1, f32[16,64,128]{2,1,0:T(8,128)S(1)} %copy-done.3), custom_call_target="tpu_custom_call" | custom-call | flops 268435456 | bytes 1048576 | tf_op jit(solution)/shard_map/inner/pallas_call | solution.py:224
  13.3 0.0 collective-permute-done.first.f_low.f_high
  13.4 2.2 %collective-permute-done.1.second.s_low.s_high = f32[5,4,64,128]{3,2,1,0:T(8,128)S(1)} collective-permute-done((f32[5,4,64,128]{3,2,1,0:T(8,128)S(1)}, f32[5,4,64,128]{3,2,1,0:T(8,128)S(1)}, u32[]{:S(2)}, u32[]{:S(2)}) %collective-permute-start.1) | collective-permute-done | bytes 655392 | tf_op jit(solution)/shard_map/ppermute | solution.py:61
  15.5 0.3 pack_y.1
  15.8 1.8 %collective-permute-start.2 = (f32[5,12,8,128]{3,2,1,0:T(8,128)S(1)}, f32[5,12,8,128]{3,2,1,0:T(8,128)S(1)}, u32[]{:S(2)}, u32[]{:S(2)}) collective-permute-start(f32[5,12,8,128]{3,2,1,0:T(8,128)S(1)} %get-tuple-element.16), channel_id=1, source_target_pairs={{0,8},{8,0},{16,24},{24,16},{1,9},{9,1},{17,25},{25,17},{2,10},{10... | collective-permute-start | bytes 737288 | tf_op jit(solution)/shard_map/ppermute | solution.py:62
  17.6 2.2 %collective-permute-start.3 = (f32[5,12,8,128]{3,2,1,0:T(8,128)S(1)}, f32[5,12,8,128]{3,2,1,0:T(8,128)S(1)}, u32[]{:S(2)}, u32[]{:S(2)}) collective-permute-start(f32[5,12,8,128]{3,2,1,0:T(8,128)S(1)} %get-tuple-element.17), channel_id=1, source_target_pairs={{0,24},{8,16},{16,8},{24,0},{1,25},{9,17},{17,9},{25,1},{2,26},{10... | collective-permute-start | bytes 737288 | tf_op jit(solution)/shard_map/ppermute | solution.py:61
  19.8 1.7 %strips.1.strip = f32[5,5,64,128]{3,2,1,0:T(8,128)S(1)} custom-call(f32[4,16,64,128]{3,2,1,0:T(8,128)S(1)} %copy-done.1, f32[16,64,128]{2,1,0:T(8,128)S(1)} %copy-done.3, f32[5,4,64,128]{3,2,1,0:T(8,128)S(1)} %collective-permute-done.first.f_low.f_high, f32[5,4,64,128]{3,2,1,0:T(8,128)S(1)} %collective-permute-done.1.second.s_low.s_high), custom_call_target="tpu_custom_call" | custom-call | flops 33554432 | bytes 1048576 | tf_op jit(solution)/shard_map/strips/pallas_call | solution.py:438
  21.5 4.9 %outer.1.after.acc2 = f32[90,8,128]{2,1,0:T(8,128)S(1)} custom-call(f32[4,16,64,128]{3,2,1,0:T(8,128)S(1)} %copy-done.1, f32[16,64,128]{2,1,0:T(8,128)S(1)} %copy-done.3, f32[3,2,2,4,64,128]{5,4,3,2,1,0:T(8,128)S(1)} %get-tuple-element.18.edge, f32[5,4,64,128]{3,2,1,0:T(8,128)S(1)} %collective-permute-done.first.f_low.f_high, ...), custom_call_target="tpu_custom_call" | custom-call | flops 134217728 | bytes 1048576 | tf_op jit(solution)/shard_map/outer/pallas_call | solution.py:387
  26.4 0.0 collective-permute-done.2.first
  26.4 0.0 collective-permute-done.3.second
  26.4 1.0 %pack_x.1 = (f32[5,24,8,128]{3,2,1,0:T(8,128)S(1)}, f32[5,5,8,128]{3,2,1,0:T(8,128)S(1)}, f32[5,72,128]{2,1,0:T(8,128)S(1)}, f32[5,72,128]{2,1,0:T(8,128)S(1)}) custom-call(f32[5,12,8,128]{3,2,1,0:T(8,128)S(1)} %collective-permute-done.2.first, f32[5,12,8,128]{3,2,1,0:T(8,128)S(1)} %collective-permute-done.3.second, f32[5,5,64,128]{3,2,1,0:T(8,128)S(1)} %strips.1.strip, ...), custom_call_target="tpu_custom_call" | custom-call | tf_op jit(solution)/shard_map/pack_x/pallas_call | solution.py:484
  27.4 1.3 %collective-permute-start.4 = (f32[5,72,128]{2,1,0:T(8,128)S(1)}, f32[5,72,128]{2,1,0:T(8,128)S(1)}, u32[]{:S(2)}, u32[]{:S(2)}) collective-permute-start(f32[5,72,128]{2,1,0:T(8,128)S(1)} %get-tuple-element.20), channel_id=1, source_target_pairs={{0,32},{32,0},{64,96},{96,64},{1,33},{33,1},{65,97},{97,65},{2,34}... | collective-permute-start | bytes 552968 | tf_op jit(solution)/shard_map/ppermute | solution.py:62
  28.7 1.8 %collective-permute-start.5 = (f32[5,72,128]{2,1,0:T(8,128)S(1)}, f32[5,72,128]{2,1,0:T(8,128)S(1)}, u32[]{:S(2)}, u32[]{:S(2)}) collective-permute-start(f32[5,72,128]{2,1,0:T(8,128)S(1)} %get-tuple-element.21), channel_id=1, source_target_pairs={{0,96},{32,64},{64,32},{96,0},{1,97},{33,65},{65,33},{97,1},{2,98}... | collective-permute-start | bytes 552968 | tf_op jit(solution)/shard_map/ppermute | solution.py:61
  30.5 4.7 %y_strip.1.acc3 = f32[90,8,128]{2,1,0:T(8,128)S(1)} custom-call(f32[5,24,2,8,128]{4,3,2,1,0:T(8,128)S(1)} %get-tuple-element.22.edges, f32[5,24,8,128]{3,2,1,0:T(8,128)S(1)} %get-tuple-element.23.rim), custom_call_target="tpu_custom_call" | custom-call | flops 134217728 | bytes 1048576 | tf_op jit(solution)/shard_map/y_strip/pallas_call | solution.py:576
  35.2 0.0 collective-permute-done.4.first
  35.2 0.0 collective-permute-done.5.second
  35.3 4.0 %x_strip.1 = f32[128,1,128]{2,1,0:T(1,128)S(1)} custom-call(f32[5,5,64,128]{3,2,1,0:T(8,128)S(1)} %strips.1.strip, f32[5,5,8,128]{3,2,1,0:T(8,128)S(1)} %get-tuple-element.19.side, f32[5,72,128]{2,1,0:T(8,128)S(1)} %collective-permute-done.4.first, f32[5,72,128]{2,1,0:T(8,128)S(1)} %collective-permute-done.5.second, ...), custom_call_target="tpu_custom_call" | custom-call | tf_op jit(solution)/shard_map/x_strip/pallas_call | solution.py:701
  39.2 19.0 %all_to_all.5.refs_0_ = f32[128,1,128]{2,1,0:T(1,128)S(1)} all-to-all(f32[128,1,128]{2,1,0:T(1,128)S(1)} %x_strip.1), channel_id=1, replica_groups=mesh['gx'=4,'gy'=4,'gz'=8] {'gx','gy','gz'}, dimensions={0} | all-to-all | bytes 131072 | tf_op jit(solution)/shard_map/all_to_all | solution.py:804
  58.2 3.9 %finish.1 = (f32[4,16,64,128]{3,2,1,0:T(8,128)}, f32[20,20]{1,0:T(8,128)}) custom-call(f32[128,1,128]{2,1,0:T(1,128)S(1)} %all_to_all.5.refs_0_, f32[4,16,64,128]{3,2,1,0:T(8,128)S(1)} %copy-done.1), custom_call_target="tpu_custom_call" | custom-call | tf_op jit(solution)/shard_map/finish/pallas_call | solution.py:775
Async XLA Ops:
  0.6 1.6 %copy-start = (f32[4,16,64,128]{3,2,1,0:T(8,128)S(1)}, f32[4,16,64,128]{3,2,1,0:T(8,128)}, u32[]{:S(2)}) copy-start(f32[4,16,64,128]{3,2,1,0:T(8,128)} %refs_1_.1) | copy-start | bytes 6291460
  2.2 1.0 %copy-start.2 = (f32[16,64,128]{2,1,0:T(8,128)S(1)}, f32[16,64,128]{2,1,0:T(8,128)}, u32[]{:S(2)}) copy-start(f32[16,64,128]{2,1,0:T(8,128)} %kappa.7) | copy-start | bytes 1572868
  3.3 3.3 %copy-start.1 = (f32[4,16,64,128]{3,2,1,0:T(8,128)S(1)}, f32[4,16,64,128]{3,2,1,0:T(8,128)}, u32[]{:S(2)}) copy-start(f32[4,16,64,128]{3,2,1,0:T(8,128)} %refs_1_.1) | copy-start | bytes 6291460
  3.3 3.3 %copy-start.3 = (f32[16,64,128]{2,1,0:T(8,128)S(1)}, f32[16,64,128]{2,1,0:T(8,128)}, u32[]{:S(2)}) copy-start(f32[16,64,128]{2,1,0:T(8,128)} %kappa.7) | copy-start | bytes 1572868
  3.7 9.6 %collective-permute-start = (f32[5,4,64,128]{3,2,1,0:T(8,128)S(1)}, f32[5,4,64,128]{3,2,1,0:T(8,128)S(1)}, u32[]{:S(2)}, u32[]{:S(2)}) collective-permute-start(f32[5,4,64,128]{3,2,1,0:T(8,128)S(1)} %get-tuple-element.13), channel_id=1, source_target_pairs={{0,1},{1,0},{2,3},{3,2},{4,5},{5,4},{6,7},{7,6},{8,9},{9,8},{10,11... | collective-permute-start | bytes 1966088 | tf_op jit(solution)/shard_map/ppermute | solution.py:62
  5.2 10.3 %collective-permute-start.1 = (f32[5,4,64,128]{3,2,1,0:T(8,128)S(1)}, f32[5,4,64,128]{3,2,1,0:T(8,128)S(1)}, u32[]{:S(2)}, u32[]{:S(2)}) collective-permute-start(f32[5,4,64,128]{3,2,1,0:T(8,128)S(1)} %get-tuple-element.14), channel_id=1, source_target_pairs={{0,7},{1,2},{2,1},{3,4},{4,3},{5,6},{6,5},{7,0},{8,15},{9,10},{10,... | collective-permute-start | bytes 1966088 | tf_op jit(solution)/shard_map/ppermute | solution.py:61
  15.8 10.6 %collective-permute-start.2 = (f32[5,12,8,128]{3,2,1,0:T(8,128)S(1)}, f32[5,12,8,128]{3,2,1,0:T(8,128)S(1)}, u32[]{:S(2)}, u32[]{:S(2)}) collective-permute-start(f32[5,12,8,128]{3,2,1,0:T(8,128)S(1)} %get-tuple-element.16), channel_id=1, source_target_pairs={{0,8},{8,0},{16,24},{24,16},{1,9},{9,1},{17,25},{25,17},{2,10},{10... | collective-permute-start | bytes 737288 | tf_op jit(solution)/shard_map/ppermute | solution.py:62
  17.6 8.8 %collective-permute-start.3 = (f32[5,12,8,128]{3,2,1,0:T(8,128)S(1)}, f32[5,12,8,128]{3,2,1,0:T(8,128)S(1)}, u32[]{:S(2)}, u32[]{:S(2)}) collective-permute-start(f32[5,12,8,128]{3,2,1,0:T(8,128)S(1)} %get-tuple-element.17), channel_id=1, source_target_pairs={{0,24},{8,16},{16,8},{24,0},{1,25},{9,17},{17,9},{25,1},{2,26},{10... | collective-permute-start | bytes 737288 | tf_op jit(solution)/shard_map/ppermute | solution.py:61
  27.4 7.8 %collective-permute-start.4 = (f32[5,72,128]{2,1,0:T(8,128)S(1)}, f32[5,72,128]{2,1,0:T(8,128)S(1)}, u32[]{:S(2)}, u32[]{:S(2)}) collective-permute-start(f32[5,72,128]{2,1,0:T(8,128)S(1)} %get-tuple-element.20), channel_id=1, source_target_pairs={{0,32},{32,0},{64,96},{96,64},{1,33},{33,1},{65,97},{97,65},{2,34}... | collective-permute-start | bytes 552968 | tf_op jit(solution)/shard_map/ppermute | solution.py:62
  28.7 6.5 %collective-permute-start.5 = (f32[5,72,128]{2,1,0:T(8,128)S(1)}, f32[5,72,128]{2,1,0:T(8,128)S(1)}, u32[]{:S(2)}, u32[]{:S(2)}) collective-permute-start(f32[5,72,128]{2,1,0:T(8,128)S(1)} %get-tuple-element.21), channel_id=1, source_target_pairs={{0,96},{32,64},{64,32},{96,0},{1,97},{33,65},{65,33},{97,1},{2,98}... | collective-permute-start | bytes 552968 | tf_op jit(solution)/shard_map/ppermute | solution.py:61

commit v3 on v2

--- a/solution.py
+++ b/solution.py
@@ -13,8 +13,8 @@
 NPAIRS = len(PAIRS)
 DEEP = BASIS
 ARRAYS = COLS + 1
-PITCH = 6 * DEEP
-SLABS = 5
+PITCH = 4 * DEEP
+SLABS = 3
 
 basis_shift = 6.0
 basis_scale = 3.0
@@ -61,6 +61,19 @@
     second = lax.ppermute(second, axis, other)
     first = lax.ppermute(first, axis, [(i, i ^ 1) for i in range(peers)])
     return first, second
+
+
+def pull(face, axis):
+    peers = lax.axis_size(axis)
+    return lax.ppermute(face, axis, [(i, (i - 1) % peers) for i in range(peers)])
+
+
+def last_on(axis):
+    return lax.axis_index(axis) == lax.axis_size(axis) - 1
+
+
+def cut(there, value):
+    return jnp.where(there, 0.0, value)
 
 
 def link(one, other, bounded):
@@ -404,10 +417,10 @@
 def strip_of(planes):
     lane = lanes(8)
     offset, group = lane % PITCH, lane // PITCH
-    index = jnp.where(offset < 8, 120 + offset, jnp.maximum(offset - 16, 0))
-    strip = jnp.zeros((8, 128), F32)
-    for g, plane in enumerate(planes):
-        strip = jnp.where(group == g, permute_lanes(plane, index), strip)
+    index = jnp.where(offset < 8, 120 + offset, offset - 8)
+    strip = permute_lanes(planes[0], index)
+    for g, plane in enumerate(planes[1:]):
+        strip = jnp.where(group == g + 1, permute_lanes(plane, index), strip)
     return strip
 
 
@@ -446,9 +459,14 @@
     )(block, kappa, first, second)
 
 
-def pack_x_kernel(first, second, strip, after, rim, side, to_first, to_second):
+HALVES = [(a, q) for a in range(ARRAYS) for q in range(SLABS)]
+
+
+def pack_x_kernel(first, second, strip, after, rim, side, face):
+    depth = rim.shape[1]
+    ny = strip.shape[2]
     half = sublanes(8) < 4
-    depth, tiles = rim.shape[1], to_first.shape[1] // 8
+    low = lanes(8) % PITCH < 8
 
     def duos(duo, carry):
         for a in range(ARRAYS):
@@ -458,37 +476,34 @@
         return carry
 
     lax.fori_loop(0, depth // 2, duos, 0, unroll=4)
-    slot = lanes(8) % PITCH // DEEP
-
-    def arrays(a, carry):
-        for q in range(SLABS):
-            side[a, q] = strip_of([rim[a, z] for z in range(q, depth, SLABS)])
-        for t in range(tiles):
-            upper = jnp.zeros((8, 128), F32)
-            lower = jnp.zeros((8, 128), F32)
-            for q in range(SLABS):
-                value = strip[a, q, tile(t)] if t < tiles - 1 else side[a, q]
-                upper = jnp.where(slot == q, pltpu.roll(value, (4 * q - 4) % 128, 1), upper)
-                lower = jnp.where(slot == q, pltpu.roll(value, (4 * q - 16) % 128, 1), lower)
-            to_first[a, tile(t)] = even_first("gx", upper, lower)
-            to_second[a, tile(t)] = even_first("gx", lower, upper)
-        return carry
-
-    lax.fori_loop(0, ARRAYS, arrays, 0)
+    for a, q in HALVES:
+        side[a, q] = strip_of([rim[a, z] for z in range(q, depth, SLABS)])
+
+    def pack(at, get):
+        for n in range(0, len(HALVES), 2):
+            value = pltpu.roll(get(*HALVES[n]), 120, 1)
+            if n + 1 < len(HALVES):
+                value = jnp.where(low, value, get(*HALVES[n + 1]))
+            face[n // 2, at] = value
+
+    def rows(t, carry):
+        at = pl.ds(pl.multiple_of(t * 8, 8), 8)
+        pack(at, lambda a, q: strip[a, q, at])
+        return carry
+
+    lax.fori_loop(0, ny // 8, rows, 0, unroll=4)
+    pack(slice(ny, ny + 8), lambda a, q: side[a, q])
 
 
 def pack_x(first, second, strip, after):
     _, _, ny, nx = strip.shape
-    depth = first.shape[1] * 2
-    face = (ARRAYS, ny + 8, nx)
+    face = ((len(HALVES) + 1) // 2, ny + 8, nx)
+    rim = (ARRAYS, 2 * first.shape[1], 8, nx)
     return pl.pallas_call(
         pack_x_kernel,
-        out_shape=[
-            jax.ShapeDtypeStruct(s, F32)
-            for s in ((ARRAYS, depth, 8, nx), (ARRAYS, SLABS, 8, nx), face, face)
-        ],
+        out_shape=[jax.ShapeDtypeStruct(s, F32) for s in (rim, (ARRAYS, SLABS, 8, nx), face)],
         in_specs=[VMEM] * 3 + [pl.BlockSpec(memory_space=pl.ANY)],
-        out_specs=[VMEM] * 4,
+        out_specs=[VMEM] * 3,
         compiler_params=params(16),
         name="pack_x",
     )(first, second, strip, after)
@@ -590,9 +605,10 @@
     )(edges, rim)
 
 
-def x_strip_kernel(strip, side, first, second, acc1, acc2, acc3, out, s0, s1, s2, s3, kr, w, wz, acc):
-    tiles = first.shape[1] // 8
+def x_strip_kernel(strip, side, face, acc1, acc2, acc3, out, s0, s1, s2, s3, kr, w, wz, acc):
+    tiles = face.shape[1] // 8
     offset = lanes(8) % PITCH
+    right_seam, left_seam = (last_on("gx") & (offset == at) for at in (7, 8))
 
     def rows(t):
         return slice(8 + 8 * t, 16 + 8 * t)
@@ -614,27 +630,21 @@
             return ref[index + (q - 1, at)]
         return pltpu.roll(ref[index + (SLABS - 1, at)], PITCH, 1)
 
-    def fill(a, put):
+    for n, (a, q) in enumerate(HALVES):
         for t in range(tiles):
-            upper, lower = sides("gx", first[a, tile(t)], second[a, tile(t)])
-            for q in range(SLABS):
-                value = strip[a, q, tile(t)] if t < tiles - 1 else side[a, q]
-                value = jnp.where(offset // 4 == 2, pltpu.roll(upper, (8 - 4 * q) % 128, 1), value)
-                value = jnp.where(offset // 4 == 3, pltpu.roll(lower, (12 - 4 * q) % 128, 1), value)
-                put(q, t, value)
-
-    fill(COLS, lambda q, t, value: lay(kr, (q,), t, value))
-
-    def fill_column(c, carry):
-        fill(c, lambda q, t, value: lay(s0, (c, q), t, value))
-        return carry
-
-    lax.fori_loop(0, COLS, fill_column, 0)
+            value = strip[a, q, tile(t)] if t < tiles - 1 else side[a, q]
+            beyond = face[n // 2, tile(t)]
+            beyond = pltpu.roll(beyond, 8, 1) if n % 2 == 0 else beyond
+            value = jnp.where(offset < 8, value, beyond)
+            if a < COLS:
+                lay(s0, (a, q), t, value)
+            else:
+                lay(kr, (q,), t, value)
 
     for q in range(SLABS):
         for t in range(tiles):
             k = kr[q, rows(t)]
-            right, left = pltpu.roll(k, 127, 1), pltpu.roll(k, 1, 1)
+            right, left = cut(right_seam, pltpu.roll(k, 127, 1)), cut(left_seam, pltpu.roll(k, 1, 1))
             above = kr[q, 9 + 8 * t : 17 + 8 * t]
             below = kr[q, 7 + 8 * t : 15 + 8 * t]
             far, near = next_slab(kr, (), q, rows(t)), last_slab(kr, (), q, rows(t))
@@ -669,21 +679,21 @@
                         lay(dst, (c, q), t, news[c])
                 if t < tiles - 1:
                     sums.products(k, olds, news)
-            sums.flush(acc.at[0 if q < SLABS - 1 else 1])
+            sums.flush(acc.at[q])
 
         for q in range(SLABS):
             slab(q)
 
     lane1 = lax.broadcasted_iota(jnp.int32, (1, 128), 1)
-    group, place = lane1 // PITCH, lane1 % PITCH // DEEP
-    here = (place == 1) | (place == 4)
-    total = jnp.zeros((acc.shape[1], 128), F32)
-    for kept, sums in (
-        ((lane1 >= DEEP) & (lane1 < 128 - DEEP), acc1[...] + acc2[...] + acc3[...]),
-        (here & (group >= 1) & (group <= 3), acc[0]),
-        (here & (group <= 3), acc[1]),
-    ):
-        total = total + jnp.where(kept, jnp.sum(sums, axis=1), 0.0)
+    z = lane1 // PITCH * SLABS
+    here = (lane1 % PITCH >= DEEP) & (lane1 % PITCH < PITCH - DEEP)
+    groups = 128 // PITCH
+    total = jnp.where(
+        (lane1 >= DEEP) & (lane1 < 128 - DEEP), jnp.sum(acc1[...] + acc2[...] + acc3[...], axis=1), 0.0
+    )
+    for q in range(SLABS):
+        kept = here & (z + q >= DEEP) & (z + q < groups * SLABS - DEEP)
+        total = total + jnp.where(kept, jnp.sum(acc[q], axis=1), 0.0)
     total = jnp.concatenate([total, jnp.zeros((128 - total.shape[0], 128), F32)], 0)
     row = lax.dot_general(
         jnp.ones((8, 128), F32),
@@ -695,77 +705,93 @@
     out[...] = jnp.broadcast_to(row[0:1][None], out.shape)
 
 
-def x_strip(strip, side, first, second, accs, peers):
-    cols, slabs, ny, nx = strip.shape
+def x_strip(strip, side, face, accs, peers):
+    _, slabs, ny, nx = strip.shape
     laid = (slabs, ny + 24, nx)
     return pl.pallas_call(
         x_strip_kernel,
         out_shape=jax.ShapeDtypeStruct((peers, 1, 128), F32),
-        in_specs=[VMEM] * 7,
+        in_specs=[VMEM] * 6,
         out_specs=VMEM,
         scratch_shapes=[pltpu.VMEM((COLS,) + laid, F32)] * 4
         + [
             pltpu.VMEM(laid, F32),
             pltpu.VMEM((4,) + laid, F32),
             pltpu.VMEM((slabs + 1,) + laid[1:], F32),
-            pltpu.VMEM((2, MOMENTS * NPAIRS, 8, nx), F32),
+            pltpu.VMEM((slabs, MOMENTS * NPAIRS, 8, nx), F32),
         ],
         compiler_params=params(16),
         name="x_strip",
-    )(strip, side, first, second, *accs)
+    )(strip, side, face, *accs)
+
+
+def factor(row, triangle, coef):
+    lane, sub = lanes(8), sublanes(8)
+    blocks = (KRYLOV + 7) // 8
+    columns = []
+    for b in range(KRYLOV):
+        parts = []
+        for i in range(blocks):
+            a = sub + 8 * i
+            low, high = jnp.minimum(a % COLS, b % COLS), jnp.maximum(a % COLS, b % COLS)
+            pair = low * COLS - (low * (low - 1)) // 2 + high - low
+            index = jnp.where(a < KRYLOV, (a // COLS + b // COLS) * NPAIRS + pair, 127)
+            parts.append(permute_lanes(row, index))
+        columns.append(parts)
+    at = 0
+    for k in range(KRYLOV):
+        i, j = k // 8, k % 8
+
+        def entry(b):
+            return jnp.broadcast_to(columns[b][i][j : j + 1], (8, 128))
+
+        pivot = entry(k)
+        inverse = 1.0 / pivot
+        root = jnp.sqrt(pivot)
+        scale = 1.0 / root
+        line = jnp.where(lane == k, root, 0.0)
+        if k < COLS:
+            coef[at] = scale
+            at += 1
+        for b in range(k + 1, KRYLOV):
+            value = entry(b)
+            line = jnp.where(lane == b, value * scale, line)
+            if b < COLS:
+                coef[at] = value * scale
+                at += 1
+            value = value * inverse
+            for n in range((k + 1) // 8, blocks):
+                columns[b][n] = columns[b][n] - columns[k][n] * value
+        triangle[k : k + 1, :] = line[0:1, 0:KRYLOV]
 
 
 def finish_kernel(ncells, parts, block, ortho, triangle, coef):
-    @pl.when(pl.program_id(0) == 0)
+    step = pl.program_id(0)
+
+    @pl.when(step == 0)
     def _():
         row = jnp.sum(parts[...], axis=0) * (1.0 / ncells)
-        row = jnp.broadcast_to(row, (24, 128))
-        a, b = sublanes(24), lanes(24)
-        c, d = a % 4, b % 4
-        low, high = jnp.minimum(c, d), jnp.maximum(c, d)
-        pair = low * 4 - (low * (low - 1)) // 2 + high - low
-        inside = (a < KRYLOV) & (b < KRYLOV)
-        index = jnp.where(inside, (a // 4 + b // 4) * NPAIRS + pair, 127)
-        matrix = permute_lanes(row, index)
-        lane = lanes(1)
-        uppers = []
-        for k in range(KRYLOV):
-            line = matrix[k : k + 1, :]
-            pivot = line[:, k : k + 1]
-            upper = jnp.where(lane >= k, line / jnp.sqrt(pivot), 0.0)
-            uppers.append(upper)
-            triangle[k : k + 1, :] = upper[:, 0:KRYLOV]
-            if k + 1 < KRYLOV:
-                matrix = matrix - matrix[:, k : k + 1] * (line / pivot)
-        at = 0
-        for i in range(COLS):
-            for j in range(i, COLS):
-                value = uppers[i][:, j : j + 1]
-                value = 1.0 / value if i == j else value
-                coef[at] = jnp.broadcast_to(value, (8, 128))
-                at += 1
+        factor(jnp.broadcast_to(row, (8, 128)), triangle, coef)
 
     u = {}
-    at = 0
     for i in range(COLS):
         for j in range(i, COLS):
-            u[i, j] = coef[at]
-            at += 1
+            u[i, j] = coef[len(u)]
+    slabs = ortho.shape[1]
 
     def slab(z, carry):
         for t in range(ortho.shape[2] // 8):
-            rows = slice(8 * t, 8 * t + 8)
             done = []
             for j in range(COLS):
-                value = block[j, z, rows]
+                value = block[j, step * slabs + z, tile(t)]
                 for i in range(j):
                     value = value - u[i, j] * done[i]
                 value = value * u[j, j]
-                ortho[j, z, rows] = value
+                ortho[j, z, tile(t)] = value
                 done.append(value)
         return carry
 
-    lax.fori_loop(0, ortho.shape[1], slab, 0)
+    lax.fori_loop(0, slabs, slab, 0, unroll=2)
 
 
 def finish(parts, block, ncells):
@@ -779,7 +805,7 @@
             jax.ShapeDtypeStruct(block.shape, F32),
             jax.ShapeDtypeStruct((KRYLOV, KRYLOV), F32),
         ],
-        in_specs=[pl.BlockSpec(parts.shape, lambda i: (0, 0, 0)), piece],
+        in_specs=[pl.BlockSpec(parts.shape, lambda i: (0, 0, 0)), VMEM],
         out_specs=[piece, pl.BlockSpec((KRYLOV, KRYLOV), lambda i: (0, 0))],
         scratch_shapes=[pltpu.VMEM((NPAIRS, 8, 128), F32)],
         compiler_params=params(16),
@@ -791,16 +817,17 @@
     axes = ("gx", "gy", "gz")
     peers = lax.axis_size(axes)
     ncells = float(kappa.size * peers)
-    first, second = swap(*pack_z(block, kappa), "gz")
+    far = [pltpu.with_memory_space_constraint(value, pltpu.HBM) for value in (block, kappa)]
+    first, second = swap(*pack_z(*far), "gz")
     acc1, edge = inner(block, kappa)
     edges, y_first, y_second = pack_y(block, kappa, first, second, acc1)
     y_first, y_second = swap(y_first, y_second, "gy")
     strip = strips(block, kappa, first, second)
     acc2 = outer(block, kappa, edge, first, second)
-    rim, side, x_first, x_second = pack_x(y_first, y_second, strip, acc2)
-    x_first, x_second = swap(x_first, x_second, "gx")
+    rim, side, face = pack_x(y_first, y_second, strip, acc2)
+    face = pull(face, "gx")
     acc3 = y_strip(edges, rim)
-    moments = x_strip(strip, side, x_first, x_second, (acc1, acc2, acc3), peers)
+    moments = x_strip(strip, side, face, (acc1, acc2, acc3), peers)
     parts = lax.all_to_all(moments, axes, 0, 0, tiled=True)
     return tuple(finish(parts, block, ncells))
 

time: 62.4 us -> 59 us (0.946)
  Pallas kernels: 27.6 us -> 24.9 us
  local copies, waits for them, and re-layouts: 2.63 us -> 0.01 us
  blocking collectives: 19 us -> 21.5 us
    unnamed x8 -> x4, local copies, waits for them, and re-layouts: 2.63 us -> 0.01 us
    ppermute x0 -> x1, starting transfers between devices: none -> 2.53 us  [pull(): lax.ppermute(face, axis, [(i, (i - 1) % peers) for i in range(peers)])]
    all_to_all x1, blocking collectives: 19 us -> 21.5 us  [shards(): parts = lax.all_to_all(moments, axes, 0, 0, tiled=True)]
    ppermute x3 -> x2, starting transfers between devices: 5.42 us -> 3.6 us  [swap(): second = lax.ppermute(second, axis, other)]
    pallas_call x1, Pallas kernels: 3.98 us -> 2.36 us  [x_strip(): pl.pallas_call(x_strip_kernel, out_shape=jax.ShapeDtypeStruct((peers, 1,...]
    pallas_call x1, Pallas kernels: 3.92 us -> 2.47 us  [finish(): pl.pallas_call(lambda *refs: finish_kernel(ncells, *refs), grid=(steps,),...]
    ppermute x3 -> x2, starting transfers between devices: 4.59 us -> 3.3 us  [swap(): first = lax.ppermute(first, axis, [(i, i ^ 1) for i in range(peers)])]
    pallas_call x1, Pallas kernels: 0.45 us -> 1.46 us  [pack_z(): pl.pallas_call(pack_z_kernel, out_shape=[face, face], in_specs=[HBM, HBM]...]
  transfers between devices with their start and end apart: 6 -> 5, of which waited for: 1 -> 1; matrix products, arithmetic and copies ran while one was open for 0% -> 0% of each run, Pallas kernels for 29% -> 30%
where the time goes in v3:
time: 59 us; the launch traced here: 58.8 us
  Pallas kernels  24.9 us (42%)
  blocking collectives  21.5 us (36%)
  starting transfers between devices  9.43 us (16%)
  waiting for transfers between devices  2.26 us (4%)
  between operations  0.73 us (1%)
    all_to_all x1, blocking collectives, shards(): parts = lax.all_to_all(moments, axes, 0, 0, tiled=True)  21.5 us
    pallas_call x1, Pallas kernels, inner(): pl.pallas_call(inner_kernel, out_shape=[jax.ShapeDtypeStruct((MOMENTS * N...  6.67 us
    pallas_call x1, Pallas kernels, outer(): pl.pallas_call(outer_kernel, out_shape=jax.ShapeDtypeStruct((MOMENTS * NP...  4.88 us
    pallas_call x1, Pallas kernels, y_strip(): pl.pallas_call(y_strip_kernel, out_shape=jax.ShapeDtypeStruct((MOMENTS *...  4.68 us
    ppermute x2, starting transfers between devices, swap(): second = lax.ppermute(second, axis, other)  3.6 us
    ppermute x2, starting transfers between devices, swap(): first = lax.ppermute(first, axis, [(i, i ^ 1) for i in range(peers)])  3.3 us
    ppermute x1, starting transfers between devices, pull(): lax.ppermute(face, axis, [(i, (i - 1) % peers) for i in range(peers)])  2.53 us
    pallas_call x1, Pallas kernels, finish(): pl.pallas_call(lambda *refs: finish_kernel(ncells, *refs), grid=(steps,),...  2.47 us
  transfers between devices with their start and end apart: 5, of which 1 were waited for; matrix products, arithmetic and copies ran while one was open for 0% of the time, Pallas kernels for 30%

profile of v3, /device:TPU:1, one launch (start us, length us, event | category | flops | bytes accessed | tf_op | source)
XLA Modules:
  0.0 58.8 jit_solution(311022400035449062)
XLA Ops:
  0.6 0.0 copy-start
  0.6 0.0 copy-start.1
  0.6 1.5 %pack_z.1 = (f32[5,4,64,128]{3,2,1,0:T(8,128)S(1)}, f32[5,4,64,128]{3,2,1,0:T(8,128)S(1)}) custom-call(f32[4,16,64,128]{3,2,1,0:T(8,128)} %refs_1_.1, f32[16,64,128]{2,1,0:T(8,128)} %kappa.7), custom_call_target="tpu_custom_call" | custom-call | tf_op jit(solution)/shard_map/pack_z/pallas_call | solution.py:164
  2.1 1.5 %collective-permute-start = (f32[5,4,64,128]{3,2,1,0:T(8,128)S(1)}, f32[5,4,64,128]{3,2,1,0:T(8,128)S(1)}, u32[]{:S(2)}, u32[]{:S(2)}) collective-permute-start(f32[5,4,64,128]{3,2,1,0:T(8,128)S(1)} %get-tuple-element.12), channel_id=1, source_target_pairs={{0,1},{1,0},{2,3},{3,2},{4,5},{5,4},{6,7},{7,6},{8,9},{9,8},{10,11... | collective-permute-start | bytes 1966088 | tf_op jit(solution)/shard_map/ppermute | solution.py:62
  3.6 1.4 %collective-permute-start.1 = (f32[5,4,64,128]{3,2,1,0:T(8,128)S(1)}, f32[5,4,64,128]{3,2,1,0:T(8,128)S(1)}, u32[]{:S(2)}, u32[]{:S(2)}) collective-permute-start(f32[5,4,64,128]{3,2,1,0:T(8,128)S(1)} %get-tuple-element.13), channel_id=1, source_target_pairs={{0,7},{1,2},{2,1},{3,4},{4,3},{5,6},{6,5},{7,0},{8,15},{9,10},{10,... | collective-permute-start | bytes 1966088 | tf_op jit(solution)/shard_map/ppermute | solution.py:61
  5.0 0.0 copy-done
  5.0 0.0 copy-done.1
  5.0 6.7 %inner.1 = (f32[90,8,128]{2,1,0:T(8,128)S(1)}, f32[3,2,2,4,64,128]{5,4,3,2,1,0:T(8,128)S(1)}) custom-call(f32[4,16,64,128]{3,2,1,0:T(8,128)S(1)} %copy-done, f32[16,64,128]{2,1,0:T(8,128)S(1)} %copy-done.1), custom_call_target="tpu_custom_call" | custom-call | flops 268435456 | bytes 1048576 | tf_op jit(solution)/shard_map/inner/pallas_call | solution.py:237
  11.7 0.0 collective-permute-done.first.f_low.f_high
  11.7 2.3 %collective-permute-done.1.second.s_low.s_high = f32[5,4,64,128]{3,2,1,0:T(8,128)S(1)} collective-permute-done((f32[5,4,64,128]{3,2,1,0:T(8,128)S(1)}, f32[5,4,64,128]{3,2,1,0:T(8,128)S(1)}, u32[]{:S(2)}, u32[]{:S(2)}) %collective-permute-start.1) | collective-permute-done | bytes 655392 | tf_op jit(solution)/shard_map/ppermute | solution.py:61
  13.9 0.3 pack_y.1
  14.2 1.8 %collective-permute-start.2 = (f32[5,12,8,128]{3,2,1,0:T(8,128)S(1)}, f32[5,12,8,128]{3,2,1,0:T(8,128)S(1)}, u32[]{:S(2)}, u32[]{:S(2)}) collective-permute-start(f32[5,12,8,128]{3,2,1,0:T(8,128)S(1)} %get-tuple-element.15), channel_id=1, source_target_pairs={{0,8},{8,0},{16,24},{24,16},{1,9},{9,1},{17,25},{25,17},{2,10},{10... | collective-permute-start | bytes 737288 | tf_op jit(solution)/shard_map/ppermute | solution.py:62
  16.0 2.2 %collective-permute-start.3 = (f32[5,12,8,128]{3,2,1,0:T(8,128)S(1)}, f32[5,12,8,128]{3,2,1,0:T(8,128)S(1)}, u32[]{:S(2)}, u32[]{:S(2)}) collective-permute-start(f32[5,12,8,128]{3,2,1,0:T(8,128)S(1)} %get-tuple-element.16), channel_id=1, source_target_pairs={{0,24},{8,16},{16,8},{24,0},{1,25},{9,17},{17,9},{25,1},{2,26},{10... | collective-permute-start | bytes 737288 | tf_op jit(solution)/shard_map/ppermute | solution.py:61
  18.2 1.6 %strips.1.strip = f32[5,3,64,128]{3,2,1,0:T(8,128)S(1)} custom-call(f32[4,16,64,128]{3,2,1,0:T(8,128)S(1)} %copy-done, f32[16,64,128]{2,1,0:T(8,128)S(1)} %copy-done.1, f32[5,4,64,128]{3,2,1,0:T(8,128)S(1)} %collective-permute-done.first.f_low.f_high, f32[5,4,64,128]{3,2,1,0:T(8,128)S(1)} %collective-permute-done.1.second.s_low.s_high), custom_call_target="tpu_custom_call" | custom-call | flops 33554432 | bytes 1048576 | tf_op jit(solution)/shard_map/strips/pallas_call | solution.py:451
  19.8 4.9 %outer.1.after.acc2 = f32[90,8,128]{2,1,0:T(8,128)S(1)} custom-call(f32[4,16,64,128]{3,2,1,0:T(8,128)S(1)} %copy-done, f32[16,64,128]{2,1,0:T(8,128)S(1)} %copy-done.1, f32[3,2,2,4,64,128]{5,4,3,2,1,0:T(8,128)S(1)} %get-tuple-element.17.edge, f32[5,4,64,128]{3,2,1,0:T(8,128)S(1)} %collective-permute-done.first.f_low.f_high, ...), custom_call_target="tpu_custom_call" | custom-call | flops 134217728 | bytes 1048576 | tf_op jit(solution)/shard_map/outer/pallas_call | solution.py:400
  24.7 0.0 collective-permute-done.2.first
  24.7 0.0 collective-permute-done.3.second
  24.7 0.6 pack_x.1
  25.3 2.5 %collective-permute-start.4 = (f32[8,72,128]{2,1,0:T(8,128)S(1)}, f32[8,72,128]{2,1,0:T(8,128)S(1)}, u32[]{:S(2)}, u32[]{:S(2)}) collective-permute-start(f32[8,72,128]{2,1,0:T(8,128)S(1)} %get-tuple-element.19), channel_id=1, source_target_pairs={{0,96},{32,0},{64,32},{96,64},{1,97},{33,1},{65,33},{97,65},{2,98}... | collective-permute-start | bytes 884744 | tf_op jit(solution)/shard_map/ppermute | solution.py:68
  27.8 4.7 %y_strip.1.acc3 = f32[90,8,128]{2,1,0:T(8,128)S(1)} custom-call(f32[5,24,2,8,128]{4,3,2,1,0:T(8,128)S(1)} %get-tuple-element.20.edges, f32[5,24,8,128]{3,2,1,0:T(8,128)S(1)} %get-tuple-element.21.rim), custom_call_target="tpu_custom_call" | custom-call | flops 134217728 | bytes 1048576 | tf_op jit(solution)/shard_map/y_strip/pallas_call | solution.py:591
  32.5 0.0 collective-permute-done.4.face
  32.5 2.4 %x_strip.1 = f32[128,1,128]{2,1,0:T(1,128)S(1)} custom-call(f32[5,3,64,128]{3,2,1,0:T(8,128)S(1)} %strips.1.strip, f32[5,3,8,128]{3,2,1,0:T(8,128)S(1)} %get-tuple-element.18.side, f32[8,72,128]{2,1,0:T(8,128)S(1)} %collective-permute-done.4.face, f32[90,8,128]{2,1,0:T(8,128)S(1)} %get-tuple-element.14.after.acc1, f32[90,8,128]{2,1,0:T(8,128)S(1)} %outer.1.after.acc2, ...), custom_call_target="tpu_custom_call" | custom-call | tf_op jit(solution)/shard_map/x_strip/pallas_call | solution.py:711
  34.9 21.5 %all_to_all.5.refs_0_ = f32[128,1,128]{2,1,0:T(1,128)S(1)} all-to-all(f32[128,1,128]{2,1,0:T(1,128)S(1)} %x_strip.1), channel_id=1, replica_groups=mesh['gx'=4,'gy'=4,'gz'=8] {'gx','gy','gz'}, dimensions={0} | all-to-all | bytes 131072 | tf_op jit(solution)/shard_map/all_to_all | solution.py:831
  56.4 2.5 %finish.1 = (f32[4,16,64,128]{3,2,1,0:T(8,128)}, f32[20,20]{1,0:T(8,128)}) custom-call(f32[128,1,128]{2,1,0:T(1,128)S(1)} %all_to_all.5.refs_0_, f32[4,16,64,128]{3,2,1,0:T(8,128)S(1)} %copy-done), custom_call_target="tpu_custom_call" | custom-call | tf_op jit(solution)/shard_map/finish/pallas_call | solution.py:801
Async XLA Ops:
  0.6 4.3 %copy-start = (f32[4,16,64,128]{3,2,1,0:T(8,128)S(1)}, f32[4,16,64,128]{3,2,1,0:T(8,128)}, u32[]{:S(2)}) copy-start(f32[4,16,64,128]{3,2,1,0:T(8,128)} %refs_1_.1) | copy-start | bytes 6291460
  0.6 4.3 %copy-start.1 = (f32[16,64,128]{2,1,0:T(8,128)S(1)}, f32[16,64,128]{2,1,0:T(8,128)}, u32[]{:S(2)}) copy-start(f32[16,64,128]{2,1,0:T(8,128)} %kappa.7) | copy-start | bytes 1572868
  2.1 9.5 %collective-permute-start = (f32[5,4,64,128]{3,2,1,0:T(8,128)S(1)}, f32[5,4,64,128]{3,2,1,0:T(8,128)S(1)}, u32[]{:S(2)}, u32[]{:S(2)}) collective-permute-start(f32[5,4,64,128]{3,2,1,0:T(8,128)S(1)} %get-tuple-element.12), channel_id=1, source_target_pairs={{0,1},{1,0},{2,3},{3,2},{4,5},{5,4},{6,7},{7,6},{8,9},{9,8},{10,11... | collective-permute-start | bytes 1966088 | tf_op jit(solution)/shard_map/ppermute | solution.py:62
  3.6 10.3 %collective-permute-start.1 = (f32[5,4,64,128]{3,2,1,0:T(8,128)S(1)}, f32[5,4,64,128]{3,2,1,0:T(8,128)S(1)}, u32[]{:S(2)}, u32[]{:S(2)}) collective-permute-start(f32[5,4,64,128]{3,2,1,0:T(8,128)S(1)} %get-tuple-element.13), channel_id=1, source_target_pairs={{0,7},{1,2},{2,1},{3,4},{4,3},{5,6},{6,5},{7,0},{8,15},{9,10},{10,... | collective-permute-start | bytes 1966088 | tf_op jit(solution)/shard_map/ppermute | solution.py:61
  14.2 10.5 %collective-permute-start.2 = (f32[5,12,8,128]{3,2,1,0:T(8,128)S(1)}, f32[5,12,8,128]{3,2,1,0:T(8,128)S(1)}, u32[]{:S(2)}, u32[]{:S(2)}) collective-permute-start(f32[5,12,8,128]{3,2,1,0:T(8,128)S(1)} %get-tuple-element.15), channel_id=1, source_target_pairs={{0,8},{8,0},{16,24},{24,16},{1,9},{9,1},{17,25},{25,17},{2,10},{10... | collective-permute-start | bytes 737288 | tf_op jit(solution)/shard_map/ppermute | solution.py:62
  16.0 8.7 %collective-permute-start.3 = (f32[5,12,8,128]{3,2,1,0:T(8,128)S(1)}, f32[5,12,8,128]{3,2,1,0:T(8,128)S(1)}, u32[]{:S(2)}, u32[]{:S(2)}) collective-permute-start(f32[5,12,8,128]{3,2,1,0:T(8,128)S(1)} %get-tuple-element.16), channel_id=1, source_target_pairs={{0,24},{8,16},{16,8},{24,0},{1,25},{9,17},{17,9},{25,1},{2,26},{10... | collective-permute-start | bytes 737288 | tf_op jit(solution)/shard_map/ppermute | solution.py:61
  25.3 7.2 %collective-permute-start.4 = (f32[8,72,128]{2,1,0:T(8,128)S(1)}, f32[8,72,128]{2,1,0:T(8,128)S(1)}, u32[]{:S(2)}, u32[]{:S(2)}) collective-permute-start(f32[8,72,128]{2,1,0:T(8,128)S(1)} %get-tuple-element.19), channel_id=1, source_target_pairs={{0,96},{32,0},{64,32},{96,64},{1,97},{33,1},{65,33},{97,65},{2,98}... | collective-permute-start | bytes 884744 | tf_op jit(solution)/shard_map/ppermute | solution.py:68

commit v4 on v3

--- a/solution.py
+++ b/solution.py
@@ -63,13 +63,23 @@
     return first, second
 
 
+def upward():
+    return lax.axis_index("gz") % 2 == 0
+
+
 def pull(face, axis):
-    peers = lax.axis_size(axis)
-    return lax.ppermute(face, axis, [(i, (i - 1) % peers) for i in range(peers)])
-
-
-def last_on(axis):
-    return lax.axis_index(axis) == lax.axis_size(axis) - 1
+    peers, layers = lax.axis_size(axis), lax.axis_size("gz")
+    pairs = []
+    for i in range(peers):
+        for z in range(layers):
+            to = (i - 1 if z % 2 == 0 else i + 1) % peers
+            pairs.append((i * layers + z, to * layers + z))
+    return lax.ppermute(face, (axis, "gz"), pairs)
+
+
+def at_seam(axis):
+    at = lax.axis_index(axis)
+    return at == jnp.where(upward(), lax.axis_size(axis) - 1, 0)
 
 
 def cut(there, value):
@@ -250,59 +260,49 @@
     )(block, kappa)
 
 
-def pack_y_kernel(
-    b_low, b_high, k_low, k_high, f_low, f_high, s_low, s_high, after, edges, to_first, to_second
-):
+def pack_y_kernel(b_low, b_high, k_low, k_high, f_low, f_high, s_low, s_high, after, kept, face):
     nz = k_low.shape[0]
+
+    def lay(a, z, low, high):
+        face[a, z] = jnp.where(upward(), low, high)
+        kept[a, z] = jnp.where(upward(), high, low)
 
     def own(z, carry):
         for a in range(ARRAYS):
-            edges[a, z + DEEP, 0] = b_low[a, z] if a < COLS else k_low[z]
-            edges[a, z + DEEP, 1] = b_high[a, z] if a < COLS else k_high[z]
+            if a < COLS:
+                lay(a, z + DEEP, b_low[a, z], b_high[a, z])
+            else:
+                lay(a, z + DEEP, k_low[z], k_high[z])
         return carry
 
     lax.fori_loop(0, nz, own, 0, unroll=4)
 
     def far(i, carry):
         for a in range(ARRAYS):
-            for at, (one, other) in enumerate(((f_low, s_low), (f_high, s_high))):
-                upper, lower = sides("gz", one[a, i], other[a, i])
-                edges[a, i, at] = lower
-                edges[a, nz + DEEP + i, at] = upper
+            low = sides("gz", f_low[a, i], s_low[a, i])
+            high = sides("gz", f_high[a, i], s_high[a, i])
+            lay(a, nz + DEEP + i, low[0], high[0])
+            lay(a, i, low[1], high[1])
         return carry
 
     lax.fori_loop(0, DEEP, far, 0, unroll=2)
-    half = sublanes(8) < 4
-
-    def pairs(duo, carry):
-        z = duo * 2
-        for a in range(ARRAYS):
-            upper = jnp.where(half, pltpu.roll(edges[a, z, 1], 4, 0), edges[a, z + 1, 1])
-            lower = jnp.where(half, edges[a, z, 0], pltpu.roll(edges[a, z + 1, 0], 4, 0))
-            to_first[a, duo] = even_first("gy", upper, lower)
-            to_second[a, duo] = even_first("gy", lower, upper)
-        return carry
-
-    lax.fori_loop(0, to_first.shape[1], pairs, 0, unroll=4)
 
 
 def pack_y(block, kappa, first, second, after):
     nz, ny, nx = kappa.shape
-    depth = nz + 2 * DEEP
     last = ny // 8 - 1
     whole = lambda shape: pl.BlockSpec(shape, lambda i: (0,) * len(shape))
     b_edge = lambda at: pl.BlockSpec((COLS, nz, 8, nx), lambda i: (0, 0, at, 0))
     k_edge = lambda at: pl.BlockSpec((nz, 8, nx), lambda i: (0, at, 0))
     f_edge = lambda at: pl.BlockSpec((ARRAYS, DEEP, 8, nx), lambda i: (0, 0, at, 0))
-    edges = (ARRAYS, depth, 2, 8, nx)
-    face = (ARRAYS, depth // 2, 8, nx)
+    face = (ARRAYS, nz + 2 * DEEP, 8, nx)
     return pl.pallas_call(
         pack_y_kernel,
         grid=(1,),
-        out_shape=[jax.ShapeDtypeStruct(s, F32) for s in (edges, face, face)],
+        out_shape=[jax.ShapeDtypeStruct(face, F32)] * 2,
         in_specs=[f(at) for f in (b_edge, k_edge, f_edge, f_edge) for at in (0, last)]
         + [pl.BlockSpec(memory_space=pl.ANY)],
-        out_specs=[whole(edges), whole(face), whole(face)],
+        out_specs=[whole(face)] * 2,
         compiler_params=params(16),
         name="pack_y",
     )(block, block, kappa, kappa, first, first, second, second, after)
@@ -462,28 +462,20 @@
 HALVES = [(a, q) for a in range(ARRAYS) for q in range(SLABS)]
 
 
-def pack_x_kernel(first, second, strip, after, rim, side, face):
+def pack_x_kernel(rim, strip, after, side, face):
     depth = rim.shape[1]
     ny = strip.shape[2]
-    half = sublanes(8) < 4
     low = lanes(8) % PITCH < 8
-
-    def duos(duo, carry):
-        for a in range(ARRAYS):
-            upper, lower = sides("gy", first[a, duo], second[a, duo])
-            rim[a, duo * 2] = jnp.where(half, upper, pltpu.roll(lower, 4, 0))
-            rim[a, duo * 2 + 1] = jnp.where(half, pltpu.roll(upper, 4, 0), lower)
-        return carry
-
-    lax.fori_loop(0, depth // 2, duos, 0, unroll=4)
     for a, q in HALVES:
         side[a, q] = strip_of([rim[a, z] for z in range(q, depth, SLABS)])
 
     def pack(at, get):
         for n in range(0, len(HALVES), 2):
-            value = pltpu.roll(get(*HALVES[n]), 120, 1)
+            value = get(*HALVES[n])
+            value = jnp.where(upward(), pltpu.roll(value, 120, 1), value)
             if n + 1 < len(HALVES):
-                value = jnp.where(low, value, get(*HALVES[n + 1]))
+                other = get(*HALVES[n + 1])
+                value = jnp.where(low, value, jnp.where(upward(), other, pltpu.roll(other, 8, 1)))
             face[n // 2, at] = value
 
     def rows(t, carry):
@@ -495,29 +487,30 @@
     pack(slice(ny, ny + 8), lambda a, q: side[a, q])
 
 
-def pack_x(first, second, strip, after):
+def pack_x(rim, strip, after):
     _, _, ny, nx = strip.shape
     face = ((len(HALVES) + 1) // 2, ny + 8, nx)
-    rim = (ARRAYS, 2 * first.shape[1], 8, nx)
     return pl.pallas_call(
         pack_x_kernel,
-        out_shape=[jax.ShapeDtypeStruct(s, F32) for s in (rim, (ARRAYS, SLABS, 8, nx), face)],
-        in_specs=[VMEM] * 3 + [pl.BlockSpec(memory_space=pl.ANY)],
-        out_specs=[VMEM] * 3,
+        out_shape=[jax.ShapeDtypeStruct(s, F32) for s in ((ARRAYS, SLABS, 8, nx), face)],
+        in_specs=[VMEM] * 2 + [pl.BlockSpec(memory_space=pl.ANY)],
+        out_specs=[VMEM] * 2,
         compiler_params=params(16),
         name="pack_x",
-    )(first, second, strip, after)
-
-
-def y_strip_kernel(edges, rim, acc, g0, g1, g2, g3, kr, w, wz):
+    )(rim, strip, after)
+
+
+def y_strip_kernel(kept, rim, acc, g0, g1, g2, g3, kr, w, wz):
     depth = rim.shape[1]
     half = sublanes(8) < 4
+    seam = [at_seam("gy") & (sublanes(8) == 7), at_seam("gy") & (sublanes(8) == 0)]
     acc[...] = jnp.zeros_like(acc)
 
     def fill(z, carry):
         for a in range(ARRAYS):
-            parts = (edges[a, z, 1], rim[a, z], edges[a, z, 0])
-            for t, part in enumerate(parts):
+            below = jnp.where(upward(), kept[a, z], rim[a, z])
+            above = jnp.where(upward(), rim[a, z], kept[a, z])
+            for t, part in enumerate((below, above)):
                 if a < COLS:
                     g0[a, z, tile(t)] = part
                 else:
@@ -527,11 +520,13 @@
     lax.fori_loop(0, depth, fill, 0, unroll=4)
 
     def weights(z, carry):
-        for t in range(3):
+        for t in range(2):
             k = kr[z, tile(t)]
             right, left = pltpu.roll(k, 127, 1), pltpu.roll(k, 1, 1)
-            above = rows_above(kr, (z,), t, 3, k)
+            above = rows_above(kr, (z,), t, 2, k)
             below = rows_below(kr, (z,), t, k)
+            above = cut(seam[0], above) if t == 0 else above
+            below = cut(seam[1], below) if t == 1 else below
             far = kr[z + 1, tile(t)]
             near = kr[jnp.maximum(z - 1, 0), tile(t)]
             w[0, z, tile(t)] = centre(k, (right, left, above, below, far, near))
@@ -549,22 +544,19 @@
         def slab(z, own, k=k, src=src, dst=dst):
             sums = Sums()
             kept = []
-            for t in range(3):
-                if dst is None and t == 1:
-                    continue
+            for t in range(2):
                 ws = tile_weights(w, z, wz, z, z - 1, t)
                 olds, news = [], []
                 for c in range(COLS):
                     v = src[c, z, tile(t)]
-                    above = rows_above(src, (c, z), t, 3, v)
+                    above = rows_above(src, (c, z), t, 2, v)
                     below = rows_below(src, (c, z), t, v)
                     news.append(apply(v, above, below, src[c, z + 1, tile(t)], src[c, z - 1, tile(t)], ws))
                     olds.append(v)
                 if dst is not None:
                     for c in range(COLS):
                         dst[c, z, tile(t)] = news[c]
-                if t != 1:
-                    kept.append((olds, news))
+                kept.append((olds, news))
             if own:
                 olds, news = (
                     [jnp.where(half, b, a) for a, b in zip(kept[0][i], kept[1][i])] for i in range(2)
@@ -582,43 +574,36 @@
             return carry
 
         if k < DEEP:
-            lax.fori_loop(0, DEEP - k, far, 0)
+            lax.fori_loop(0, DEEP - k, far, 0, unroll=True)
         lax.fori_loop(DEEP, depth - DEEP, own, 0, unroll=4)
 
 
-def y_strip(edges, rim):
+def y_strip(kept, rim):
     _, depth, _, nx = rim.shape
     return pl.pallas_call(
         y_strip_kernel,
         out_shape=jax.ShapeDtypeStruct((MOMENTS * NPAIRS, 8, nx), F32),
         in_specs=[VMEM] * 2,
         out_specs=VMEM,
-        scratch_shapes=[pltpu.VMEM((COLS, depth, 24, nx), F32)] * 4
+        scratch_shapes=[pltpu.VMEM((COLS, depth, 16, nx), F32)] * 4
         + [
-            pltpu.VMEM((depth, 24, nx), F32),
-            pltpu.VMEM((4, depth, 24, nx), F32),
-            pltpu.VMEM((depth, 24, nx), F32),
+            pltpu.VMEM((depth, 16, nx), F32),
+            pltpu.VMEM((4, depth, 16, nx), F32),
+            pltpu.VMEM((depth, 16, nx), F32),
         ],
         compiler_params=params(16),
         cost_estimate=cost(1 << 27),
         name="y_strip",
-    )(edges, rim)
+    )(kept, rim)
 
 
 def x_strip_kernel(strip, side, face, acc1, acc2, acc3, out, s0, s1, s2, s3, kr, w, wz, acc):
     tiles = face.shape[1] // 8
     offset = lanes(8) % PITCH
-    right_seam, left_seam = (last_on("gx") & (offset == at) for at in (7, 8))
-
-    def rows(t):
-        return slice(8 + 8 * t, 16 + 8 * t)
-
-    def lay(ref, index, t, value):
-        ref[index + (rows(t),)] = value
-        if t == 0:
-            ref[index + (slice(8 + 8 * tiles, 16 + 8 * tiles),)] = value
-        if t == tiles - 1:
-            ref[index + (slice(0, 8),)] = value
+    half = sublanes(8) < 4
+    right_seam, left_seam = (at_seam("gx") & (offset == at) for at in (7, 8))
+    above_seam, below_seam = (at_seam("gy") & (sublanes(8) == at) for at in (7, 0))
+    shift = jnp.where(upward(), 0, 1)
 
     def next_slab(ref, index, q, at):
         if q < SLABS - 1:
@@ -632,32 +617,38 @@
 
     for n, (a, q) in enumerate(HALVES):
         for t in range(tiles):
-            value = strip[a, q, tile(t)] if t < tiles - 1 else side[a, q]
+            own = strip[a, q, tile(t)] if t < tiles - 1 else side[a, q]
             beyond = face[n // 2, tile(t)]
-            beyond = pltpu.roll(beyond, 8, 1) if n % 2 == 0 else beyond
-            value = jnp.where(offset < 8, value, beyond)
+            if n % 2 == 0:
+                beyond = jnp.where(upward(), pltpu.roll(beyond, 8, 1), beyond)
+            else:
+                beyond = jnp.where(upward(), beyond, pltpu.roll(beyond, 120, 1))
+            value = jnp.where((offset < 8) == upward(), own, beyond)
+            at = t + shift if t < tiles - 1 else (tiles - 1) * (1 - shift)
+            at = pl.ds(pl.multiple_of(at * 8, 8), 8)
             if a < COLS:
-                lay(s0, (a, q), t, value)
+                s0[a, q, at] = value
             else:
-                lay(kr, (q,), t, value)
+                kr[q, at] = value
 
     for q in range(SLABS):
         for t in range(tiles):
-            k = kr[q, rows(t)]
+            k = kr[q, tile(t)]
             right, left = cut(right_seam, pltpu.roll(k, 127, 1)), cut(left_seam, pltpu.roll(k, 1, 1))
-            above = kr[q, 9 + 8 * t : 17 + 8 * t]
-            below = kr[q, 7 + 8 * t : 15 + 8 * t]
-            far, near = next_slab(kr, (), q, rows(t)), last_slab(kr, (), q, rows(t))
-            w[0, q, rows(t)] = centre(k, (right, left, above, below, far, near))
-            w[1, q, rows(t)] = link(k, right, True)
-            w[2, q, rows(t)] = link(k, left, True)
-            above = link(k, above, True)
-            w[3, q, rows(t)] = above
-            if t == tiles - 1:
-                w[3, q, 0:8] = above
-            wz[q + 1, rows(t)] = link(k, far, True)
+            above = rows_above(kr, (q,), t, tiles, k)
+            below = rows_below(kr, (q,), t, k)
+            if t == 0 or t == tiles - 2:
+                above = cut(above_seam & (upward() == (t > 0)), above)
+            if t == 1 or t == tiles - 1:
+                below = cut(below_seam & (upward() == (t > 1)), below)
+            far, near = next_slab(kr, (), q, tile(t)), last_slab(kr, (), q, tile(t))
+            w[0, q, tile(t)] = centre(k, (right, left, above, below, far, near))
+            w[1, q, tile(t)] = link(k, right, True)
+            w[2, q, tile(t)] = link(k, left, True)
+            w[3, q, tile(t)] = link(k, above, True)
+            wz[q + 1, tile(t)] = link(k, far, True)
             if q == 0:
-                wz[0, rows(t)] = link(k, near, True)
+                wz[0, tile(t)] = link(k, near, True)
     acc[...] = jnp.zeros_like(acc)
     fields = (s0, s1, s2, s3, None)
     for k in range(1, BASIS + 1):
@@ -665,20 +656,29 @@
 
         def slab(q):
             sums = Sums()
-            for t in range(tiles if dst is not None else tiles - 1):
-                at, above, below = rows(t), slice(9 + 8 * t, 17 + 8 * t), slice(7 + 8 * t, 15 + 8 * t)
-                ws = [w[i, q, at] for i in range(4)] + [w[3, q, below], wz[q + 1, at], wz[q, at]]
+
+            def step(t):
+                ws = tile_weights(w, q, wz, q + 1, q, t)
                 olds, news = [], []
                 for c in range(COLS):
-                    v = src[c, q, at]
-                    far, near = next_slab(src, (c,), q, at), last_slab(src, (c,), q, at)
-                    news.append(apply(v, src[c, q, above], src[c, q, below], far, near, ws))
+                    v = src[c, q, tile(t)]
+                    above = rows_above(src, (c, q), t, tiles, v)
+                    below = rows_below(src, (c, q), t, v)
+                    far, near = next_slab(src, (c,), q, tile(t)), last_slab(src, (c,), q, tile(t))
+                    news.append(apply(v, above, below, far, near, ws))
                     olds.append(v)
                 if dst is not None:
                     for c in range(COLS):
-                        lay(dst, (c, q), t, news[c])
-                if t < tiles - 1:
-                    sums.products(k, olds, news)
+                        dst[c, q, tile(t)] = news[c]
+                return olds, news
+
+            first, last = step(0), step(tiles - 1)
+            olds, news = (
+                [jnp.where(half, b, a) for a, b in zip(first[i], last[i])] for i in range(2)
+            )
+            sums.products(k, olds, news)
+            for t in range(1, tiles - 1):
+                sums.products(k, *step(t))
             sums.flush(acc.at[q])
 
         for q in range(SLABS):
@@ -707,7 +707,7 @@
 
 def x_strip(strip, side, face, accs, peers):
     _, slabs, ny, nx = strip.shape
-    laid = (slabs, ny + 24, nx)
+    laid = (slabs, ny + 8, nx)
     return pl.pallas_call(
         x_strip_kernel,
         out_shape=jax.ShapeDtypeStruct((peers, 1, 128), F32),
@@ -820,13 +820,13 @@
     far = [pltpu.with_memory_space_constraint(value, pltpu.HBM) for value in (block, kappa)]
     first, second = swap(*pack_z(*far), "gz")
     acc1, edge = inner(block, kappa)
-    edges, y_first, y_second = pack_y(block, kappa, first, second, acc1)
-    y_first, y_second = swap(y_first, y_second, "gy")
+    kept, face = pack_y(block, kappa, first, second, acc1)
+    rim = pull(face, "gy")
     strip = strips(block, kappa, first, second)
     acc2 = outer(block, kappa, edge, first, second)
-    rim, side, face = pack_x(y_first, y_second, strip, acc2)
+    side, face = pack_x(rim, strip, acc2)
     face = pull(face, "gx")
-    acc3 = y_strip(edges, rim)
+    acc3 = y_strip(kept, rim)
     moments = x_strip(strip, side, face, (acc1, acc2, acc3), peers)
     parts = lax.all_to_all(moments, axes, 0, 0, tiled=True)
     return tuple(finish(parts, block, ncells))

time: 59 us -> 57 us (0.966)
  waiting for transfers between devices: 2.26 us -> 5.83 us
  starting transfers between devices: 9.43 us -> 5.93 us
  blocking collectives: 21.5 us -> 20 us
  Pallas kernels: 24.9 us -> 24.3 us
    ppermute x1 -> x2, waiting for transfers between devices: 0.01 us -> 3.65 us  [pull(): return lax.ppermute(face, (axis, 'gz'), pairs)]
    ppermute x2 -> x1, starting transfers between devices: 3.6 us -> 1.36 us  [swap(): second = lax.ppermute(second, axis, other)]
    ppermute x2 -> x1, starting transfers between devices: 3.3 us -> 1.5 us  [swap(): first = lax.ppermute(first, axis, [(i, i ^ 1) for i in range(peers)])]
    all_to_all x1, blocking collectives: 21.5 us -> 20 us  [shards(): parts = lax.all_to_all(moments, axes, 0, 0, tiled=True)]
    pallas_call x1, Pallas kernels: 4.68 us -> 3.77 us  [y_strip(): pl.pallas_call(y_strip_kernel, out_shape=jax.ShapeDtypeStruct((MOMENTS *...]
    ppermute x1 -> x2, starting transfers between devices: 2.53 us -> 3.07 us  [pull(): return lax.ppermute(face, (axis, 'gz'), pairs)]
    ppermute x2 -> x1, waiting for transfers between devices: 2.25 us -> 2.18 us  [swap(): second = lax.ppermute(second, axis, other)]
  transfers between devices with their start and end apart: 5 -> 4, of which waited for: 1 -> 3; matrix products, arithmetic and copies ran while one was open for 0% -> 0% of each run, Pallas kernels for 30% -> 30%
where the time goes in v4:
time: 57 us; the launch traced here: 56.8 us
  Pallas kernels  24.3 us (43%)
  blocking collectives  20 us (35%)
  starting transfers between devices  5.93 us (10%)
  waiting for transfers between devices  5.83 us (10%)
  between operations  0.71 us (1%)
    all_to_all x1, blocking collectives, shards(): parts = lax.all_to_all(moments, axes, 0, 0, tiled=True)  20 us
    pallas_call x1, Pallas kernels, inner(): pl.pallas_call(inner_kernel, out_shape=[jax.ShapeDtypeStruct((MOMENTS * N...  6.75 us
    pallas_call x1, Pallas kernels, outer(): pl.pallas_call(outer_kernel, out_shape=jax.ShapeDtypeStruct((MOMENTS * NP...  4.88 us
    pallas_call x1, Pallas kernels, y_strip(): pl.pallas_call(y_strip_kernel, out_shape=jax.ShapeDtypeStruct((MOMENTS *...  3.77 us
    ppermute x2, waiting for transfers between devices, pull(): return lax.ppermute(face, (axis, 'gz'), pairs)  3.65 us
    ppermute x2, starting transfers between devices, pull(): return lax.ppermute(face, (axis, 'gz'), pairs)  3.07 us
    pallas_call x1, Pallas kernels, x_strip(): pl.pallas_call(x_strip_kernel, out_shape=jax.ShapeDtypeStruct((peers, 1,...  2.64 us
    pallas_call x1, Pallas kernels, finish(): pl.pallas_call(lambda *refs: finish_kernel(ncells, *refs), grid=(steps,),...  2.47 us
  transfers between devices with their start and end apart: 4, of which 3 were waited for; matrix products, arithmetic and copies ran while one was open for 0% of the time, Pallas kernels for 30%

profile of v4, /device:TPU:1, one launch (start us, length us, event | category | flops | bytes accessed | tf_op | source)
XLA Modules:
  0.0 56.8 jit_solution(13366186278401850265)
XLA Ops:
  0.6 0.0 copy-start
  0.6 0.0 copy-start.1
  0.6 1.5 %pack_z.1 = (f32[5,4,64,128]{3,2,1,0:T(8,128)S(1)}, f32[5,4,64,128]{3,2,1,0:T(8,128)S(1)}) custom-call(f32[4,16,64,128]{3,2,1,0:T(8,128)} %refs_1_.1, f32[16,64,128]{2,1,0:T(8,128)} %kappa.7), custom_call_target="tpu_custom_call" | custom-call | tf_op jit(solution)/shard_map/pack_z/pallas_call | solution.py:174
  2.1 1.5 %collective-permute-start = (f32[5,4,64,128]{3,2,1,0:T(8,128)S(1)}, f32[5,4,64,128]{3,2,1,0:T(8,128)S(1)}, u32[]{:S(2)}, u32[]{:S(2)}) collective-permute-start(f32[5,4,64,128]{3,2,1,0:T(8,128)S(1)} %get-tuple-element.10), channel_id=1, source_target_pairs={{0,1},{1,0},{2,3},{3,2},{4,5},{5,4},{6,7},{7,6},{8,9},{9,8},{10,11... | collective-permute-start | bytes 1966088 | tf_op jit(solution)/shard_map/ppermute | solution.py:62
  3.6 1.4 %collective-permute-start.1 = (f32[5,4,64,128]{3,2,1,0:T(8,128)S(1)}, f32[5,4,64,128]{3,2,1,0:T(8,128)S(1)}, u32[]{:S(2)}, u32[]{:S(2)}) collective-permute-start(f32[5,4,64,128]{3,2,1,0:T(8,128)S(1)} %get-tuple-element.11), channel_id=1, source_target_pairs={{0,7},{1,2},{2,1},{3,4},{4,3},{5,6},{6,5},{7,0},{8,15},{9,10},{10,... | collective-permute-start | bytes 1966088 | tf_op jit(solution)/shard_map/ppermute | solution.py:61
  5.0 0.0 copy-done
  5.0 0.0 copy-done.1
  5.0 6.7 %inner.1 = (f32[90,8,128]{2,1,0:T(8,128)S(1)}, f32[3,2,2,4,64,128]{5,4,3,2,1,0:T(8,128)S(1)}) custom-call(f32[4,16,64,128]{3,2,1,0:T(8,128)S(1)} %copy-done, f32[16,64,128]{2,1,0:T(8,128)S(1)} %copy-done.1), custom_call_target="tpu_custom_call" | custom-call | flops 268435456 | bytes 1048576 | tf_op jit(solution)/shard_map/inner/pallas_call | solution.py:247
  11.7 0.0 collective-permute-done.first.f_low.f_high
  11.7 2.2 %collective-permute-done.1.second.s_low.s_high = f32[5,4,64,128]{3,2,1,0:T(8,128)S(1)} collective-permute-done((f32[5,4,64,128]{3,2,1,0:T(8,128)S(1)}, f32[5,4,64,128]{3,2,1,0:T(8,128)S(1)}, u32[]{:S(2)}, u32[]{:S(2)}) %collective-permute-start.1) | collective-permute-done | bytes 655392 | tf_op jit(solution)/shard_map/ppermute | solution.py:61
  13.9 0.2 pack_y.1
  14.2 1.8 %collective-permute-start.2 = (f32[5,24,8,128]{3,2,1,0:T(8,128)S(1)}, f32[5,24,8,128]{3,2,1,0:T(8,128)S(1)}, u32[]{:S(2)}, u32[]{:S(2)}) collective-permute-start(f32[5,24,8,128]{3,2,1,0:T(8,128)S(1)} %get-tuple-element.13), channel_id=1, source_target_pairs={{0,24},{1,9},{2,26},{3,11},{4,28},{5,13},{6,30},{7,15},{8,0},{9,17... | collective-permute-start | bytes 1474568 | tf_op jit(solution)/shard_map/ppermute | solution.py:77
  16.0 1.6 %strips.1.strip = f32[5,3,64,128]{3,2,1,0:T(8,128)S(1)} custom-call(f32[4,16,64,128]{3,2,1,0:T(8,128)S(1)} %copy-done, f32[16,64,128]{2,1,0:T(8,128)S(1)} %copy-done.1, f32[5,4,64,128]{3,2,1,0:T(8,128)S(1)} %collective-permute-done.first.f_low.f_high, f32[5,4,64,128]{3,2,1,0:T(8,128)S(1)} %collective-permute-done.1.second.s_low.s_high), custom_call_target="tpu_custom_call" | custom-call | flops 33554432 | bytes 1048576 | tf_op jit(solution)/shard_map/strips/pallas_call | solution.py:451
  17.5 4.9 %outer.1.after.acc2 = f32[90,8,128]{2,1,0:T(8,128)S(1)} custom-call(f32[4,16,64,128]{3,2,1,0:T(8,128)S(1)} %copy-done, f32[16,64,128]{2,1,0:T(8,128)S(1)} %copy-done.1, f32[3,2,2,4,64,128]{5,4,3,2,1,0:T(8,128)S(1)} %get-tuple-element.14.edge, f32[5,4,64,128]{3,2,1,0:T(8,128)S(1)} %collective-permute-done.first.f_low.f_high, ...), custom_call_target="tpu_custom_call" | custom-call | flops 134217728 | bytes 1048576 | tf_op jit(solution)/shard_map/outer/pallas_call | solution.py:400
  22.4 1.9 %collective-permute-done.2.rim = f32[5,24,8,128]{3,2,1,0:T(8,128)S(1)} collective-permute-done((f32[5,24,8,128]{3,2,1,0:T(8,128)S(1)}, f32[5,24,8,128]{3,2,1,0:T(8,128)S(1)}, u32[]{:S(2)}, u32[]{:S(2)}) %collective-permute-start.2) | collective-permute-done | bytes 491552 | tf_op jit(solution)/shard_map/ppermute | solution.py:77
  24.3 0.5 pack_x.1
  24.8 1.3 %collective-permute-start.3 = (f32[8,72,128]{2,1,0:T(8,128)S(1)}, f32[8,72,128]{2,1,0:T(8,128)S(1)}, u32[]{:S(2)}, u32[]{:S(2)}) collective-permute-start(f32[8,72,128]{2,1,0:T(8,128)S(1)} %get-tuple-element.16), channel_id=1, source_target_pairs={{0,96},{1,33},{2,98},{3,35},{4,100},{5,37},{6,102},{7,39},{32,0},{... | collective-permute-start | bytes 884744 | tf_op jit(solution)/shard_map/ppermute | solution.py:77
  26.1 3.8 %y_strip.1.acc3 = f32[90,8,128]{2,1,0:T(8,128)S(1)} custom-call(f32[5,24,8,128]{3,2,1,0:T(8,128)S(1)} %get-tuple-element.17.kept, f32[5,24,8,128]{3,2,1,0:T(8,128)S(1)} %collective-permute-done.2.rim), custom_call_target="tpu_custom_call" | custom-call | flops 134217728 | bytes 1048576 | tf_op jit(solution)/shard_map/y_strip/pallas_call | solution.py:583
  29.9 1.8 %collective-permute-done.3.face = f32[8,72,128]{2,1,0:T(8,128)S(1)} collective-permute-done((f32[8,72,128]{2,1,0:T(8,128)S(1)}, f32[8,72,128]{2,1,0:T(8,128)S(1)}, u32[]{:S(2)}, u32[]{:S(2)}) %collective-permute-start.3) | collective-permute-done | bytes 294944 | tf_op jit(solution)/shard_map/ppermute | solution.py:77
  31.7 2.6 %x_strip.1 = f32[128,1,128]{2,1,0:T(1,128)S(1)} custom-call(f32[5,3,64,128]{3,2,1,0:T(8,128)S(1)} %strips.1.strip, f32[5,3,8,128]{3,2,1,0:T(8,128)S(1)} %get-tuple-element.15.side, f32[8,72,128]{2,1,0:T(8,128)S(1)} %collective-permute-done.3.face, f32[90,8,128]{2,1,0:T(8,128)S(1)} %get-tuple-element.12.after.acc1, f32[90,8,128]{2,1,0:T(8,128)S(1)} %outer.1.after.acc2, ...), custom_call_target="tpu_custom_call" | custom-call | tf_op jit(solution)/shard_map/x_strip/pallas_call | solution.py:711
  34.3 20.0 %all_to_all.5.refs_0_ = f32[128,1,128]{2,1,0:T(1,128)S(1)} all-to-all(f32[128,1,128]{2,1,0:T(1,128)S(1)} %x_strip.1), channel_id=1, replica_groups=mesh['gx'=4,'gy'=4,'gz'=8] {'gx','gy','gz'}, dimensions={0} | all-to-all | bytes 131072 | tf_op jit(solution)/shard_map/all_to_all | solution.py:831
  54.4 2.5 %finish.1 = (f32[4,16,64,128]{3,2,1,0:T(8,128)}, f32[20,20]{1,0:T(8,128)}) custom-call(f32[128,1,128]{2,1,0:T(1,128)S(1)} %all_to_all.5.refs_0_, f32[4,16,64,128]{3,2,1,0:T(8,128)S(1)} %copy-done), custom_call_target="tpu_custom_call" | custom-call | tf_op jit(solution)/shard_map/finish/pallas_call | solution.py:801
Async XLA Ops:
  0.6 4.3 %copy-start = (f32[4,16,64,128]{3,2,1,0:T(8,128)S(1)}, f32[4,16,64,128]{3,2,1,0:T(8,128)}, u32[]{:S(2)}) copy-start(f32[4,16,64,128]{3,2,1,0:T(8,128)} %refs_1_.1) | copy-start | bytes 6291460
  0.6 4.3 %copy-start.1 = (f32[16,64,128]{2,1,0:T(8,128)S(1)}, f32[16,64,128]{2,1,0:T(8,128)}, u32[]{:S(2)}) copy-start(f32[16,64,128]{2,1,0:T(8,128)} %kappa.7) | copy-start | bytes 1572868
  2.1 9.6 %collective-permute-start = (f32[5,4,64,128]{3,2,1,0:T(8,128)S(1)}, f32[5,4,64,128]{3,2,1,0:T(8,128)S(1)}, u32[]{:S(2)}, u32[]{:S(2)}) collective-permute-start(f32[5,4,64,128]{3,2,1,0:T(8,128)S(1)} %get-tuple-element.10), channel_id=1, source_target_pairs={{0,1},{1,0},{2,3},{3,2},{4,5},{5,4},{6,7},{7,6},{8,9},{9,8},{10,11... | collective-permute-start | bytes 1966088 | tf_op jit(solution)/shard_map/ppermute | solution.py:62
  3.6 10.3 %collective-permute-start.1 = (f32[5,4,64,128]{3,2,1,0:T(8,128)S(1)}, f32[5,4,64,128]{3,2,1,0:T(8,128)S(1)}, u32[]{:S(2)}, u32[]{:S(2)}) collective-permute-start(f32[5,4,64,128]{3,2,1,0:T(8,128)S(1)} %get-tuple-element.11), channel_id=1, source_target_pairs={{0,7},{1,2},{2,1},{3,4},{4,3},{5,6},{6,5},{7,0},{8,15},{9,10},{10,... | collective-permute-start | bytes 1966088 | tf_op jit(solution)/shard_map/ppermute | solution.py:61
  14.2 10.1 %collective-permute-start.2 = (f32[5,24,8,128]{3,2,1,0:T(8,128)S(1)}, f32[5,24,8,128]{3,2,1,0:T(8,128)S(1)}, u32[]{:S(2)}, u32[]{:S(2)}) collective-permute-start(f32[5,24,8,128]{3,2,1,0:T(8,128)S(1)} %get-tuple-element.13), channel_id=1, source_target_pairs={{0,24},{1,9},{2,26},{3,11},{4,28},{5,13},{6,30},{7,15},{8,0},{9,17... | collective-permute-start | bytes 1474568 | tf_op jit(solution)/shard_map/ppermute | solution.py:77
  24.8 6.9 %collective-permute-start.3 = (f32[8,72,128]{2,1,0:T(8,128)S(1)}, f32[8,72,128]{2,1,0:T(8,128)S(1)}, u32[]{:S(2)}, u32[]{:S(2)}) collective-permute-start(f32[8,72,128]{2,1,0:T(8,128)S(1)} %get-tuple-element.16), channel_id=1, source_target_pairs={{0,96},{1,33},{2,98},{3,35},{4,100},{5,37},{6,102},{7,39},{32,0},{... | collective-permute-start | bytes 884744 | tf_op jit(solution)/shard_map/ppermute | solution.py:77

commit v5 on v4

--- a/solution.py
+++ b/solution.py
@@ -1,5 +1,6 @@
 import jax
 import jax.numpy as jnp
+import numpy as np
 from jax import lax
 from jax.experimental import pallas as pl
 from jax.experimental.pallas import tpu as pltpu
@@ -67,14 +68,14 @@
     return lax.axis_index("gz") % 2 == 0
 
 
-def pull(face, axis):
-    peers, layers = lax.axis_size(axis), lax.axis_size("gz")
+def pull(face, *axes):
+    sizes = [lax.axis_size(axis) for axis in axes] + [lax.axis_size("gz")]
     pairs = []
-    for i in range(peers):
-        for z in range(layers):
-            to = (i - 1 if z % 2 == 0 else i + 1) % peers
-            pairs.append((i * layers + z, to * layers + z))
-    return lax.ppermute(face, (axis, "gz"), pairs)
+    for at in np.ndindex(*sizes):
+        step = -1 if at[-1] % 2 == 0 else 1
+        to = [(i + step) % size for i, size in zip(at[:-1], sizes)] + [at[-1]]
+        pairs.append(tuple(int(np.ravel_multi_index(place, sizes)) for place in (at, to)))
+    return lax.ppermute(face, (*axes, "gz"), pairs)
 
 
 def at_seam(axis):
@@ -203,7 +204,7 @@
             wz[z, tile(t)] = link(k, far, False)
         return carry
 
-    lax.fori_loop(0, nz - 1, weights, 0, unroll=3)
+    lax.fori_loop(0, nz - 1, weights, 0, unroll=5)
     fields = (block, p1, p2, p3, None)
     for k in range(1, BASIS + 1):
         src, dst = fields[k - 1], fields[k]
@@ -235,7 +236,7 @@
             sums.flush(acc)
             return carry
 
-        lax.fori_loop(k, nz - k, slab, 0, unroll=2)
+        lax.fori_loop(k, nz - k, slab, 0, unroll=(nz - 2 * k + 1) // 2)
         if dst is not None:
             for i in range(2):
                 edge[k - 1, 0, i] = dst[:, k + i]
@@ -260,55 +261,179 @@
     )(block, kappa)
 
 
-def pack_y_kernel(b_low, b_high, k_low, k_high, f_low, f_high, s_low, s_high, after, kept, face):
-    nz = k_low.shape[0]
-
-    def lay(a, z, low, high):
-        face[a, z] = jnp.where(upward(), low, high)
-        kept[a, z] = jnp.where(upward(), high, low)
-
-    def own(z, carry):
+def strip_of(planes):
+    lane = lanes(8)
+    offset, group = lane % PITCH, lane // PITCH
+    index = jnp.where(offset < 8, 120 + offset, offset - 8)
+    strip = None
+    for g, plane in enumerate(planes):
+        if plane is not None:
+            value = permute_lanes(plane, index)
+            strip = value if strip is None else jnp.where(group == g, value, strip)
+    return strip
+
+
+def pack_halves(one, other):
+    value = jnp.where(upward(), pltpu.roll(one, 120, 1), one)
+    if other is None:
+        return value
+    low = lanes(8) % PITCH < 8
+    return jnp.where(low, value, jnp.where(upward(), other, pltpu.roll(other, 8, 1)))
+
+
+HALVES = [(a, q) for a in range(ARRAYS) for q in range(SLABS)]
+DUOS = [HALVES[n : n + 2] for n in range(0, len(HALVES), 2)]
+FAR = 2 * DEEP
+
+
+def pack_duo(duo, get):
+    return pack_halves(get(*duo[0]), get(*duo[1]) if len(duo) > 1 else None)
+
+
+def faces_kernel(block, kappa, strip, x_face, y_face, y_kept):
+    nz, ny, _ = kappa.shape
+
+    def rows(t, carry):
+        at = pl.ds(pl.multiple_of(t * 8, 8), 8)
+
+        def plane(a, z):
+            if z < 0 or z >= nz:
+                return None
+            return block[a, z, at] if a < COLS else kappa[z, at]
+
+        held = {}
+        for a, q in HALVES:
+            held[a, q] = strip_of([plane(a, z - DEEP) for z in range(q, nz + FAR, SLABS)])
+            strip[a, q, at] = held[a, q]
+        for n, duo in enumerate(DUOS):
+            x_face[n, at] = pack_duo(duo, lambda a, q: held[a, q])
+        return carry
+
+    lax.fori_loop(0, ny // 8, rows, 0, unroll=2)
+
+    def slabs(z, carry):
         for a in range(ARRAYS):
-            if a < COLS:
-                lay(a, z + DEEP, b_low[a, z], b_high[a, z])
-            else:
-                lay(a, z + DEEP, k_low[z], k_high[z])
-        return carry
-
-    lax.fori_loop(0, nz, own, 0, unroll=4)
-
-    def far(i, carry):
+            low, high = (block[a, z, at] if a < COLS else kappa[z, at] for at in (slice(0, 8), slice(ny - 8, ny)))
+            y_face[a, z] = jnp.where(upward(), low, high)
+            y_kept[a, z] = jnp.where(upward(), high, low)
+        return carry
+
+    lax.fori_loop(0, nz, slabs, 0, unroll=4)
+
+
+def faces(block, kappa):
+    nz, ny, nx = kappa.shape
+    shapes = ((ARRAYS, SLABS, ny, nx), (len(DUOS), ny, nx), (ARRAYS, nz, 8, nx), (ARRAYS, nz, 8, nx))
+    return pl.pallas_call(
+        faces_kernel,
+        out_shape=[jax.ShapeDtypeStruct(shape, F32) for shape in shapes],
+        in_specs=[VMEM] * 2,
+        out_specs=[VMEM] * 4,
+        compiler_params=params(16),
+        cost_estimate=cost(1 << 24),
+        name="faces",
+    )(block, kappa)
+
+
+def far_y_kernel(f_low, f_high, s_low, s_high, after, face, kept):
+    def slabs(i, carry):
         for a in range(ARRAYS):
             low = sides("gz", f_low[a, i], s_low[a, i])
             high = sides("gz", f_high[a, i], s_high[a, i])
-            lay(a, nz + DEEP + i, low[0], high[0])
-            lay(a, i, low[1], high[1])
-        return carry
-
-    lax.fori_loop(0, DEEP, far, 0, unroll=2)
-
-
-def pack_y(block, kappa, first, second, after):
-    nz, ny, nx = kappa.shape
+            for at, which in ((i, 1), (DEEP + i, 0)):
+                face[a, at] = jnp.where(upward(), low[which], high[which])
+                kept[a, at] = jnp.where(upward(), high[which], low[which])
+        return carry
+
+    lax.fori_loop(0, DEEP, slabs, 0, unroll=2)
+
+
+def far_y(first, second, after):
+    _, _, ny, nx = first.shape
     last = ny // 8 - 1
     whole = lambda shape: pl.BlockSpec(shape, lambda i: (0,) * len(shape))
-    b_edge = lambda at: pl.BlockSpec((COLS, nz, 8, nx), lambda i: (0, 0, at, 0))
-    k_edge = lambda at: pl.BlockSpec((nz, 8, nx), lambda i: (0, at, 0))
-    f_edge = lambda at: pl.BlockSpec((ARRAYS, DEEP, 8, nx), lambda i: (0, 0, at, 0))
-    face = (ARRAYS, nz + 2 * DEEP, 8, nx)
+    edge = lambda at: pl.BlockSpec((ARRAYS, DEEP, 8, nx), lambda i: (0, 0, at, 0))
+    shape = (ARRAYS, FAR, 8, nx)
     return pl.pallas_call(
-        pack_y_kernel,
+        far_y_kernel,
         grid=(1,),
-        out_shape=[jax.ShapeDtypeStruct(face, F32)] * 2,
-        in_specs=[f(at) for f in (b_edge, k_edge, f_edge, f_edge) for at in (0, last)]
-        + [pl.BlockSpec(memory_space=pl.ANY)],
-        out_specs=[whole(face)] * 2,
+        out_shape=[jax.ShapeDtypeStruct(shape, F32)] * 2,
+        in_specs=[edge(0), edge(last), edge(0), edge(last), pl.BlockSpec(memory_space=pl.ANY)],
+        out_specs=[whole(shape)] * 2,
         compiler_params=params(16),
-        name="pack_y",
-    )(block, block, kappa, kappa, first, first, second, second, after)
-
-
-def outer_kernel(block, kappa, edge, first, second, acc, f0, f1, f2, f3, kz, w, wz):
+        name="far_y",
+    )(first, first, second, second, after)
+
+
+def far_strips_kernel(first, second, after, strip):
+    def rows(t, carry):
+        at = pl.ds(pl.multiple_of(t * 8, 8), 8)
+        for a in range(ARRAYS):
+            uppers, lowers = zip(*[sides("gz", first[a, i, at], second[a, i, at]) for i in range(DEEP)])
+            strip[a, at] = strip_of(lowers + uppers)
+        return carry
+
+    lax.fori_loop(0, strip.shape[1] // 8, rows, 0, unroll=2)
+
+
+def far_strips(first, second, after):
+    _, _, ny, nx = first.shape
+    return pl.pallas_call(
+        far_strips_kernel,
+        out_shape=jax.ShapeDtypeStruct((ARRAYS, ny, nx), F32),
+        in_specs=[VMEM] * 2 + [pl.BlockSpec(memory_space=pl.ANY)],
+        out_specs=VMEM,
+        compiler_params=params(16),
+        cost_estimate=cost(1 << 23),
+        name="far_strips",
+    )(first, second, after)
+
+
+def far_pairs():
+    return [(n, n + 1 if n + 1 < ARRAYS else None) for n in range(0, ARRAYS, 2)]
+
+
+def pack_x_kernel(own_face, rim, far_strip, side, face, corner):
+    nz = rim.shape[1]
+    tiles = far_strip.shape[1] // 8
+
+    def plane(a, z):
+        return rim[a, z] if 0 <= z < nz else None
+
+    def far_tile(a, t):
+        return None if a is None else far_strip[a, tile(t)]
+
+    for n in range(len(DUOS)):
+        for t in range(tiles):
+            face[n * tiles + t] = own_face[n, tile(t)]
+    at = len(DUOS) * tiles
+    for n, (one, other) in enumerate(far_pairs()):
+        packed = [pack_halves(far_tile(one, t), far_tile(other, t)) for t in range(tiles)]
+        for t in range(tiles):
+            face[at + n * tiles + t] = packed[t]
+        corner[n] = jnp.where(upward(), packed[0], packed[tiles - 1])
+    at += len(far_pairs()) * tiles
+    for a, q in HALVES:
+        side[a, q] = strip_of([plane(a, z - DEEP) for z in range(q, nz + FAR, SLABS)])
+    for n, duo in enumerate(DUOS):
+        face[at + n] = pack_duo(duo, lambda a, q: side[a, q])
+
+
+def pack_x(own_face, rim, far_strip):
+    _, ny, nx = far_strip.shape
+    count = (len(DUOS) + len(far_pairs())) * ny // 8 + len(DUOS)
+    shapes = ((ARRAYS, SLABS, 8, nx), (count, 8, nx), (len(far_pairs()), 8, nx))
+    return pl.pallas_call(
+        pack_x_kernel,
+        out_shape=[jax.ShapeDtypeStruct(shape, F32) for shape in shapes],
+        in_specs=[VMEM] * 3,
+        out_specs=[VMEM] * 3,
+        compiler_params=params(16),
+        name="pack_x",
+    )(own_face, rim, far_strip)
+
+
+def outer_kernel(block, kappa, edge, first, second, after, acc, f0, f1, f2, f3, kz, w, wz):
     nz, ny, _ = kappa.shape
     tiles = ny // 8
     half = sublanes(8) < 4
@@ -353,7 +478,7 @@
             wz[at, tile(t)] = link(k, far, True)
         return carry
 
-    lax.fori_loop(0, 16, weights, 0, unroll=2)
+    lax.fori_loop(0, 16, weights, 0, unroll=4)
     fields = (f0, f1, f2, f3, None)
     for k in range(1, BASIS + 1):
         src, dst = fields[k - 1], fields[k]
@@ -395,12 +520,12 @@
         lax.fori_loop(0, 2, both, 0)
 
 
-def outer(block, kappa, edge, first, second):
+def outer(block, kappa, edge, first, second, after):
     nz, ny, nx = kappa.shape
     return pl.pallas_call(
         outer_kernel,
         out_shape=jax.ShapeDtypeStruct((MOMENTS * NPAIRS, 8, nx), F32),
-        in_specs=[VMEM] * 5,
+        in_specs=[VMEM] * 5 + [pl.BlockSpec(memory_space=pl.ANY)],
         out_specs=VMEM,
         scratch_shapes=[pltpu.VMEM((2, COLS, DEEP + 2, ny, nx), F32)] * 4
         + [
@@ -411,113 +536,37 @@
         compiler_params=params(24),
         cost_estimate=cost(1 << 27),
         name="outer",
-    )(block, kappa, edge, first, second)
-
-
-def strip_of(planes):
-    lane = lanes(8)
-    offset, group = lane % PITCH, lane // PITCH
-    index = jnp.where(offset < 8, 120 + offset, offset - 8)
-    strip = permute_lanes(planes[0], index)
-    for g, plane in enumerate(planes[1:]):
-        strip = jnp.where(group == g + 1, permute_lanes(plane, index), strip)
-    return strip
-
-
-def strips_kernel(block, kappa, first, second, strip):
-    nz, ny, _ = kappa.shape
-
-    def rows(t, carry):
-        at = pl.ds(pl.multiple_of(t * 8, 8), 8)
-        for a in range(ARRAYS):
-            ends = [sides("gz", first[a, i, at], second[a, i, at]) for i in range(DEEP)]
-
-            def plane(z):
-                if z < DEEP:
-                    return ends[z][1]
-                if z >= nz + DEEP:
-                    return ends[z - nz - DEEP][0]
-                return block[a, z - DEEP, at] if a < COLS else kappa[z - DEEP, at]
-
-            for q in range(SLABS):
-                strip[a, q, at] = strip_of([plane(z) for z in range(q, nz + 2 * DEEP, SLABS)])
-        return carry
-
-    lax.fori_loop(0, ny // 8, rows, 0)
-
-
-def strips(block, kappa, first, second):
-    nz, ny, nx = kappa.shape
-    return pl.pallas_call(
-        strips_kernel,
-        out_shape=jax.ShapeDtypeStruct((ARRAYS, SLABS, ny, nx), F32),
-        in_specs=[VMEM] * 4,
-        out_specs=VMEM,
-        compiler_params=params(16),
-        cost_estimate=cost(1 << 25),
-        name="strips",
-    )(block, kappa, first, second)
-
-
-HALVES = [(a, q) for a in range(ARRAYS) for q in range(SLABS)]
-
-
-def pack_x_kernel(rim, strip, after, side, face):
-    depth = rim.shape[1]
-    ny = strip.shape[2]
-    low = lanes(8) % PITCH < 8
-    for a, q in HALVES:
-        side[a, q] = strip_of([rim[a, z] for z in range(q, depth, SLABS)])
-
-    def pack(at, get):
-        for n in range(0, len(HALVES), 2):
-            value = get(*HALVES[n])
-            value = jnp.where(upward(), pltpu.roll(value, 120, 1), value)
-            if n + 1 < len(HALVES):
-                other = get(*HALVES[n + 1])
-                value = jnp.where(low, value, jnp.where(upward(), other, pltpu.roll(other, 8, 1)))
-            face[n // 2, at] = value
-
-    def rows(t, carry):
-        at = pl.ds(pl.multiple_of(t * 8, 8), 8)
-        pack(at, lambda a, q: strip[a, q, at])
-        return carry
-
-    lax.fori_loop(0, ny // 8, rows, 0, unroll=4)
-    pack(slice(ny, ny + 8), lambda a, q: side[a, q])
-
-
-def pack_x(rim, strip, after):
-    _, _, ny, nx = strip.shape
-    face = ((len(HALVES) + 1) // 2, ny + 8, nx)
-    return pl.pallas_call(
-        pack_x_kernel,
-        out_shape=[jax.ShapeDtypeStruct(s, F32) for s in ((ARRAYS, SLABS, 8, nx), face)],
-        in_specs=[VMEM] * 2 + [pl.BlockSpec(memory_space=pl.ANY)],
-        out_specs=[VMEM] * 2,
-        compiler_params=params(16),
-        name="pack_x",
-    )(rim, strip, after)
-
-
-def y_strip_kernel(kept, rim, acc, g0, g1, g2, g3, kr, w, wz):
-    depth = rim.shape[1]
+    )(block, kappa, edge, first, second, after)
+
+
+def y_strip_kernel(kept, far_kept, rim, far_rim, acc, g0, g1, g2, g3, kr, w, wz):
+    nz = rim.shape[1]
+    depth = nz + FAR
     half = sublanes(8) < 4
     seam = [at_seam("gy") & (sublanes(8) == 7), at_seam("gy") & (sublanes(8) == 0)]
     acc[...] = jnp.zeros_like(acc)
 
-    def fill(z, carry):
+    def lay(z, kept, rim, at):
         for a in range(ARRAYS):
-            below = jnp.where(upward(), kept[a, z], rim[a, z])
-            above = jnp.where(upward(), rim[a, z], kept[a, z])
+            below = jnp.where(upward(), kept[a, at], rim[a, at])
+            above = jnp.where(upward(), rim[a, at], kept[a, at])
             for t, part in enumerate((below, above)):
                 if a < COLS:
                     g0[a, z, tile(t)] = part
                 else:
                     kr[z, tile(t)] = part
-        return carry
-
-    lax.fori_loop(0, depth, fill, 0, unroll=4)
+
+    def fill(z, carry):
+        lay(z + DEEP, kept, rim, z)
+        return carry
+
+    def fill_far(i, carry):
+        lay(i, far_kept, far_rim, i)
+        lay(nz + DEEP + i, far_kept, far_rim, DEEP + i)
+        return carry
+
+    lax.fori_loop(0, nz, fill, 0, unroll=4)
+    lax.fori_loop(0, DEEP, fill_far, 0, unroll=2)
 
     def weights(z, carry):
         for t in range(2):
@@ -575,15 +624,16 @@
 
         if k < DEEP:
             lax.fori_loop(0, DEEP - k, far, 0, unroll=True)
-        lax.fori_loop(DEEP, depth - DEEP, own, 0, unroll=4)
-
-
-def y_strip(kept, rim):
-    _, depth, _, nx = rim.shape
+        lax.fori_loop(DEEP, depth - DEEP, own, 0, unroll=16)
+
+
+def y_strip(kept, far_kept, rim, far_rim):
+    _, nz, _, nx = rim.shape
+    depth = nz + FAR
     return pl.pallas_call(
         y_strip_kernel,
         out_shape=jax.ShapeDtypeStruct((MOMENTS * NPAIRS, 8, nx), F32),
-        in_specs=[VMEM] * 2,
+        in_specs=[VMEM] * 4,
         out_specs=VMEM,
         scratch_shapes=[pltpu.VMEM((COLS, depth, 16, nx), F32)] * 4
         + [
@@ -594,12 +644,13 @@
         compiler_params=params(16),
         cost_estimate=cost(1 << 27),
         name="y_strip",
-    )(kept, rim)
-
-
-def x_strip_kernel(strip, side, face, acc1, acc2, acc3, out, s0, s1, s2, s3, kr, w, wz, acc):
-    tiles = face.shape[1] // 8
-    offset = lanes(8) % PITCH
+    )(kept, far_kept, rim, far_rim)
+
+
+def x_strip_kernel(strip, side, far_strip, far_rim, face, corner, acc1, acc2, acc3, out, s0, s1, s2, s3, kr, w, wz, acc):
+    tiles = strip.shape[2] // 8 + 1
+    lane = lanes(8)
+    offset = lane % PITCH
     half = sublanes(8) < 4
     right_seam, left_seam = (at_seam("gx") & (offset == at) for at in (7, 8))
     above_seam, below_seam = (at_seam("gy") & (sublanes(8) == at) for at in (7, 0))
@@ -615,15 +666,27 @@
             return ref[index + (q - 1, at)]
         return pltpu.roll(ref[index + (SLABS - 1, at)], PITCH, 1)
 
+    own_side = (offset < 8) == upward()
+    depth = 128 // PITCH * SLABS
+    far_at = len(DUOS) * (tiles - 1)
+    rim_at = far_at + len(far_pairs()) * (tiles - 1)
+    far_side = [strip_of([far_rim[a, i] for i in range(FAR)]) for a in range(ARRAYS)]
     for n, (a, q) in enumerate(HALVES):
+        z = lane // PITCH * SLABS + q
+        far = (z < DEEP) | (z >= depth - DEEP)
+        index = jnp.where(z < DEEP, z, jnp.where(far, z - (depth - FAR), 0)) * PITCH
         for t in range(tiles):
             own = strip[a, q, tile(t)] if t < tiles - 1 else side[a, q]
-            beyond = face[n // 2, tile(t)]
+            beyond = face[n // 2 * (tiles - 1) + t] if t < tiles - 1 else face[rim_at + n // 2]
             if n % 2 == 0:
                 beyond = jnp.where(upward(), pltpu.roll(beyond, 8, 1), beyond)
             else:
                 beyond = jnp.where(upward(), beyond, pltpu.roll(beyond, 120, 1))
-            value = jnp.where((offset < 8) == upward(), own, beyond)
+            far_own = far_strip[a, tile(t)] if t < tiles - 1 else far_side[a]
+            far_beyond = face[far_at + a // 2 * (tiles - 1) + t] if t < tiles - 1 else corner[a // 2]
+            far_own = permute_lanes(far_own, index + offset)
+            far_beyond = permute_lanes(far_beyond, index + offset % 8 + 8 * (a % 2))
+            value = jnp.where(own_side, jnp.where(far, far_own, own), jnp.where(far, far_beyond, beyond))
             at = t + shift if t < tiles - 1 else (tiles - 1) * (1 - shift)
             at = pl.ds(pl.multiple_of(at * 8, 8), 8)
             if a < COLS:
@@ -705,13 +768,13 @@
     out[...] = jnp.broadcast_to(row[0:1][None], out.shape)
 
 
-def x_strip(strip, side, face, accs, peers):
+def x_strip(strip, side, far_strip, far_rim, face, corner, accs, peers):
     _, slabs, ny, nx = strip.shape
     laid = (slabs, ny + 8, nx)
     return pl.pallas_call(
         x_strip_kernel,
         out_shape=jax.ShapeDtypeStruct((peers, 1, 128), F32),
-        in_specs=[VMEM] * 6,
+        in_specs=[VMEM] * 9,
         out_specs=VMEM,
         scratch_shapes=[pltpu.VMEM((COLS,) + laid, F32)] * 4
         + [
@@ -722,7 +785,7 @@
         ],
         compiler_params=params(16),
         name="x_strip",
-    )(strip, side, face, *accs)
+    )(strip, side, far_strip, far_rim, face, corner, *accs)
 
 
 def factor(row, triangle, coef):
@@ -819,15 +882,18 @@
     ncells = float(kappa.size * peers)
     far = [pltpu.with_memory_space_constraint(value, pltpu.HBM) for value in (block, kappa)]
     first, second = swap(*pack_z(*far), "gz")
+    strip, x_face, y_face, y_kept = faces(block, kappa)
+    rim = pull(y_face, "gy")
     acc1, edge = inner(block, kappa)
-    kept, face = pack_y(block, kappa, first, second, acc1)
-    rim = pull(face, "gy")
-    strip = strips(block, kappa, first, second)
-    acc2 = outer(block, kappa, edge, first, second)
-    side, face = pack_x(rim, strip, acc2)
-    face = pull(face, "gx")
-    acc3 = y_strip(kept, rim)
-    moments = x_strip(strip, side, face, (acc1, acc2, acc3), peers)
+    far_face, far_kept = far_y(first, second, acc1)
+    far_rim = pull(far_face, "gy")
+    far_strip = far_strips(first, second, far_kept)
+    side, x_face, corner = pack_x(x_face, rim, far_strip)
+    x_face, corner = pull(x_face, "gx"), pull(corner, "gx", "gy")
+    acc2 = outer(block, kappa, edge, first, second, side)
+    acc3 = y_strip(y_kept, far_kept, rim, far_rim)
+    accs = (acc1, acc2, acc3)
+    moments = x_strip(strip, side, far_strip, far_rim, x_face, corner, accs, peers)
     parts = lax.all_to_all(moments, axes, 0, 0, tiled=True)
     return tuple(finish(parts, block, ncells))
 

time: 57 us -> 51.3 us (0.90)
  waiting for transfers between devices: 5.83 us -> 0.02 us
  starting transfers between devices: 5.93 us -> 9.74 us
  blocking collectives: 20 us -> 17.3 us
  Pallas kernels: 24.3 us -> 23.4 us
    ppermute x2 -> x4, starting transfers between devices: 3.07 us -> 6.88 us  [pull(): return lax.ppermute(face, (*axes, 'gz'), pairs)]
    ppermute x2 -> x4, waiting for transfers between devices: 3.65 us -> 0.01 us  [pull(): return lax.ppermute(face, (*axes, 'gz'), pairs)]
    all_to_all x1, blocking collectives: 20 us -> 17.3 us  [shards(): parts = lax.all_to_all(moments, axes, 0, 0, tiled=True)]
    ppermute x1, waiting for transfers between devices: 2.18 us -> 0.01 us  [swap(): second = lax.ppermute(second, axis, other)]
    pallas_call x1, Pallas kernels: 3.77 us -> 3.04 us  [y_strip(): pl.pallas_call(y_strip_kernel, out_shape=jax.ShapeDtypeStruct((MOMENTS *...]
    pallas_call x1, Pallas kernels: 6.75 us -> 6.11 us  [inner(): pl.pallas_call(inner_kernel, out_shape=[jax.ShapeDtypeStruct((MOMENTS * N...]
    pallas_call x3 -> x4, Pallas kernels: 2.35 us -> 2.62 us  [the longest x1 1.61 us: faces(): pl.pallas_call(faces_kernel, out_shape=[jax.ShapeDtypeStruct(shape, F32)...]
  transfers between devices with their start and end apart: 4 -> 6, of which waited for: 3 -> 0; matrix products, arithmetic and copies ran while one was open for 0% -> 0% of each run, Pallas kernels for 30% -> 31%
where the time goes in v5:
time: 51.3 us; the launch traced here: 51.2 us
  Pallas kernels  23.4 us (46%)
  blocking collectives  17.3 us (34%)
  starting transfers between devices  9.74 us (19%)
  between operations  0.76 us (1%)
    all_to_all x1, blocking collectives, shards(): parts = lax.all_to_all(moments, axes, 0, 0, tiled=True)  17.3 us
    ppermute x4, starting transfers between devices, pull(): return lax.ppermute(face, (*axes, 'gz'), pairs)  6.88 us
    pallas_call x1, Pallas kernels, inner(): pl.pallas_call(inner_kernel, out_shape=[jax.ShapeDtypeStruct((MOMENTS * N...  6.11 us
    pallas_call x1, Pallas kernels, outer(): pl.pallas_call(outer_kernel, out_shape=jax.ShapeDtypeStruct((MOMENTS * NP...  4.59 us
    pallas_call x1, Pallas kernels, x_strip(): pl.pallas_call(x_strip_kernel, out_shape=jax.ShapeDtypeStruct((peers, 1,...  3.16 us
    pallas_call x1, Pallas kernels, y_strip(): pl.pallas_call(y_strip_kernel, out_shape=jax.ShapeDtypeStruct((MOMENTS *...  3.04 us
    pallas_call x1, Pallas kernels, finish(): pl.pallas_call(lambda *refs: finish_kernel(ncells, *refs), grid=(steps,),...  2.47 us
    pallas_call x1, Pallas kernels, faces(): pl.pallas_call(faces_kernel, out_shape=[jax.ShapeDtypeStruct(shape, F32)...  1.61 us
  transfers between devices with their start and end apart: 6, of which 0 were waited for; matrix products, arithmetic and copies ran while one was open for 0% of the time, Pallas kernels for 31%

profile of v5, /device:TPU:1, one launch (start us, length us, event | category | flops | bytes accessed | tf_op | source)
XLA Modules:
  0.0 51.2 jit_solution(3353744327930563749)
XLA Ops:
  0.6 0.0 copy-start
  0.6 0.0 copy-start.1
  0.6 1.5 %pack_z.1 = (f32[5,4,64,128]{3,2,1,0:T(8,128)S(1)}, f32[5,4,64,128]{3,2,1,0:T(8,128)S(1)}) custom-call(f32[4,16,64,128]{3,2,1,0:T(8,128)} %refs_1_.1, f32[16,64,128]{2,1,0:T(8,128)} %kappa.7), custom_call_target="tpu_custom_call" | custom-call | tf_op jit(solution)/shard_map/pack_z/pallas_call | solution.py:175
  2.1 1.5 %collective-permute-start.1 = (f32[5,4,64,128]{3,2,1,0:T(8,128)S(1)}, f32[5,4,64,128]{3,2,1,0:T(8,128)S(1)}, u32[]{:S(2)}, u32[]{:S(2)}) collective-permute-start(f32[5,4,64,128]{3,2,1,0:T(8,128)S(1)} %get-tuple-element.18), channel_id=1, source_target_pairs={{0,1},{1,0},{2,3},{3,2},{4,5},{5,4},{6,7},{7,6},{8,9},{9,8},{10,11... | collective-permute-start | bytes 1966088 | tf_op jit(solution)/shard_map/ppermute | solution.py:63
  3.6 1.4 %collective-permute-start.2 = (f32[5,4,64,128]{3,2,1,0:T(8,128)S(1)}, f32[5,4,64,128]{3,2,1,0:T(8,128)S(1)}, u32[]{:S(2)}, u32[]{:S(2)}) collective-permute-start(f32[5,4,64,128]{3,2,1,0:T(8,128)S(1)} %get-tuple-element.19), channel_id=1, source_target_pairs={{0,7},{1,2},{2,1},{3,4},{4,3},{5,6},{6,5},{7,0},{8,15},{9,10},{10,... | collective-permute-start | bytes 1966088 | tf_op jit(solution)/shard_map/ppermute | solution.py:62
  5.0 0.0 copy-done
  5.0 0.0 copy-done.1
  5.0 1.6 %faces.1 = (f32[5,3,64,128]{3,2,1,0:T(8,128)S(1)}, f32[8,64,128]{2,1,0:T(8,128)S(1)}, f32[5,16,8,128]{3,2,1,0:T(8,128)S(1)}, f32[5,16,8,128]{3,2,1,0:T(8,128)S(1)}) custom-call(f32[4,16,64,128]{3,2,1,0:T(8,128)S(1)} %copy-done, f32[16,64,128]{2,1,0:T(8,128)S(1)} %copy-done.1), custom_call_target="tpu_custom_call" | custom-call | flops 16777216 | bytes 1048576 | tf_op jit(solution)/shard_map/faces/pallas_call | solution.py:327
  6.6 1.7 %collective-permute-start = (f32[5,16,8,128]{3,2,1,0:T(8,128)S(1)}, f32[5,16,8,128]{3,2,1,0:T(8,128)S(1)}, u32[]{:S(2)}, u32[]{:S(2)}) collective-permute-start(f32[5,16,8,128]{3,2,1,0:T(8,128)S(1)} %get-tuple-element.17), channel_id=1, source_target_pairs={{0,24},{1,9},{2,26},{3,11},{4,28},{5,13},{6,30},{7,15},{8,0},{9,17... | collective-permute-start | bytes 983048 | tf_op jit(solution)/shard_map/ppermute | solution.py:78
  8.3 6.1 %inner.1 = (f32[90,8,128]{2,1,0:T(8,128)S(1)}, f32[3,2,2,4,64,128]{5,4,3,2,1,0:T(8,128)S(1)}) custom-call(f32[4,16,64,128]{3,2,1,0:T(8,128)S(1)} %copy-done, f32[16,64,128]{2,1,0:T(8,128)S(1)} %copy-done.1), custom_call_target="tpu_custom_call" | custom-call | flops 268435456 | bytes 1048576 | tf_op jit(solution)/shard_map/inner/pallas_call | solution.py:248
  14.4 0.0 collective-permute-done.1.f_low.f_high.first
  14.4 0.0 collective-permute-done.2.s_low.s_high.second
  14.4 0.1 far_y.1
  14.5 0.7 %far_strips.1.far_strip = f32[5,64,128]{2,1,0:T(8,128)S(1)} custom-call(f32[5,4,64,128]{3,2,1,0:T(8,128)S(1)} %collective-permute-done.1.f_low.f_high.first, f32[5,4,64,128]{3,2,1,0:T(8,128)S(1)} %collective-permute-done.2.s_low.s_high.second, f32[5,8,8,128]{3,2,1,0:T(8,128)S(1)} %get-tuple-element.21.after.far_kept), custom_call_target="tpu_custom_call" | custom-call | flops 8388608 | bytes 1048576 | tf_op jit(solution)/shard_map/far_strips/pallas_call | solution.py:381
  15.2 0.0 collective-permute-done.rim
  15.2 0.3 pack_x.1
  15.5 1.3 %collective-permute-start.4 = (f32[96,8,128]{2,1,0:T(8,128)S(1)}, f32[96,8,128]{2,1,0:T(8,128)S(1)}, u32[]{:S(2)}, u32[]{:S(2)}) collective-permute-start(f32[96,8,128]{2,1,0:T(8,128)S(1)} %get-tuple-element.24), channel_id=1, source_target_pairs={{0,96},{1,33},{2,98},{3,35},{4,100},{5,37},{6,102},{7,39},{32,0},{... | collective-permute-start | bytes 1179656 | tf_op jit(solution)/shard_map/ppermute | solution.py:78
  16.7 1.6 %collective-permute-start.3 = (f32[5,8,8,128]{3,2,1,0:T(8,128)S(1)}, f32[5,8,8,128]{3,2,1,0:T(8,128)S(1)}, u32[]{:S(2)}, u32[]{:S(2)}) collective-permute-start(f32[5,8,8,128]{3,2,1,0:T(8,128)S(1)} %get-tuple-element.23), channel_id=1, source_target_pairs={{0,24},{1,9},{2,26},{3,11},{4,28},{5,13},{6,30},{7,15},{8,0},{9,17... | collective-permute-start | bytes 491528 | tf_op jit(solution)/shard_map/ppermute | solution.py:78
  18.4 2.3 %collective-permute-start.5 = (f32[3,8,128]{2,1,0:T(8,128)S(1)}, f32[3,8,128]{2,1,0:T(8,128)S(1)}, u32[]{:S(2)}, u32[]{:S(2)}) collective-permute-start(f32[3,8,128]{2,1,0:T(8,128)S(1)} %get-tuple-element.25), channel_id=1, source_target_pairs={{0,120},{1,41},{2,122},{3,43},{4,124},{5,45},{6,126},{7,47},{8,96}... | collective-permute-start | bytes 36872 | tf_op jit(solution)/shard_map/ppermute | solution.py:78
  20.6 4.6 %outer.1.acc2 = f32[90,8,128]{2,1,0:T(8,128)S(1)} custom-call(f32[4,16,64,128]{3,2,1,0:T(8,128)S(1)} %copy-done, f32[16,64,128]{2,1,0:T(8,128)S(1)} %copy-done.1, f32[3,2,2,4,64,128]{5,4,3,2,1,0:T(8,128)S(1)} %get-tuple-element.26.edge, f32[5,4,64,128]{3,2,1,0:T(8,128)S(1)} %collective-permute-done.1.f_low.f_high.first, ...), custom_call_target="tpu_custom_call" | custom-call | flops 134217728 | bytes 1048576 | tf_op jit(solution)/shard_map/outer/pallas_call | solution.py:525
  25.2 0.0 collective-permute-done.3.far_rim
  25.3 3.0 %y_strip.1.acc3 = f32[90,8,128]{2,1,0:T(8,128)S(1)} custom-call(f32[5,16,8,128]{3,2,1,0:T(8,128)S(1)} %get-tuple-element.27.kept, f32[5,8,8,128]{3,2,1,0:T(8,128)S(1)} %get-tuple-element.21.after.far_kept, f32[5,16,8,128]{3,2,1,0:T(8,128)S(1)} %collective-permute-done.rim, f32[5,8,8,128]{3,2,1,0:T(8,128)S(1)} %collective-permute-done.3.far_rim), custom_call_target="tpu_custom_call" | custom-call | flops 134217728 | bytes 1048576 | tf_op jit(solution)/shard_map/y_strip/pallas_call | solution.py:633
  28.3 0.0 collective-permute-done.5.corner
  28.3 0.0 collective-permute-done.4.face
  28.3 3.2 %x_strip.1 = f32[128,1,128]{2,1,0:T(1,128)S(1)} custom-call(f32[5,3,64,128]{3,2,1,0:T(8,128)S(1)} %get-tuple-element.15.strip, f32[5,3,8,128]{3,2,1,0:T(8,128)S(1)} %get-tuple-element.22.after.side, f32[5,64,128]{2,1,0:T(8,128)S(1)} %far_strips.1.far_strip, f32[5,8,8,128]{3,2,1,0:T(8,128)S(1)} %collective-permute-done.3.far_rim, ...), custom_call_target="tpu_custom_call" | custom-call | tf_op jit(solution)/shard_map/x_strip/pallas_call | solution.py:774
  31.5 17.3 %all_to_all.5.refs_0_ = f32[128,1,128]{2,1,0:T(1,128)S(1)} all-to-all(f32[128,1,128]{2,1,0:T(1,128)S(1)} %x_strip.1), channel_id=1, replica_groups=mesh['gx'=4,'gy'=4,'gz'=8] {'gx','gy','gz'}, dimensions={0} | all-to-all | bytes 131072 | tf_op jit(solution)/shard_map/all_to_all | solution.py:897
  48.7 2.5 %finish.1 = (f32[4,16,64,128]{3,2,1,0:T(8,128)}, f32[20,20]{1,0:T(8,128)}) custom-call(f32[128,1,128]{2,1,0:T(1,128)S(1)} %all_to_all.5.refs_0_, f32[4,16,64,128]{3,2,1,0:T(8,128)S(1)} %copy-done), custom_call_target="tpu_custom_call" | custom-call | tf_op jit(solution)/shard_map/finish/pallas_call | solution.py:864
Async XLA Ops:
  0.6 4.3 %copy-start = (f32[4,16,64,128]{3,2,1,0:T(8,128)S(1)}, f32[4,16,64,128]{3,2,1,0:T(8,128)}, u32[]{:S(2)}) copy-start(f32[4,16,64,128]{3,2,1,0:T(8,128)} %refs_1_.1) | copy-start | bytes 6291460
  0.6 4.3 %copy-start.1 = (f32[16,64,128]{2,1,0:T(8,128)S(1)}, f32[16,64,128]{2,1,0:T(8,128)}, u32[]{:S(2)}) copy-start(f32[16,64,128]{2,1,0:T(8,128)} %kappa.7) | copy-start | bytes 1572868
  2.1 12.3 %collective-permute-start.1 = (f32[5,4,64,128]{3,2,1,0:T(8,128)S(1)}, f32[5,4,64,128]{3,2,1,0:T(8,128)S(1)}, u32[]{:S(2)}, u32[]{:S(2)}) collective-permute-start(f32[5,4,64,128]{3,2,1,0:T(8,128)S(1)} %get-tuple-element.18), channel_id=1, source_target_pairs={{0,1},{1,0},{2,3},{3,2},{4,5},{5,4},{6,7},{7,6},{8,9},{9,8},{10,11... | collective-permute-start | bytes 1966088 | tf_op jit(solution)/shard_map/ppermute | solution.py:63
  3.6 10.8 %collective-permute-start.2 = (f32[5,4,64,128]{3,2,1,0:T(8,128)S(1)}, f32[5,4,64,128]{3,2,1,0:T(8,128)S(1)}, u32[]{:S(2)}, u32[]{:S(2)}) collective-permute-start(f32[5,4,64,128]{3,2,1,0:T(8,128)S(1)} %get-tuple-element.19), channel_id=1, source_target_pairs={{0,7},{1,2},{2,1},{3,4},{4,3},{5,6},{6,5},{7,0},{8,15},{9,10},{10,... | collective-permute-start | bytes 1966088 | tf_op jit(solution)/shard_map/ppermute | solution.py:62
  6.6 8.6 %collective-permute-start = (f32[5,16,8,128]{3,2,1,0:T(8,128)S(1)}, f32[5,16,8,128]{3,2,1,0:T(8,128)S(1)}, u32[]{:S(2)}, u32[]{:S(2)}) collective-permute-start(f32[5,16,8,128]{3,2,1,0:T(8,128)S(1)} %get-tuple-element.17), channel_id=1, source_target_pairs={{0,24},{1,9},{2,26},{3,11},{4,28},{5,13},{6,30},{7,15},{8,0},{9,17... | collective-permute-start | bytes 983048 | tf_op jit(solution)/shard_map/ppermute | solution.py:78
  15.5 12.8 %collective-permute-start.4 = (f32[96,8,128]{2,1,0:T(8,128)S(1)}, f32[96,8,128]{2,1,0:T(8,128)S(1)}, u32[]{:S(2)}, u32[]{:S(2)}) collective-permute-start(f32[96,8,128]{2,1,0:T(8,128)S(1)} %get-tuple-element.24), channel_id=1, source_target_pairs={{0,96},{1,33},{2,98},{3,35},{4,100},{5,37},{6,102},{7,39},{32,0},{... | collective-permute-start | bytes 1179656 | tf_op jit(solution)/shard_map/ppermute | solution.py:78
  16.7 8.5 %collective-permute-start.3 = (f32[5,8,8,128]{3,2,1,0:T(8,128)S(1)}, f32[5,8,8,128]{3,2,1,0:T(8,128)S(1)}, u32[]{:S(2)}, u32[]{:S(2)}) collective-permute-start(f32[5,8,8,128]{3,2,1,0:T(8,128)S(1)} %get-tuple-element.23), channel_id=1, source_target_pairs={{0,24},{1,9},{2,26},{3,11},{4,28},{5,13},{6,30},{7,15},{8,0},{9,17... | collective-permute-start | bytes 491528 | tf_op jit(solution)/shard_map/ppermute | solution.py:78
  18.4 9.9 %collective-permute-start.5 = (f32[3,8,128]{2,1,0:T(8,128)S(1)}, f32[3,8,128]{2,1,0:T(8,128)S(1)}, u32[]{:S(2)}, u32[]{:S(2)}) collective-permute-start(f32[3,8,128]{2,1,0:T(8,128)S(1)} %get-tuple-element.25), channel_id=1, source_target_pairs={{0,120},{1,41},{2,122},{3,43},{4,124},{5,45},{6,126},{7,47},{8,96}... | collective-permute-start | bytes 36872 | tf_op jit(solution)/shard_map/ppermute | solution.py:78

commit v6 on v5

--- a/solution.py
+++ b/solution.py
@@ -642,7 +642,7 @@
             pltpu.VMEM((depth, 16, nx), F32),
         ],
         compiler_params=params(16),
-        cost_estimate=cost(1 << 27),
+        cost_estimate=cost(1 << 30),
         name="y_strip",
     )(kept, far_kept, rim, far_rim)
 
@@ -859,7 +859,7 @@
 
 def finish(parts, block, ncells):
     cols, nz, ny, nx = block.shape
-    steps = 4
+    steps = 2
     piece = pl.BlockSpec((cols, nz // steps, ny, nx), lambda i: (0, i, 0, 0))
     return pl.pallas_call(
         lambda *refs: finish_kernel(ncells, *refs),

time: 51.3 us -> 50.9 us (level)
  transfers between devices with their start and end apart: 6 -> 6, of which waited for: 0 -> 0; matrix products, arithmetic and copies ran while one was open for 0% -> 0% of each run, Pallas kernels for 31% -> 32%
where the time goes in v6:
time: 50.9 us; the launch traced here: 50.8 us
  Pallas kernels  23 us (45%)
  blocking collectives  17.3 us (34%)
  starting transfers between devices  9.74 us (19%)
  between operations  0.76 us (1%)
    all_to_all x1, blocking collectives, shards(): parts = lax.all_to_all(moments, axes, 0, 0, tiled=True)  17.3 us
    ppermute x4, starting transfers between devices, pull(): return lax.ppermute(face, (*axes, 'gz'), pairs)  6.88 us
    pallas_call x1, Pallas kernels, inner(): pl.pallas_call(inner_kernel, out_shape=[jax.ShapeDtypeStruct((MOMENTS * N...  6.11 us
    pallas_call x1, Pallas kernels, outer(): pl.pallas_call(outer_kernel, out_shape=jax.ShapeDtypeStruct((MOMENTS * NP...  4.59 us
    pallas_call x1, Pallas kernels, x_strip(): pl.pallas_call(x_strip_kernel, out_shape=jax.ShapeDtypeStruct((peers, 1,...  3.15 us
    pallas_call x1, Pallas kernels, y_strip(): pl.pallas_call(y_strip_kernel, out_shape=jax.ShapeDtypeStruct((MOMENTS *...  3.04 us
    pallas_call x1, Pallas kernels, finish(): pl.pallas_call(lambda *refs: finish_kernel(ncells, *refs), grid=(steps,),...  2.03 us
    pallas_call x1, Pallas kernels, faces(): pl.pallas_call(faces_kernel, out_shape=[jax.ShapeDtypeStruct(shape, F32)...  1.61 us
  transfers between devices with their start and end apart: 6, of which 0 were waited for; matrix products, arithmetic and copies ran while one was open for 0% of the time, Pallas kernels for 32%

profile of v6, /device:TPU:1, one launch (start us, length us, event | category | flops | bytes accessed | tf_op | source)
XLA Modules:
  0.0 50.8 jit_solution(247713790950663873)
XLA Ops:
  0.6 0.0 copy-start
  0.6 0.0 copy-start.1
  0.6 1.5 %pack_z.1 = (f32[5,4,64,128]{3,2,1,0:T(8,128)S(1)}, f32[5,4,64,128]{3,2,1,0:T(8,128)S(1)}) custom-call(f32[4,16,64,128]{3,2,1,0:T(8,128)} %refs_1_.1, f32[16,64,128]{2,1,0:T(8,128)} %kappa.7), custom_call_target="tpu_custom_call" | custom-call | tf_op jit(solution)/shard_map/pack_z/pallas_call | solution.py:175
  2.1 1.5 %collective-permute-start.1 = (f32[5,4,64,128]{3,2,1,0:T(8,128)S(1)}, f32[5,4,64,128]{3,2,1,0:T(8,128)S(1)}, u32[]{:S(2)}, u32[]{:S(2)}) collective-permute-start(f32[5,4,64,128]{3,2,1,0:T(8,128)S(1)} %get-tuple-element.18), channel_id=1, source_target_pairs={{0,1},{1,0},{2,3},{3,2},{4,5},{5,4},{6,7},{7,6},{8,9},{9,8},{10,11... | collective-permute-start | bytes 1966088 | tf_op jit(solution)/shard_map/ppermute | solution.py:63
  3.6 1.4 %collective-permute-start.2 = (f32[5,4,64,128]{3,2,1,0:T(8,128)S(1)}, f32[5,4,64,128]{3,2,1,0:T(8,128)S(1)}, u32[]{:S(2)}, u32[]{:S(2)}) collective-permute-start(f32[5,4,64,128]{3,2,1,0:T(8,128)S(1)} %get-tuple-element.19), channel_id=1, source_target_pairs={{0,7},{1,2},{2,1},{3,4},{4,3},{5,6},{6,5},{7,0},{8,15},{9,10},{10,... | collective-permute-start | bytes 1966088 | tf_op jit(solution)/shard_map/ppermute | solution.py:62
  5.0 0.0 copy-done
  5.0 0.0 copy-done.1
  5.0 1.6 %faces.1 = (f32[5,3,64,128]{3,2,1,0:T(8,128)S(1)}, f32[8,64,128]{2,1,0:T(8,128)S(1)}, f32[5,16,8,128]{3,2,1,0:T(8,128)S(1)}, f32[5,16,8,128]{3,2,1,0:T(8,128)S(1)}) custom-call(f32[4,16,64,128]{3,2,1,0:T(8,128)S(1)} %copy-done, f32[16,64,128]{2,1,0:T(8,128)S(1)} %copy-done.1), custom_call_target="tpu_custom_call" | custom-call | flops 16777216 | bytes 1048576 | tf_op jit(solution)/shard_map/faces/pallas_call | solution.py:327
  6.6 1.7 %collective-permute-start = (f32[5,16,8,128]{3,2,1,0:T(8,128)S(1)}, f32[5,16,8,128]{3,2,1,0:T(8,128)S(1)}, u32[]{:S(2)}, u32[]{:S(2)}) collective-permute-start(f32[5,16,8,128]{3,2,1,0:T(8,128)S(1)} %get-tuple-element.17), channel_id=1, source_target_pairs={{0,24},{1,9},{2,26},{3,11},{4,28},{5,13},{6,30},{7,15},{8,0},{9,17... | collective-permute-start | bytes 983048 | tf_op jit(solution)/shard_map/ppermute | solution.py:78
  8.3 6.1 %inner.1 = (f32[90,8,128]{2,1,0:T(8,128)S(1)}, f32[3,2,2,4,64,128]{5,4,3,2,1,0:T(8,128)S(1)}) custom-call(f32[4,16,64,128]{3,2,1,0:T(8,128)S(1)} %copy-done, f32[16,64,128]{2,1,0:T(8,128)S(1)} %copy-done.1), custom_call_target="tpu_custom_call" | custom-call | flops 268435456 | bytes 1048576 | tf_op jit(solution)/shard_map/inner/pallas_call | solution.py:248
  14.4 0.0 collective-permute-done.1.f_low.f_high.first
  14.4 0.0 collective-permute-done.2.s_low.s_high.second
  14.4 0.1 far_y.1
  14.5 0.7 %far_strips.1.far_strip = f32[5,64,128]{2,1,0:T(8,128)S(1)} custom-call(f32[5,4,64,128]{3,2,1,0:T(8,128)S(1)} %collective-permute-done.1.f_low.f_high.first, f32[5,4,64,128]{3,2,1,0:T(8,128)S(1)} %collective-permute-done.2.s_low.s_high.second, f32[5,8,8,128]{3,2,1,0:T(8,128)S(1)} %get-tuple-element.21.after.far_kept), custom_call_target="tpu_custom_call" | custom-call | flops 8388608 | bytes 1048576 | tf_op jit(solution)/shard_map/far_strips/pallas_call | solution.py:381
  15.2 0.0 collective-permute-done.rim
  15.2 0.3 pack_x.1
  15.5 1.3 %collective-permute-start.4 = (f32[96,8,128]{2,1,0:T(8,128)S(1)}, f32[96,8,128]{2,1,0:T(8,128)S(1)}, u32[]{:S(2)}, u32[]{:S(2)}) collective-permute-start(f32[96,8,128]{2,1,0:T(8,128)S(1)} %get-tuple-element.24), channel_id=1, source_target_pairs={{0,96},{1,33},{2,98},{3,35},{4,100},{5,37},{6,102},{7,39},{32,0},{... | collective-permute-start | bytes 1179656 | tf_op jit(solution)/shard_map/ppermute | solution.py:78
  16.7 1.6 %collective-permute-start.3 = (f32[5,8,8,128]{3,2,1,0:T(8,128)S(1)}, f32[5,8,8,128]{3,2,1,0:T(8,128)S(1)}, u32[]{:S(2)}, u32[]{:S(2)}) collective-permute-start(f32[5,8,8,128]{3,2,1,0:T(8,128)S(1)} %get-tuple-element.23), channel_id=1, source_target_pairs={{0,24},{1,9},{2,26},{3,11},{4,28},{5,13},{6,30},{7,15},{8,0},{9,17... | collective-permute-start | bytes 491528 | tf_op jit(solution)/shard_map/ppermute | solution.py:78
  18.4 2.3 %collective-permute-start.5 = (f32[3,8,128]{2,1,0:T(8,128)S(1)}, f32[3,8,128]{2,1,0:T(8,128)S(1)}, u32[]{:S(2)}, u32[]{:S(2)}) collective-permute-start(f32[3,8,128]{2,1,0:T(8,128)S(1)} %get-tuple-element.25), channel_id=1, source_target_pairs={{0,120},{1,41},{2,122},{3,43},{4,124},{5,45},{6,126},{7,47},{8,96}... | collective-permute-start | bytes 36872 | tf_op jit(solution)/shard_map/ppermute | solution.py:78
  20.6 4.6 %outer.1.acc2 = f32[90,8,128]{2,1,0:T(8,128)S(1)} custom-call(f32[4,16,64,128]{3,2,1,0:T(8,128)S(1)} %copy-done, f32[16,64,128]{2,1,0:T(8,128)S(1)} %copy-done.1, f32[3,2,2,4,64,128]{5,4,3,2,1,0:T(8,128)S(1)} %get-tuple-element.26.edge, f32[5,4,64,128]{3,2,1,0:T(8,128)S(1)} %collective-permute-done.1.f_low.f_high.first, ...), custom_call_target="tpu_custom_call" | custom-call | flops 134217728 | bytes 1048576 | tf_op jit(solution)/shard_map/outer/pallas_call | solution.py:525
  25.2 0.0 collective-permute-done.3.far_rim
  25.3 3.0 %y_strip.1.acc3 = f32[90,8,128]{2,1,0:T(8,128)S(1)} custom-call(f32[5,16,8,128]{3,2,1,0:T(8,128)S(1)} %get-tuple-element.27.kept, f32[5,8,8,128]{3,2,1,0:T(8,128)S(1)} %get-tuple-element.21.after.far_kept, f32[5,16,8,128]{3,2,1,0:T(8,128)S(1)} %collective-permute-done.rim, f32[5,8,8,128]{3,2,1,0:T(8,128)S(1)} %collective-permute-done.3.far_rim), custom_call_target="tpu_custom_call" | custom-call | flops 1073741824 | bytes 1048576 | tf_op jit(solution)/shard_map/y_strip/pallas_call | solution.py:633
  28.3 0.0 collective-permute-done.5.corner
  28.3 0.0 collective-permute-done.4.face
  28.3 3.1 %x_strip.1 = f32[128,1,128]{2,1,0:T(1,128)S(1)} custom-call(f32[5,3,64,128]{3,2,1,0:T(8,128)S(1)} %get-tuple-element.15.strip, f32[5,3,8,128]{3,2,1,0:T(8,128)S(1)} %get-tuple-element.22.after.side, f32[5,64,128]{2,1,0:T(8,128)S(1)} %far_strips.1.far_strip, f32[5,8,8,128]{3,2,1,0:T(8,128)S(1)} %collective-permute-done.3.far_rim, ...), custom_call_target="tpu_custom_call" | custom-call | tf_op jit(solution)/shard_map/x_strip/pallas_call | solution.py:774
  31.5 17.3 %all_to_all.5.refs_0_ = f32[128,1,128]{2,1,0:T(1,128)S(1)} all-to-all(f32[128,1,128]{2,1,0:T(1,128)S(1)} %x_strip.1), channel_id=1, replica_groups=mesh['gx'=4,'gy'=4,'gz'=8] {'gx','gy','gz'}, dimensions={0} | all-to-all | bytes 131072 | tf_op jit(solution)/shard_map/all_to_all | solution.py:897
  48.7 2.0 %finish.1 = (f32[4,16,64,128]{3,2,1,0:T(8,128)}, f32[20,20]{1,0:T(8,128)}) custom-call(f32[128,1,128]{2,1,0:T(1,128)S(1)} %all_to_all.5.refs_0_, f32[4,16,64,128]{3,2,1,0:T(8,128)S(1)} %copy-done), custom_call_target="tpu_custom_call" | custom-call | tf_op jit(solution)/shard_map/finish/pallas_call | solution.py:864
Async XLA Ops:
  0.6 4.3 %copy-start = (f32[4,16,64,128]{3,2,1,0:T(8,128)S(1)}, f32[4,16,64,128]{3,2,1,0:T(8,128)}, u32[]{:S(2)}) copy-start(f32[4,16,64,128]{3,2,1,0:T(8,128)} %refs_1_.1) | copy-start | bytes 6291460
  0.6 4.3 %copy-start.1 = (f32[16,64,128]{2,1,0:T(8,128)S(1)}, f32[16,64,128]{2,1,0:T(8,128)}, u32[]{:S(2)}) copy-start(f32[16,64,128]{2,1,0:T(8,128)} %kappa.7) | copy-start | bytes 1572868
  2.1 12.3 %collective-permute-start.1 = (f32[5,4,64,128]{3,2,1,0:T(8,128)S(1)}, f32[5,4,64,128]{3,2,1,0:T(8,128)S(1)}, u32[]{:S(2)}, u32[]{:S(2)}) collective-permute-start(f32[5,4,64,128]{3,2,1,0:T(8,128)S(1)} %get-tuple-element.18), channel_id=1, source_target_pairs={{0,1},{1,0},{2,3},{3,2},{4,5},{5,4},{6,7},{7,6},{8,9},{9,8},{10,11... | collective-permute-start | bytes 1966088 | tf_op jit(solution)/shard_map/ppermute | solution.py:63
  3.6 10.8 %collective-permute-start.2 = (f32[5,4,64,128]{3,2,1,0:T(8,128)S(1)}, f32[5,4,64,128]{3,2,1,0:T(8,128)S(1)}, u32[]{:S(2)}, u32[]{:S(2)}) collective-permute-start(f32[5,4,64,128]{3,2,1,0:T(8,128)S(1)} %get-tuple-element.19), channel_id=1, source_target_pairs={{0,7},{1,2},{2,1},{3,4},{4,3},{5,6},{6,5},{7,0},{8,15},{9,10},{10,... | collective-permute-start | bytes 1966088 | tf_op jit(solution)/shard_map/ppermute | solution.py:62
  6.6 8.6 %collective-permute-start = (f32[5,16,8,128]{3,2,1,0:T(8,128)S(1)}, f32[5,16,8,128]{3,2,1,0:T(8,128)S(1)}, u32[]{:S(2)}, u32[]{:S(2)}) collective-permute-start(f32[5,16,8,128]{3,2,1,0:T(8,128)S(1)} %get-tuple-element.17), channel_id=1, source_target_pairs={{0,24},{1,9},{2,26},{3,11},{4,28},{5,13},{6,30},{7,15},{8,0},{9,17... | collective-permute-start | bytes 983048 | tf_op jit(solution)/shard_map/ppermute | solution.py:78
  15.5 12.8 %collective-permute-start.4 = (f32[96,8,128]{2,1,0:T(8,128)S(1)}, f32[96,8,128]{2,1,0:T(8,128)S(1)}, u32[]{:S(2)}, u32[]{:S(2)}) collective-permute-start(f32[96,8,128]{2,1,0:T(8,128)S(1)} %get-tuple-element.24), channel_id=1, source_target_pairs={{0,96},{1,33},{2,98},{3,35},{4,100},{5,37},{6,102},{7,39},{32,0},{... | collective-permute-start | bytes 1179656 | tf_op jit(solution)/shard_map/ppermute | solution.py:78
  16.7 8.5 %collective-permute-start.3 = (f32[5,8,8,128]{3,2,1,0:T(8,128)S(1)}, f32[5,8,8,128]{3,2,1,0:T(8,128)S(1)}, u32[]{:S(2)}, u32[]{:S(2)}) collective-permute-start(f32[5,8,8,128]{3,2,1,0:T(8,128)S(1)} %get-tuple-element.23), channel_id=1, source_target_pairs={{0,24},{1,9},{2,26},{3,11},{4,28},{5,13},{6,30},{7,15},{8,0},{9,17... | collective-permute-start | bytes 491528 | tf_op jit(solution)/shard_map/ppermute | solution.py:78
  18.4 9.9 %collective-permute-start.5 = (f32[3,8,128]{2,1,0:T(8,128)S(1)}, f32[3,8,128]{2,1,0:T(8,128)S(1)}, u32[]{:S(2)}, u32[]{:S(2)}) collective-permute-start(f32[3,8,128]{2,1,0:T(8,128)S(1)} %get-tuple-element.25), channel_id=1, source_target_pairs={{0,120},{1,41},{2,122},{3,43},{4,124},{5,45},{6,126},{7,47},{8,96}... | collective-permute-start | bytes 36872 | tf_op jit(solution)/shard_map/ppermute | solution.py:78

commit v7 on v6

--- a/solution.py
+++ b/solution.py
@@ -309,7 +309,7 @@
             x_face[n, at] = pack_duo(duo, lambda a, q: held[a, q])
         return carry
 
-    lax.fori_loop(0, ny // 8, rows, 0, unroll=2)
+    lax.fori_loop(0, ny // 8, rows, 0, unroll=4)
 
     def slabs(z, carry):
         for a in range(ARRAYS):
@@ -373,7 +373,7 @@
             strip[a, at] = strip_of(lowers + uppers)
         return carry
 
-    lax.fori_loop(0, strip.shape[1] // 8, rows, 0, unroll=2)
+    lax.fori_loop(0, strip.shape[1] // 8, rows, 0, unroll=4)
 
 
 def far_strips(first, second, after):
@@ -450,7 +450,7 @@
                 kz[1, DEEP - 1 - i] = upper
         return carry
 
-    lax.fori_loop(0, DEEP, far, 0)
+    lax.fori_loop(0, DEEP, far, 0, unroll=4)
     for i in range(2):
         for c in range(COLS):
             f0[0, c, DEEP + i] = block[c, i]
@@ -478,7 +478,7 @@
             wz[at, tile(t)] = link(k, far, True)
         return carry
 
-    lax.fori_loop(0, 16, weights, 0, unroll=4)
+    lax.fori_loop(0, 16, weights, 0, unroll=8)
     fields = (f0, f1, f2, f3, None)
     for k in range(1, BASIS + 1):
         src, dst = fields[k - 1], fields[k]

time: 50.9 us -> 50.4 us (level)
  transfers between devices with their start and end apart: 6 -> 6, of which waited for: 0 -> 0; matrix products, arithmetic and copies ran while one was open for 0% -> 0% of each run, Pallas kernels for 32% -> 31%
where the time goes in v7:
time: 50.4 us; the launch traced here: 50.2 us
  Pallas kernels  22.5 us (45%)
  blocking collectives  17.2 us (34%)
  starting transfers between devices  9.74 us (19%)
  between operations  0.76 us (2%)
    all_to_all x1, blocking collectives, shards(): parts = lax.all_to_all(moments, axes, 0, 0, tiled=True)  17.2 us
    ppermute x4, starting transfers between devices, pull(): return lax.ppermute(face, (*axes, 'gz'), pairs)  6.88 us
    pallas_call x1, Pallas kernels, inner(): pl.pallas_call(inner_kernel, out_shape=[jax.ShapeDtypeStruct((MOMENTS * N...  6.11 us
    pallas_call x1, Pallas kernels, outer(): pl.pallas_call(outer_kernel, out_shape=jax.ShapeDtypeStruct((MOMENTS * NP...  4.38 us
    pallas_call x1, Pallas kernels, x_strip(): pl.pallas_call(x_strip_kernel, out_shape=jax.ShapeDtypeStruct((peers, 1,...  3.15 us
    pallas_call x1, Pallas kernels, y_strip(): pl.pallas_call(y_strip_kernel, out_shape=jax.ShapeDtypeStruct((MOMENTS *...  3.04 us
    pallas_call x1, Pallas kernels, finish(): pl.pallas_call(lambda *refs: finish_kernel(ncells, *refs), grid=(steps,),...  2.03 us
    ppermute x1, starting transfers between devices, swap(): first = lax.ppermute(first, axis, [(i, i ^ 1) for i in range(peers)])  1.5 us
  transfers between devices with their start and end apart: 6, of which 0 were waited for; matrix products, arithmetic and copies ran while one was open for 0% of the time, Pallas kernels for 31%

profile of v7, /device:TPU:1, one launch (start us, length us, event | category | flops | bytes accessed | tf_op | source)
XLA Modules:
  0.0 50.2 jit_solution(16143085045507973050)
XLA Ops:
  0.6 0.0 copy-start
  0.6 0.0 copy-start.1
  0.6 1.5 %pack_z.1 = (f32[5,4,64,128]{3,2,1,0:T(8,128)S(1)}, f32[5,4,64,128]{3,2,1,0:T(8,128)S(1)}) custom-call(f32[4,16,64,128]{3,2,1,0:T(8,128)} %refs_1_.1, f32[16,64,128]{2,1,0:T(8,128)} %kappa.7), custom_call_target="tpu_custom_call" | custom-call | tf_op jit(solution)/shard_map/pack_z/pallas_call | solution.py:175
  2.1 1.5 %collective-permute-start.1 = (f32[5,4,64,128]{3,2,1,0:T(8,128)S(1)}, f32[5,4,64,128]{3,2,1,0:T(8,128)S(1)}, u32[]{:S(2)}, u32[]{:S(2)}) collective-permute-start(f32[5,4,64,128]{3,2,1,0:T(8,128)S(1)} %get-tuple-element.18), channel_id=1, source_target_pairs={{0,1},{1,0},{2,3},{3,2},{4,5},{5,4},{6,7},{7,6},{8,9},{9,8},{10,11... | collective-permute-start | bytes 1966088 | tf_op jit(solution)/shard_map/ppermute | solution.py:63
  3.6 1.4 %collective-permute-start.2 = (f32[5,4,64,128]{3,2,1,0:T(8,128)S(1)}, f32[5,4,64,128]{3,2,1,0:T(8,128)S(1)}, u32[]{:S(2)}, u32[]{:S(2)}) collective-permute-start(f32[5,4,64,128]{3,2,1,0:T(8,128)S(1)} %get-tuple-element.19), channel_id=1, source_target_pairs={{0,7},{1,2},{2,1},{3,4},{4,3},{5,6},{6,5},{7,0},{8,15},{9,10},{10,... | collective-permute-start | bytes 1966088 | tf_op jit(solution)/shard_map/ppermute | solution.py:62
  5.0 0.0 copy-done
  5.0 0.0 copy-done.1
  5.0 1.5 %faces.1 = (f32[5,3,64,128]{3,2,1,0:T(8,128)S(1)}, f32[8,64,128]{2,1,0:T(8,128)S(1)}, f32[5,16,8,128]{3,2,1,0:T(8,128)S(1)}, f32[5,16,8,128]{3,2,1,0:T(8,128)S(1)}) custom-call(f32[4,16,64,128]{3,2,1,0:T(8,128)S(1)} %copy-done, f32[16,64,128]{2,1,0:T(8,128)S(1)} %copy-done.1), custom_call_target="tpu_custom_call" | custom-call | flops 16777216 | bytes 1048576 | tf_op jit(solution)/shard_map/faces/pallas_call | solution.py:327
  6.4 1.7 %collective-permute-start = (f32[5,16,8,128]{3,2,1,0:T(8,128)S(1)}, f32[5,16,8,128]{3,2,1,0:T(8,128)S(1)}, u32[]{:S(2)}, u32[]{:S(2)}) collective-permute-start(f32[5,16,8,128]{3,2,1,0:T(8,128)S(1)} %get-tuple-element.17), channel_id=1, source_target_pairs={{0,24},{1,9},{2,26},{3,11},{4,28},{5,13},{6,30},{7,15},{8,0},{9,17... | collective-permute-start | bytes 983048 | tf_op jit(solution)/shard_map/ppermute | solution.py:78
  8.2 6.1 %inner.1 = (f32[90,8,128]{2,1,0:T(8,128)S(1)}, f32[3,2,2,4,64,128]{5,4,3,2,1,0:T(8,128)S(1)}) custom-call(f32[4,16,64,128]{3,2,1,0:T(8,128)S(1)} %copy-done, f32[16,64,128]{2,1,0:T(8,128)S(1)} %copy-done.1), custom_call_target="tpu_custom_call" | custom-call | flops 268435456 | bytes 1048576 | tf_op jit(solution)/shard_map/inner/pallas_call | solution.py:248
  14.3 0.0 collective-permute-done.1.f_low.f_high.first
  14.3 0.0 collective-permute-done.2.s_low.s_high.second
  14.3 0.1 far_y.1
  14.4 0.5 far_strips.1.far_strip
  14.9 0.0 collective-permute-done.rim
  14.9 0.3 pack_x.1
  15.2 1.3 %collective-permute-start.4 = (f32[96,8,128]{2,1,0:T(8,128)S(1)}, f32[96,8,128]{2,1,0:T(8,128)S(1)}, u32[]{:S(2)}, u32[]{:S(2)}) collective-permute-start(f32[96,8,128]{2,1,0:T(8,128)S(1)} %get-tuple-element.24), channel_id=1, source_target_pairs={{0,96},{1,33},{2,98},{3,35},{4,100},{5,37},{6,102},{7,39},{32,0},{... | collective-permute-start | bytes 1179656 | tf_op jit(solution)/shard_map/ppermute | solution.py:78
  16.4 1.6 %collective-permute-start.3 = (f32[5,8,8,128]{3,2,1,0:T(8,128)S(1)}, f32[5,8,8,128]{3,2,1,0:T(8,128)S(1)}, u32[]{:S(2)}, u32[]{:S(2)}) collective-permute-start(f32[5,8,8,128]{3,2,1,0:T(8,128)S(1)} %get-tuple-element.23), channel_id=1, source_target_pairs={{0,24},{1,9},{2,26},{3,11},{4,28},{5,13},{6,30},{7,15},{8,0},{9,17... | collective-permute-start | bytes 491528 | tf_op jit(solution)/shard_map/ppermute | solution.py:78
  18.1 2.3 %collective-permute-start.5 = (f32[3,8,128]{2,1,0:T(8,128)S(1)}, f32[3,8,128]{2,1,0:T(8,128)S(1)}, u32[]{:S(2)}, u32[]{:S(2)}) collective-permute-start(f32[3,8,128]{2,1,0:T(8,128)S(1)} %get-tuple-element.25), channel_id=1, source_target_pairs={{0,120},{1,41},{2,122},{3,43},{4,124},{5,45},{6,126},{7,47},{8,96}... | collective-permute-start | bytes 36872 | tf_op jit(solution)/shard_map/ppermute | solution.py:78
  20.3 4.4 %outer.1.acc2 = f32[90,8,128]{2,1,0:T(8,128)S(1)} custom-call(f32[4,16,64,128]{3,2,1,0:T(8,128)S(1)} %copy-done, f32[16,64,128]{2,1,0:T(8,128)S(1)} %copy-done.1, f32[3,2,2,4,64,128]{5,4,3,2,1,0:T(8,128)S(1)} %get-tuple-element.26.edge, f32[5,4,64,128]{3,2,1,0:T(8,128)S(1)} %collective-permute-done.1.f_low.f_high.first, ...), custom_call_target="tpu_custom_call" | custom-call | flops 134217728 | bytes 1048576 | tf_op jit(solution)/shard_map/outer/pallas_call | solution.py:525
  24.7 0.0 collective-permute-done.3.far_rim
  24.7 3.0 %y_strip.1.acc3 = f32[90,8,128]{2,1,0:T(8,128)S(1)} custom-call(f32[5,16,8,128]{3,2,1,0:T(8,128)S(1)} %get-tuple-element.27.kept, f32[5,8,8,128]{3,2,1,0:T(8,128)S(1)} %get-tuple-element.21.after.far_kept, f32[5,16,8,128]{3,2,1,0:T(8,128)S(1)} %collective-permute-done.rim, f32[5,8,8,128]{3,2,1,0:T(8,128)S(1)} %collective-permute-done.3.far_rim), custom_call_target="tpu_custom_call" | custom-call | flops 1073741824 | bytes 1048576 | tf_op jit(solution)/shard_map/y_strip/pallas_call | solution.py:633
  27.8 0.0 collective-permute-done.5.corner
  27.8 0.0 collective-permute-done.4.face
  27.8 3.1 %x_strip.1 = f32[128,1,128]{2,1,0:T(1,128)S(1)} custom-call(f32[5,3,64,128]{3,2,1,0:T(8,128)S(1)} %get-tuple-element.15.strip, f32[5,3,8,128]{3,2,1,0:T(8,128)S(1)} %get-tuple-element.22.after.side, f32[5,64,128]{2,1,0:T(8,128)S(1)} %far_strips.1.far_strip, f32[5,8,8,128]{3,2,1,0:T(8,128)S(1)} %collective-permute-done.3.far_rim, ...), custom_call_target="tpu_custom_call" | custom-call | tf_op jit(solution)/shard_map/x_strip/pallas_call | solution.py:774
  31.0 17.2 %all_to_all.5.refs_0_ = f32[128,1,128]{2,1,0:T(1,128)S(1)} all-to-all(f32[128,1,128]{2,1,0:T(1,128)S(1)} %x_strip.1), channel_id=1, replica_groups=mesh['gx'=4,'gy'=4,'gz'=8] {'gx','gy','gz'}, dimensions={0} | all-to-all | bytes 131072 | tf_op jit(solution)/shard_map/all_to_all | solution.py:897
  48.2 2.0 %finish.1 = (f32[4,16,64,128]{3,2,1,0:T(8,128)}, f32[20,20]{1,0:T(8,128)}) custom-call(f32[128,1,128]{2,1,0:T(1,128)S(1)} %all_to_all.5.refs_0_, f32[4,16,64,128]{3,2,1,0:T(8,128)S(1)} %copy-done), custom_call_target="tpu_custom_call" | custom-call | tf_op jit(solution)/shard_map/finish/pallas_call | solution.py:864
Async XLA Ops:
  0.6 4.3 %copy-start = (f32[4,16,64,128]{3,2,1,0:T(8,128)S(1)}, f32[4,16,64,128]{3,2,1,0:T(8,128)}, u32[]{:S(2)}) copy-start(f32[4,16,64,128]{3,2,1,0:T(8,128)} %refs_1_.1) | copy-start | bytes 6291460
  0.6 4.3 %copy-start.1 = (f32[16,64,128]{2,1,0:T(8,128)S(1)}, f32[16,64,128]{2,1,0:T(8,128)}, u32[]{:S(2)}) copy-start(f32[16,64,128]{2,1,0:T(8,128)} %kappa.7) | copy-start | bytes 1572868
  2.1 12.2 %collective-permute-start.1 = (f32[5,4,64,128]{3,2,1,0:T(8,128)S(1)}, f32[5,4,64,128]{3,2,1,0:T(8,128)S(1)}, u32[]{:S(2)}, u32[]{:S(2)}) collective-permute-start(f32[5,4,64,128]{3,2,1,0:T(8,128)S(1)} %get-tuple-element.18), channel_id=1, source_target_pairs={{0,1},{1,0},{2,3},{3,2},{4,5},{5,4},{6,7},{7,6},{8,9},{9,8},{10,11... | collective-permute-start | bytes 1966088 | tf_op jit(solution)/shard_map/ppermute | solution.py:63
  3.6 10.7 %collective-permute-start.2 = (f32[5,4,64,128]{3,2,1,0:T(8,128)S(1)}, f32[5,4,64,128]{3,2,1,0:T(8,128)S(1)}, u32[]{:S(2)}, u32[]{:S(2)}) collective-permute-start(f32[5,4,64,128]{3,2,1,0:T(8,128)S(1)} %get-tuple-element.19), channel_id=1, source_target_pairs={{0,7},{1,2},{2,1},{3,4},{4,3},{5,6},{6,5},{7,0},{8,15},{9,10},{10,... | collective-permute-start | bytes 1966088 | tf_op jit(solution)/shard_map/ppermute | solution.py:62
  6.4 8.4 %collective-permute-start = (f32[5,16,8,128]{3,2,1,0:T(8,128)S(1)}, f32[5,16,8,128]{3,2,1,0:T(8,128)S(1)}, u32[]{:S(2)}, u32[]{:S(2)}) collective-permute-start(f32[5,16,8,128]{3,2,1,0:T(8,128)S(1)} %get-tuple-element.17), channel_id=1, source_target_pairs={{0,24},{1,9},{2,26},{3,11},{4,28},{5,13},{6,30},{7,15},{8,0},{9,17... | collective-permute-start | bytes 983048 | tf_op jit(solution)/shard_map/ppermute | solution.py:78
  15.2 12.6 %collective-permute-start.4 = (f32[96,8,128]{2,1,0:T(8,128)S(1)}, f32[96,8,128]{2,1,0:T(8,128)S(1)}, u32[]{:S(2)}, u32[]{:S(2)}) collective-permute-start(f32[96,8,128]{2,1,0:T(8,128)S(1)} %get-tuple-element.24), channel_id=1, source_target_pairs={{0,96},{1,33},{2,98},{3,35},{4,100},{5,37},{6,102},{7,39},{32,0},{... | collective-permute-start | bytes 1179656 | tf_op jit(solution)/shard_map/ppermute | solution.py:78
  16.4 8.3 %collective-permute-start.3 = (f32[5,8,8,128]{3,2,1,0:T(8,128)S(1)}, f32[5,8,8,128]{3,2,1,0:T(8,128)S(1)}, u32[]{:S(2)}, u32[]{:S(2)}) collective-permute-start(f32[5,8,8,128]{3,2,1,0:T(8,128)S(1)} %get-tuple-element.23), channel_id=1, source_target_pairs={{0,24},{1,9},{2,26},{3,11},{4,28},{5,13},{6,30},{7,15},{8,0},{9,17... | collective-permute-start | bytes 491528 | tf_op jit(solution)/shard_map/ppermute | solution.py:78
  18.1 9.7 %collective-permute-start.5 = (f32[3,8,128]{2,1,0:T(8,128)S(1)}, f32[3,8,128]{2,1,0:T(8,128)S(1)}, u32[]{:S(2)}, u32[]{:S(2)}) collective-permute-start(f32[3,8,128]{2,1,0:T(8,128)S(1)} %get-tuple-element.25), channel_id=1, source_target_pairs={{0,120},{1,41},{2,122},{3,43},{4,124},{5,45},{6,126},{7,47},{8,96}... | collective-permute-start | bytes 36872 | tf_op jit(solution)/shard_map/ppermute | solution.py:78

commit v8 on v7

--- a/solution.py
+++ b/solution.py
@@ -433,11 +433,11 @@
     )(own_face, rim, far_strip)
 
 
-def outer_kernel(block, kappa, edge, first, second, after, acc, f0, f1, f2, f3, kz, w, wz):
+def outer_kernel(block, kappa, edge, first, second, start, after, acc, f0, f1, f2, f3, kz, w, wz):
     nz, ny, _ = kappa.shape
     tiles = ny // 8
     half = sublanes(8) < 4
-    acc[...] = jnp.zeros_like(acc)
+    acc[...] = start[...]
 
     def far(i, carry):
         for a in range(ARRAYS):
@@ -520,12 +520,12 @@
         lax.fori_loop(0, 2, both, 0)
 
 
-def outer(block, kappa, edge, first, second, after):
+def outer(block, kappa, edge, first, second, start, after):
     nz, ny, nx = kappa.shape
     return pl.pallas_call(
         outer_kernel,
         out_shape=jax.ShapeDtypeStruct((MOMENTS * NPAIRS, 8, nx), F32),
-        in_specs=[VMEM] * 5 + [pl.BlockSpec(memory_space=pl.ANY)],
+        in_specs=[VMEM] * 6 + [pl.BlockSpec(memory_space=pl.ANY)],
         out_specs=VMEM,
         scratch_shapes=[pltpu.VMEM((2, COLS, DEEP + 2, ny, nx), F32)] * 4
         + [
@@ -536,7 +536,7 @@
         compiler_params=params(24),
         cost_estimate=cost(1 << 27),
         name="outer",
-    )(block, kappa, edge, first, second, after)
+    )(block, kappa, edge, first, second, start, after)
 
 
 def y_strip_kernel(kept, far_kept, rim, far_rim, acc, g0, g1, g2, g3, kr, w, wz):
@@ -647,7 +647,7 @@
     )(kept, far_kept, rim, far_rim)
 
 
-def x_strip_kernel(strip, side, far_strip, far_rim, face, corner, acc1, acc2, acc3, out, s0, s1, s2, s3, kr, w, wz, acc):
+def x_strip_kernel(strip, side, far_strip, far_rim, face, corner, acc1, acc2, out, s0, s1, s2, s3, kr, w, wz, acc):
     tiles = strip.shape[2] // 8 + 1
     lane = lanes(8)
     offset = lane % PITCH
@@ -752,7 +752,7 @@
     here = (lane1 % PITCH >= DEEP) & (lane1 % PITCH < PITCH - DEEP)
     groups = 128 // PITCH
     total = jnp.where(
-        (lane1 >= DEEP) & (lane1 < 128 - DEEP), jnp.sum(acc1[...] + acc2[...] + acc3[...], axis=1), 0.0
+        (lane1 >= DEEP) & (lane1 < 128 - DEEP), jnp.sum(acc1[...] + acc2[...], axis=1), 0.0
     )
     for q in range(SLABS):
         kept = here & (z + q >= DEEP) & (z + q < groups * SLABS - DEEP)
@@ -774,7 +774,7 @@
     return pl.pallas_call(
         x_strip_kernel,
         out_shape=jax.ShapeDtypeStruct((peers, 1, 128), F32),
-        in_specs=[VMEM] * 9,
+        in_specs=[VMEM] * 8,
         out_specs=VMEM,
         scratch_shapes=[pltpu.VMEM((COLS,) + laid, F32)] * 4
         + [
@@ -890,9 +890,9 @@
     far_strip = far_strips(first, second, far_kept)
     side, x_face, corner = pack_x(x_face, rim, far_strip)
     x_face, corner = pull(x_face, "gx"), pull(corner, "gx", "gy")
-    acc2 = outer(block, kappa, edge, first, second, side)
+    acc2 = outer(block, kappa, edge, first, second, acc1, side)
     acc3 = y_strip(y_kept, far_kept, rim, far_rim)
-    accs = (acc1, acc2, acc3)
+    accs = (acc2, acc3)
     moments = x_strip(strip, side, far_strip, far_rim, x_face, corner, accs, peers)
     parts = lax.all_to_all(moments, axes, 0, 0, tiled=True)
     return tuple(finish(parts, block, ncells))

time: 50.4 us -> 50.2 us (level)
  no operation moved by 1% of the time
where the time goes in v8:
time: 50.2 us; the launch traced here: 50.1 us
  Pallas kernels  22.3 us (44%)
  blocking collectives  17.1 us (34%)
  starting transfers between devices  9.84 us (20%)
  between operations  0.76 us (2%)
    all_to_all x1, blocking collectives, shards(): parts = lax.all_to_all(moments, axes, 0, 0, tiled=True)  17.1 us
    ppermute x4, starting transfers between devices, pull(): return lax.ppermute(face, (*axes, 'gz'), pairs)  6.98 us
    pallas_call x1, Pallas kernels, inner(): pl.pallas_call(inner_kernel, out_shape=[jax.ShapeDtypeStruct((MOMENTS * N...  6.01 us
    pallas_call x1, Pallas kernels, outer(): pl.pallas_call(outer_kernel, out_shape=jax.ShapeDtypeStruct((MOMENTS * NP...  4.4 us
    pallas_call x1, Pallas kernels, x_strip(): pl.pallas_call(x_strip_kernel, out_shape=jax.ShapeDtypeStruct((peers, 1,...  3.13 us
    pallas_call x1, Pallas kernels, y_strip(): pl.pallas_call(y_strip_kernel, out_shape=jax.ShapeDtypeStruct((MOMENTS *...  3.02 us
    pallas_call x1, Pallas kernels, finish(): pl.pallas_call(lambda *refs: finish_kernel(ncells, *refs), grid=(steps,),...  2.03 us
    ppermute x1, starting transfers between devices, swap(): first = lax.ppermute(first, axis, [(i, i ^ 1) for i in range(peers)])  1.5 us
  transfers between devices with their start and end apart: 6, of which 0 were waited for; matrix products, arithmetic and copies ran while one was open for 0% of the time, Pallas kernels for 31%

profile of v8, /device:TPU:1, one launch (start us, length us, event | category | flops | bytes accessed | tf_op | source)
XLA Modules:
  0.0 50.1 jit_solution(16630658481503538216)
XLA Ops:
  0.6 0.0 copy-start
  0.6 0.0 copy-start.1
  0.6 1.5 %pack_z.1 = (f32[5,4,64,128]{3,2,1,0:T(8,128)S(1)}, f32[5,4,64,128]{3,2,1,0:T(8,128)S(1)}) custom-call(f32[4,16,64,128]{3,2,1,0:T(8,128)} %refs_1_.1, f32[16,64,128]{2,1,0:T(8,128)} %kappa.7), custom_call_target="tpu_custom_call" | custom-call | tf_op jit(solution)/shard_map/pack_z/pallas_call | solution.py:175
  2.1 1.5 %collective-permute-start.1 = (f32[5,4,64,128]{3,2,1,0:T(8,128)S(1)}, f32[5,4,64,128]{3,2,1,0:T(8,128)S(1)}, u32[]{:S(2)}, u32[]{:S(2)}) collective-permute-start(f32[5,4,64,128]{3,2,1,0:T(8,128)S(1)} %get-tuple-element.18), channel_id=1, source_target_pairs={{0,1},{1,0},{2,3},{3,2},{4,5},{5,4},{6,7},{7,6},{8,9},{9,8},{10,11... | collective-permute-start | bytes 1966088 | tf_op jit(solution)/shard_map/ppermute | solution.py:63
  3.6 1.4 %collective-permute-start.2 = (f32[5,4,64,128]{3,2,1,0:T(8,128)S(1)}, f32[5,4,64,128]{3,2,1,0:T(8,128)S(1)}, u32[]{:S(2)}, u32[]{:S(2)}) collective-permute-start(f32[5,4,64,128]{3,2,1,0:T(8,128)S(1)} %get-tuple-element.19), channel_id=1, source_target_pairs={{0,7},{1,2},{2,1},{3,4},{4,3},{5,6},{6,5},{7,0},{8,15},{9,10},{10,... | collective-permute-start | bytes 1966088 | tf_op jit(solution)/shard_map/ppermute | solution.py:62
  5.0 0.0 copy-done
  5.0 0.0 copy-done.1
  5.0 1.5 %faces.1 = (f32[5,3,64,128]{3,2,1,0:T(8,128)S(1)}, f32[8,64,128]{2,1,0:T(8,128)S(1)}, f32[5,16,8,128]{3,2,1,0:T(8,128)S(1)}, f32[5,16,8,128]{3,2,1,0:T(8,128)S(1)}) custom-call(f32[4,16,64,128]{3,2,1,0:T(8,128)S(1)} %copy-done, f32[16,64,128]{2,1,0:T(8,128)S(1)} %copy-done.1), custom_call_target="tpu_custom_call" | custom-call | flops 16777216 | bytes 1048576 | tf_op jit(solution)/shard_map/faces/pallas_call | solution.py:327
  6.4 1.7 %collective-permute-start = (f32[5,16,8,128]{3,2,1,0:T(8,128)S(1)}, f32[5,16,8,128]{3,2,1,0:T(8,128)S(1)}, u32[]{:S(2)}, u32[]{:S(2)}) collective-permute-start(f32[5,16,8,128]{3,2,1,0:T(8,128)S(1)} %get-tuple-element.17), channel_id=1, source_target_pairs={{0,24},{1,9},{2,26},{3,11},{4,28},{5,13},{6,30},{7,15},{8,0},{9,17... | collective-permute-start | bytes 983048 | tf_op jit(solution)/shard_map/ppermute | solution.py:78
  8.2 6.0 %inner.1 = (f32[90,8,128]{2,1,0:T(8,128)S(1)}, f32[3,2,2,4,64,128]{5,4,3,2,1,0:T(8,128)S(1)}) custom-call(f32[4,16,64,128]{3,2,1,0:T(8,128)S(1)} %copy-done, f32[16,64,128]{2,1,0:T(8,128)S(1)} %copy-done.1), custom_call_target="tpu_custom_call" | custom-call | flops 268435456 | bytes 1048576 | tf_op jit(solution)/shard_map/inner/pallas_call | solution.py:248
  14.2 0.0 collective-permute-done.1.f_low.f_high.first
  14.2 0.0 collective-permute-done.2.s_low.s_high.second
  14.2 0.1 far_y.1
  14.3 0.5 far_strips.1.far_strip
  14.8 0.0 collective-permute-done.rim
  14.8 0.3 pack_x.1
  15.1 1.3 %collective-permute-start.4 = (f32[96,8,128]{2,1,0:T(8,128)S(1)}, f32[96,8,128]{2,1,0:T(8,128)S(1)}, u32[]{:S(2)}, u32[]{:S(2)}) collective-permute-start(f32[96,8,128]{2,1,0:T(8,128)S(1)} %get-tuple-element.24), channel_id=1, source_target_pairs={{0,96},{1,33},{2,98},{3,35},{4,100},{5,37},{6,102},{7,39},{32,0},{... | collective-permute-start | bytes 1179656 | tf_op jit(solution)/shard_map/ppermute | solution.py:78
  16.3 1.6 %collective-permute-start.3 = (f32[5,8,8,128]{3,2,1,0:T(8,128)S(1)}, f32[5,8,8,128]{3,2,1,0:T(8,128)S(1)}, u32[]{:S(2)}, u32[]{:S(2)}) collective-permute-start(f32[5,8,8,128]{3,2,1,0:T(8,128)S(1)} %get-tuple-element.23), channel_id=1, source_target_pairs={{0,24},{1,9},{2,26},{3,11},{4,28},{5,13},{6,30},{7,15},{8,0},{9,17... | collective-permute-start | bytes 491528 | tf_op jit(solution)/shard_map/ppermute | solution.py:78
  18.0 2.4 %collective-permute-start.5 = (f32[3,8,128]{2,1,0:T(8,128)S(1)}, f32[3,8,128]{2,1,0:T(8,128)S(1)}, u32[]{:S(2)}, u32[]{:S(2)}) collective-permute-start(f32[3,8,128]{2,1,0:T(8,128)S(1)} %get-tuple-element.25), channel_id=1, source_target_pairs={{0,120},{1,41},{2,122},{3,43},{4,124},{5,45},{6,126},{7,47},{8,96}... | collective-permute-start | bytes 36872 | tf_op jit(solution)/shard_map/ppermute | solution.py:78
  20.3 4.4 %outer.1.acc1 = f32[90,8,128]{2,1,0:T(8,128)S(1)} custom-call(f32[4,16,64,128]{3,2,1,0:T(8,128)S(1)} %copy-done, f32[16,64,128]{2,1,0:T(8,128)S(1)} %copy-done.1, f32[3,2,2,4,64,128]{5,4,3,2,1,0:T(8,128)S(1)} %get-tuple-element.26.edge, f32[5,4,64,128]{3,2,1,0:T(8,128)S(1)} %collective-permute-done.1.f_low.f_high.first, ...), custom_call_target="tpu_custom_call" | custom-call | flops 134217728 | bytes 1048576 | tf_op jit(solution)/shard_map/outer/pallas_call | solution.py:525
  24.7 0.0 collective-permute-done.3.far_rim
  24.8 3.0 %y_strip.1.acc2 = f32[90,8,128]{2,1,0:T(8,128)S(1)} custom-call(f32[5,16,8,128]{3,2,1,0:T(8,128)S(1)} %get-tuple-element.27.kept, f32[5,8,8,128]{3,2,1,0:T(8,128)S(1)} %get-tuple-element.21.after.far_kept, f32[5,16,8,128]{3,2,1,0:T(8,128)S(1)} %collective-permute-done.rim, f32[5,8,8,128]{3,2,1,0:T(8,128)S(1)} %collective-permute-done.3.far_rim), custom_call_target="tpu_custom_call" | custom-call | flops 1073741824 | bytes 1048576 | tf_op jit(solution)/shard_map/y_strip/pallas_call | solution.py:633
  27.8 0.0 collective-permute-done.5.corner
  27.8 0.0 collective-permute-done.4.face
  27.8 3.1 %x_strip.1 = f32[128,1,128]{2,1,0:T(1,128)S(1)} custom-call(f32[5,3,64,128]{3,2,1,0:T(8,128)S(1)} %get-tuple-element.15.strip, f32[5,3,8,128]{3,2,1,0:T(8,128)S(1)} %get-tuple-element.22.after.side, f32[5,64,128]{2,1,0:T(8,128)S(1)} %far_strips.1.far_strip, f32[5,8,8,128]{3,2,1,0:T(8,128)S(1)} %collective-permute-done.3.far_rim, ...), custom_call_target="tpu_custom_call" | custom-call | tf_op jit(solution)/shard_map/x_strip/pallas_call | solution.py:774
  30.9 17.1 %all_to_all.5.refs_0_ = f32[128,1,128]{2,1,0:T(1,128)S(1)} all-to-all(f32[128,1,128]{2,1,0:T(1,128)S(1)} %x_strip.1), channel_id=1, replica_groups=mesh['gx'=4,'gy'=4,'gz'=8] {'gx','gy','gz'}, dimensions={0} | all-to-all | bytes 131072 | tf_op jit(solution)/shard_map/all_to_all | solution.py:897
  48.1 2.0 %finish.1 = (f32[4,16,64,128]{3,2,1,0:T(8,128)}, f32[20,20]{1,0:T(8,128)}) custom-call(f32[128,1,128]{2,1,0:T(1,128)S(1)} %all_to_all.5.refs_0_, f32[4,16,64,128]{3,2,1,0:T(8,128)S(1)} %copy-done), custom_call_target="tpu_custom_call" | custom-call | tf_op jit(solution)/shard_map/finish/pallas_call | solution.py:864
Async XLA Ops:
  0.6 4.3 %copy-start = (f32[4,16,64,128]{3,2,1,0:T(8,128)S(1)}, f32[4,16,64,128]{3,2,1,0:T(8,128)}, u32[]{:S(2)}) copy-start(f32[4,16,64,128]{3,2,1,0:T(8,128)} %refs_1_.1) | copy-start | bytes 6291460
  0.6 4.3 %copy-start.1 = (f32[16,64,128]{2,1,0:T(8,128)S(1)}, f32[16,64,128]{2,1,0:T(8,128)}, u32[]{:S(2)}) copy-start(f32[16,64,128]{2,1,0:T(8,128)} %kappa.7) | copy-start | bytes 1572868
  2.1 12.1 %collective-permute-start.1 = (f32[5,4,64,128]{3,2,1,0:T(8,128)S(1)}, f32[5,4,64,128]{3,2,1,0:T(8,128)S(1)}, u32[]{:S(2)}, u32[]{:S(2)}) collective-permute-start(f32[5,4,64,128]{3,2,1,0:T(8,128)S(1)} %get-tuple-element.18), channel_id=1, source_target_pairs={{0,1},{1,0},{2,3},{3,2},{4,5},{5,4},{6,7},{7,6},{8,9},{9,8},{10,11... | collective-permute-start | bytes 1966088 | tf_op jit(solution)/shard_map/ppermute | solution.py:63
  3.6 10.6 %collective-permute-start.2 = (f32[5,4,64,128]{3,2,1,0:T(8,128)S(1)}, f32[5,4,64,128]{3,2,1,0:T(8,128)S(1)}, u32[]{:S(2)}, u32[]{:S(2)}) collective-permute-start(f32[5,4,64,128]{3,2,1,0:T(8,128)S(1)} %get-tuple-element.19), channel_id=1, source_target_pairs={{0,7},{1,2},{2,1},{3,4},{4,3},{5,6},{6,5},{7,0},{8,15},{9,10},{10,... | collective-permute-start | bytes 1966088 | tf_op jit(solution)/shard_map/ppermute | solution.py:62
  6.4 8.3 %collective-permute-start = (f32[5,16,8,128]{3,2,1,0:T(8,128)S(1)}, f32[5,16,8,128]{3,2,1,0:T(8,128)S(1)}, u32[]{:S(2)}, u32[]{:S(2)}) collective-permute-start(f32[5,16,8,128]{3,2,1,0:T(8,128)S(1)} %get-tuple-element.17), channel_id=1, source_target_pairs={{0,24},{1,9},{2,26},{3,11},{4,28},{5,13},{6,30},{7,15},{8,0},{9,17... | collective-permute-start | bytes 983048 | tf_op jit(solution)/shard_map/ppermute | solution.py:78
  15.1 12.7 %collective-permute-start.4 = (f32[96,8,128]{2,1,0:T(8,128)S(1)}, f32[96,8,128]{2,1,0:T(8,128)S(1)}, u32[]{:S(2)}, u32[]{:S(2)}) collective-permute-start(f32[96,8,128]{2,1,0:T(8,128)S(1)} %get-tuple-element.24), channel_id=1, source_target_pairs={{0,96},{1,33},{2,98},{3,35},{4,100},{5,37},{6,102},{7,39},{32,0},{... | collective-permute-start | bytes 1179656 | tf_op jit(solution)/shard_map/ppermute | solution.py:78
  16.3 8.4 %collective-permute-start.3 = (f32[5,8,8,128]{3,2,1,0:T(8,128)S(1)}, f32[5,8,8,128]{3,2,1,0:T(8,128)S(1)}, u32[]{:S(2)}, u32[]{:S(2)}) collective-permute-start(f32[5,8,8,128]{3,2,1,0:T(8,128)S(1)} %get-tuple-element.23), channel_id=1, source_target_pairs={{0,24},{1,9},{2,26},{3,11},{4,28},{5,13},{6,30},{7,15},{8,0},{9,17... | collective-permute-start | bytes 491528 | tf_op jit(solution)/shard_map/ppermute | solution.py:78
  18.0 9.8 %collective-permute-start.5 = (f32[3,8,128]{2,1,0:T(8,128)S(1)}, f32[3,8,128]{2,1,0:T(8,128)S(1)}, u32[]{:S(2)}, u32[]{:S(2)}) collective-permute-start(f32[3,8,128]{2,1,0:T(8,128)S(1)} %get-tuple-element.25), channel_id=1, source_target_pairs={{0,120},{1,41},{2,122},{3,43},{4,124},{5,45},{6,126},{7,47},{8,96}... | collective-permute-start | bytes 36872 | tf_op jit(solution)/shard_map/ppermute | solution.py:78
